TPU v7x, 32 devices: a whole 2x2x4 slice. The times are simulated.
32 devices in a mesh: blk: 8 (over y, x, core), rep: 4 (over z).
Axes of the slice: x: 2, y: 2, z: 4, core: 2. Of those that a mesh axis runs over, the one named last changes fastest.
Arguments:
- p_tiles: float32 [8, 4, 4, 5, 128, 128], P('blk', 'rep'), may hold values from -1 to 1
- tasks: int32 [8, 4, 4, 3, 48], P('blk', 'rep'), may hold values from 0 to 19, as said below
Outputs:
- density_square: float32 [8, 4, 16, 128, 128], P('blk', 'rep')
Inputs may be any that keep to these rules, and one draw needn't show every extreme that they name: Row 0 of tasks[b, r, s] indexes the 20 tiles of left_s, row 1 the 20 tiles of right_s, row 2 the target tile, where 16 marks an unused slot. Used slots come first in each list; each list has 12 to 48 used slots, and some list has all 48.
All inputs are finite; a program needn't handle non-finite values.
Results may differ from a plain program's by a relative error of at most 0.0003.
Values sent between devices are 32-bit elements; how exact they have to be, the bound alone decides.
No kernel may reach another device: no remote copies, remote signals or barrier semaphores. Data moves between devices by JAX's collectives and lax.ppermute only.
A program may use at most 192 MiB of HBM per device.

v0:
```python
import jax
import jax.numpy as jnp
from jax import lax
from jax.sharding import PartitionSpec as P

NC = 16


def from_behind(value, axis, steps):
    count = lax.axis_size(axis)
    pairs = [(source, (source + steps) % count) for source in range(count)]
    return lax.ppermute(value, axis, pairs)


def multiply_slots(left_tiles, right_tiles, task_list, begin, finish, targets):
    left_pick = left_tiles[task_list[0, begin:finish]]
    right_pick = right_tiles[task_list[1, begin:finish]]
    product = jnp.einsum("nij,njk->nik", left_pick, right_pick, precision=lax.Precision.HIGHEST)
    return jax.ops.segment_sum(product, task_list[2, begin:finish], num_segments=targets + 1)


def contract(left_tiles, right_tiles, task_list, targets):
    slots = task_list.shape[1]
    return multiply_slots(left_tiles, right_tiles, task_list, 0, slots, targets)


def per_device(p_tiles, tasks):
    own_tiles = p_tiles[0, 0]
    task_lists = tasks[0, 0]
    steps = own_tiles.shape[0]
    tile = own_tiles.shape[-1]
    summed = jnp.zeros((NC + 1, tile, tile), own_tiles.dtype)
    whole_panel = lax.all_gather(own_tiles[None], "rep", axis=0, tiled=True)
    carried = own_tiles
    for step in range(steps):
        if step > 0:
            carried = from_behind(carried, "blk", 1)
        column_group = whole_panel[:, step]
        left_tiles = column_group.reshape(-1, tile, tile)
        right_tiles = carried.reshape(-1, tile, tile)
        summed = summed + contract(left_tiles, right_tiles, task_lists[step], NC)
    return summed[:NC][None, None]


def solution(mesh):
    return jax.shard_map(
        per_device,
        mesh=mesh,
        in_specs=(P("blk", "rep", None, None, None, None), P("blk", "rep", None, None, None)),
        out_specs=P("blk", "rep", None, None, None),
        check_vma=False,
    )
```

profile of v0, /device:TPU:1, one launch (start us, length us, event | category | flops | bytes accessed | tf_op | source)
XLA Modules:
  0.0 191.3 jit_solution(14923705854876231536)
XLA Ops:
  7.3 2.7 %collective-permute-start = (f32[4,5,128,128]{3,2,1,0:T(8,128)}, f32[4,5,128,128]{3,2,1,0:T(8,128)S(1)}, u32[]{:S(2)}, u32[]{:S(2)}) collective-permute-start(f32[4,5,128,128]{3,2,1,0:T(8,128)} %bitcast.64), channel_id=1, source_target_pairs={{0,4},{4,8},{8,12},{12,16},{16,20},{20,24},{24,28},{28,0},{1,5},{5... | collective-permute-start | bytes 3932168 | tf_op jit(solution)/shard_map/ppermute | solution.py:12
  9.9 14.9 %collective-permute-done = f32[4,5,128,128]{3,2,1,0:T(8,128)S(1)} collective-permute-done((f32[4,5,128,128]{3,2,1,0:T(8,128)}, f32[4,5,128,128]{3,2,1,0:T(8,128)S(1)}, u32[]{:S(2)}, u32[]{:S(2)}) %collective-permute-start) | collective-permute-done | bytes 1310752 | tf_op jit(solution)/shard_map/ppermute | solution.py:12
  24.8 2.4 %collective-permute-start.1 = (f32[4,5,128,128]{3,2,1,0:T(8,128)S(1)}, f32[4,5,128,128]{3,2,1,0:T(8,128)}, u32[]{:S(2)}, u32[]{:S(2)}) collective-permute-start(f32[4,5,128,128]{3,2,1,0:T(8,128)S(1)} %collective-permute-done), channel_id=1, source_target_pairs={{0,4},{4,8},{8,12},{12,16},{16,20},{20,24},{24,28},{28,0},{1,5},{5... | collective-permute-start | bytes 3932168 | tf_op jit(solution)/shard_map/ppermute | solution.py:12
  27.2 14.6 %collective-permute-done.1 = f32[4,5,128,128]{3,2,1,0:T(8,128)} collective-permute-done((f32[4,5,128,128]{3,2,1,0:T(8,128)S(1)}, f32[4,5,128,128]{3,2,1,0:T(8,128)}, u32[]{:S(2)}, u32[]{:S(2)}) %collective-permute-start.1) | collective-permute-done | bytes 1310752 | tf_op jit(solution)/shard_map/ppermute | solution.py:12
  41.7 2.6 %collective-permute-start.2 = (f32[4,5,128,128]{3,2,1,0:T(8,128)}, f32[4,5,128,128]{3,2,1,0:T(8,128)}, u32[]{:S(2)}, u32[]{:S(2)}) collective-permute-start(f32[4,5,128,128]{3,2,1,0:T(8,128)} %collective-permute-done.1), channel_id=1, source_target_pairs={{0,4},{4,8},{8,12},{12,16},{16,20},{20,24},{24,28},{28,0},{1,5},{5... | collective-permute-start | bytes 3932168 | tf_op jit(solution)/shard_map/ppermute | solution.py:12
  45.2 2.5 %gather_fusion.1 = f32[48,128,128]{2,1,0:T(8,128)} fusion(f32[20,128,128]{2,1,0:T(8,128)S(1)} %bitcast.65, s32[1024]{0:T(1024)S(1)} %get-tuple-element.27), kind=kCustom, calls=%fused_computation.1 | custom fusion | bytes 6291648 | tf_op jit(solution)/shard_map/gather | solution.py:17
  48.5 2.4 %gather_fusion.3 = f32[48,128,128]{2,1,0:T(8,128)} fusion(f32[20,128,128]{2,1,0:T(8,128)S(1)} %bitcast.66, s32[1024]{0:T(1024)S(1)} %get-tuple-element.25), kind=kCustom, calls=%fused_computation.3 | custom fusion | bytes 6291648 | tf_op jit(solution)/shard_map/gather | solution.py:17
  50.9 3.8 %gather_fusion.5 = f32[48,128,128]{2,1,0:T(8,128)} fusion(f32[20,128,128]{2,1,0:T(8,128)} %bitcast.20, s32[1024]{0:T(1024)S(1)} %get-tuple-element.23), kind=kCustom, calls=%fused_computation.5 | custom fusion | bytes 6291648 | tf_op jit(solution)/shard_map/gather | solution.py:17
  54.7 4.4 %collective-permute-done.2 = f32[4,5,128,128]{3,2,1,0:T(8,128)} collective-permute-done((f32[4,5,128,128]{3,2,1,0:T(8,128)}, f32[4,5,128,128]{3,2,1,0:T(8,128)}, u32[]{:S(2)}, u32[]{:S(2)}) %collective-permute-start.2) | collective-permute-done | bytes 1310752 | tf_op jit(solution)/shard_map/ppermute | solution.py:12
  59.2 3.7 %gather_fusion.7 = f32[48,128,128]{2,1,0:T(8,128)} fusion(f32[20,128,128]{2,1,0:T(8,128)} %bitcast.27, s32[1024]{0:T(1024)S(1)} %get-tuple-element.21), kind=kCustom, calls=%fused_computation.7 | custom fusion | bytes 6291648 | tf_op jit(solution)/shard_map/gather | solution.py:17
  62.9 46.4 %all-gather.3.cloned.1.call-done = f32[4,1,4,5,128,128]{5,4,3,2,1,0:T(8,128)} async-done(((f32[1,1,4,5,128,128]{5,4,3,2,1,0:T(8,128)}), f32[4,1,4,5,128,128]{5,4,3,2,1,0:T(8,128)}) %all-gather.3.cloned.1.call-update) | async-done | bytes 5242896 | tf_op jit(solution)/shard_map/all_gather | solution.py:33
  109.3 4.5 %fusion.9 = (f32[4,1,5,128,128]{4,3,2,1,0:T(8,128)}, f32[4,1,5,128,128]{4,3,2,1,0:T(8,128)}, f32[4,1,5,128,128]{4,3,2,1,0:T(8,128)S(1)}, f32[4,1,5,128,128]{4,3,2,1,0:T(8,128)S(1)}) fusion(f32[4,4,5,128,128]{4,3,2,1,0:T(8,128)} %bitcast.67), kind=kLoop, calls=%fused_computation.42 | loop fusion | bytes 10485760 | tf_op jit(solution)/shard_map/slice | solution.py:38
  113.7 2.4 %gather_fusion.2 = f32[48,128,128]{2,1,0:T(8,128)} fusion(f32[20,128,128]{2,1,0:T(8,128)S(1)} %bitcast.63, s32[1024]{0:T(1024)S(1)} %get-tuple-element.26), kind=kCustom, calls=%fused_computation.2 | custom fusion | bytes 6291648 | tf_op jit(solution)/shard_map/gather | solution.py:16
  116.1 7.7 %fusion.11 = f32[48,128,128]{2,1,0:T(8,128)} fusion(f32[48,128,128]{2,1,0:T(8,128)} %gather_fusion.2, f32[48,128,128]{2,1,0:T(8,128)} %gather_fusion.3), kind=kOutput, calls=%fused_computation.44 | convolution fusion | flops 1207959552 | bytes 9437184 | tf_op jit(solution)/shard_map/nij,njk->nik/dot_general | solution.py:18
  123.8 2.4 %gather_fusion = f32[48,128,128]{2,1,0:T(8,128)} fusion(f32[20,128,128]{2,1,0:T(8,128)S(1)} %bitcast.62, s32[1024]{0:T(1024)S(1)} %get-tuple-element.28), kind=kCustom, calls=%fused_computation | custom fusion | bytes 6291648 | tf_op jit(solution)/shard_map/gather | solution.py:16
  126.2 7.7 %fusion.10 = f32[48,128,128]{2,1,0:T(8,128)} fusion(f32[48,128,128]{2,1,0:T(8,128)} %gather_fusion, f32[48,128,128]{2,1,0:T(8,128)} %gather_fusion.1), kind=kOutput, calls=%fused_computation.43 | convolution fusion | flops 1207959552 | bytes 9437184 | tf_op jit(solution)/shard_map/nij,njk->nik/dot_general | solution.py:18
  134.0 6.9 %scatter_fusion.1 = f32[17,128,128]{2,1,0:T(8,128)S(1)} fusion(f32[17,128,128]{2,1,0:T(8,128)S(1)} %broadcast.121.clone.2, s32[48]{0:T(128)S(1)} %get-tuple-element.19, f32[48,128,128]{2,1,0:T(8,128)} %fusion.11), kind=kCustom, calls=%fused_computation.9 | custom fusion | flops 786432 | bytes 9437376 | tf_op jit(solution)/shard_map/scatter-add | solution.py:19
  141.0 6.7 %scatter_fusion = f32[17,128,128]{2,1,0:T(8,128)S(1)} fusion(f32[17,128,128]{2,1,0:T(8,128)S(1)} %broadcast.121.clone.1, s32[48]{0:T(128)S(1)} %get-tuple-element.20, f32[48,128,128]{2,1,0:T(8,128)} %fusion.10), kind=kCustom, calls=%fused_computation.8 | custom fusion | flops 786432 | bytes 9437376 | tf_op jit(solution)/shard_map/scatter-add | solution.py:19
  147.9 3.8 %gather_fusion.4 = f32[48,128,128]{2,1,0:T(8,128)} fusion(f32[20,128,128]{2,1,0:T(8,128)} %bitcast.61, s32[1024]{0:T(1024)S(1)} %get-tuple-element.24), kind=kCustom, calls=%fused_computation.4 | custom fusion | bytes 6291648 | tf_op jit(solution)/shard_map/gather | solution.py:16
  151.7 7.8 %fusion.12 = f32[48,128,128]{2,1,0:T(8,128)} fusion(f32[48,128,128]{2,1,0:T(8,128)} %gather_fusion.4, f32[48,128,128]{2,1,0:T(8,128)} %gather_fusion.5), kind=kOutput, calls=%fused_computation.45 | convolution fusion | flops 1207959552 | bytes 9437184 | tf_op jit(solution)/shard_map/nij,njk->nik/dot_general | solution.py:18
  159.6 2.5 %gather_fusion.6 = f32[48,128,128]{2,1,0:T(8,128)} fusion(f32[20,128,128]{2,1,0:T(8,128)S(1)} %bitcast.60, s32[1024]{0:T(1024)S(1)} %get-tuple-element.22), kind=kCustom, calls=%fused_computation.6 | custom fusion | bytes 6291648 | tf_op jit(solution)/shard_map/gather | solution.py:16
  162.0 7.8 %fusion.13 = f32[48,128,128]{2,1,0:T(8,128)} fusion(f32[48,128,128]{2,1,0:T(8,128)} %gather_fusion.6, f32[48,128,128]{2,1,0:T(8,128)} %gather_fusion.7), kind=kOutput, calls=%fused_computation.46 | convolution fusion | flops 1207959552 | bytes 9437184 | tf_op jit(solution)/shard_map/nij,njk->nik/dot_general | solution.py:18
  169.8 6.7 %scatter_fusion.2 = f32[17,128,128]{2,1,0:T(8,128)S(1)} fusion(f32[17,128,128]{2,1,0:T(8,128)S(1)} %add.100, s32[48]{0:T(128)S(1)} %get-tuple-element.17, f32[48,128,128]{2,1,0:T(8,128)} %fusion.12), kind=kCustom, calls=%fused_computation.10 | custom fusion | flops 786432 | bytes 9437376 | tf_op jit(solution)/shard_map/scatter-add | solution.py:19
  176.7 6.7 %scatter_fusion.3 = f32[17,128,128]{2,1,0:T(8,128)S(1)} fusion(f32[17,128,128]{2,1,0:T(8,128)S(1)} %broadcast.121.clone, s32[48]{0:T(128)S(1)} %get-tuple-element.18, f32[48,128,128]{2,1,0:T(8,128)} %fusion.13), kind=kCustom, calls=%fused_computation.11 | custom fusion | flops 786432 | bytes 9437376 | tf_op jit(solution)/shard_map/scatter-add | solution.py:19
  (17 shorter events, 4.0 us)
Async XLA Ops:
  6.5 38.7 %copy-start.1 = (f32[1,1,4,5,128,128]{5,4,3,2,1,0:T(8,128)S(1)}, f32[1,1,4,5,128,128]{5,4,3,2,1,0:T(8,128)}, u32[]{:S(2)}) copy-start(f32[1,1,4,5,128,128]{5,4,3,2,1,0:T(8,128)} %param.2) | copy-start | bytes 3932164
  6.5 102.7 %all-gather.3.cloned.1.call-start = ((), (), s32[]{:S(2)}) async-start(), calls=%async_computation | async-start | bytes 6553600 | tf_op jit(solution)/shard_map/all_gather | solution.py:33
  7.3 17.5 %collective-permute-start = (f32[4,5,128,128]{3,2,1,0:T(8,128)}, f32[4,5,128,128]{3,2,1,0:T(8,128)S(1)}, u32[]{:S(2)}, u32[]{:S(2)}) collective-permute-start(f32[4,5,128,128]{3,2,1,0:T(8,128)} %bitcast.64), channel_id=1, source_target_pairs={{0,4},{4,8},{8,12},{12,16},{16,20},{20,24},{24,28},{28,0},{1,5},{5... | collective-permute-start | bytes 3932168 | tf_op jit(solution)/shard_map/ppermute | solution.py:12
  24.8 16.9 %collective-permute-start.1 = (f32[4,5,128,128]{3,2,1,0:T(8,128)S(1)}, f32[4,5,128,128]{3,2,1,0:T(8,128)}, u32[]{:S(2)}, u32[]{:S(2)}) collective-permute-start(f32[4,5,128,128]{3,2,1,0:T(8,128)S(1)} %collective-permute-done), channel_id=1, source_target_pairs={{0,4},{4,8},{8,12},{12,16},{16,20},{20,24},{24,28},{28,0},{1,5},{5... | collective-permute-start | bytes 3932168 | tf_op jit(solution)/shard_map/ppermute | solution.py:12
  41.7 17.5 %collective-permute-start.2 = (f32[4,5,128,128]{3,2,1,0:T(8,128)}, f32[4,5,128,128]{3,2,1,0:T(8,128)}, u32[]{:S(2)}, u32[]{:S(2)}) collective-permute-start(f32[4,5,128,128]{3,2,1,0:T(8,128)} %collective-permute-done.1), channel_id=1, source_target_pairs={{0,4},{4,8},{8,12},{12,16},{16,20},{20,24},{24,28},{28,0},{1,5},{5... | collective-permute-start | bytes 3932168 | tf_op jit(solution)/shard_map/ppermute | solution.py:12
  151.7 7.8 %copy-start = (f32[4,1,5,128,128]{4,3,2,1,0:T(8,128)S(1)}, f32[4,1,5,128,128]{4,3,2,1,0:T(8,128)}, u32[]{:S(2)}) copy-start(f32[4,1,5,128,128]{4,3,2,1,0:T(8,128)} %get-tuple-element.6) | copy-start | bytes 3932164
Sparse Core Ops, SparseCore 0:
  8.9 100.2 all-gather.2
where the time goes:
time: 193 us; the launch traced here: 191 us
  waiting for transfers between devices  81 us (42%)
  matrix products  31.1 us (16%)
  other arithmetic  29.2 us (15%)
  local copies, waits for them, and re-layouts  29 us (15%)
  between operations  13.5 us (7%)
  starting transfers between devices  7.62 us (4%)
    all_gather x1, waiting for transfers between devices, per_device(): whole_panel = lax.all_gather(own_tiles[None], 'rep', axis=0, tiled=True)  46.4 us
    ppermute x3, waiting for transfers between devices, from_behind(): return lax.ppermute(value, axis, pairs)  33.9 us
    dot_general x4, matrix products, multiply_slots(): jnp.einsum('nij,njk->nik', left_pick, right_pick, precision=lax.Precision...  31.1 us
    scatter-add x4, other arithmetic, multiply_slots(): jax.ops.segment_sum(product, task_list[2, begin:finish], num_segments=tar...  27.1 us
    gather x4, local copies, waits for them, and re-layouts, multiply_slots(): right_pick = right_tiles[task_list[1, begin:finish]]  12.4 us
    gather x4, local copies, waits for them, and re-layouts, multiply_slots(): left_pick = left_tiles[task_list[0, begin:finish]]  11 us
    ppermute x3, starting transfers between devices, from_behind(): return lax.ppermute(value, axis, pairs)  7.61 us
    slice x1, local copies, waits for them, and re-layouts, per_device(): column_group = whole_panel[:, step]  4.47 us
  transfers between devices with their start and end apart: 4, of which 4 were waited for; matrix products, arithmetic and copies ran while one was open for 7% of the time, Pallas kernels for 0%

commit v1 on v0

v1 whole, which is shorter than its diff:
```python
import functools

import jax
import jax.numpy as jnp
from jax import lax
from jax.experimental import pallas as pl
from jax.experimental.pallas import tpu as pltpu
from jax.sharding import PartitionSpec as P

NC = 16
UNROLL = 4


def split(value):
    high = value.astype(jnp.bfloat16)
    low = (value - high.astype(jnp.float32)).astype(jnp.bfloat16)
    return high, low


def contract_kernel(n_left, first, last, tasks_ref, *refs):
    left_refs, right_ref = refs[:n_left], refs[n_left]
    rest = refs[n_left + 1 :]
    if first:
        out_ref, left_split, total, live = rest
    else:
        before_ref, out_ref, left_split, total, live = rest
    tile = right_ref.shape[-1]
    slots = tasks_ref.shape[-1]

    if first:
        total[...] = jnp.zeros_like(total)
    else:
        total[:NC] = before_ref[...]

    def pack(j, count):
        live[count] = j
        return count + jnp.where(tasks_ref[2, j] < NC, 1, 0)

    count = lax.fori_loop(0, slots, pack, 0)
    for extra in range(UNROLL):
        live[count + extra] = slots

    base = 0
    for ref in left_refs:
        for t in range(ref.shape[0]):
            high, low = split(ref[t])
            left_split[base + t, :, :tile] = high
            left_split[base + t, :, tile:] = low
        base += ref.shape[0]

    def some(i, carry):
        products, targets = [], []
        for u in range(UNROLL):
            j = live[i * UNROLL + u]
            dead = j >= slots
            at = jnp.where(dead, 0, j)
            high, low = split(right_ref[tasks_ref[1, at]])
            both = jnp.concatenate(
                [
                    jnp.concatenate([high, low], axis=1),
                    jnp.concatenate([high, jnp.zeros_like(low)], axis=1),
                ],
                axis=0,
            )
            wide = jnp.dot(
                left_split[tasks_ref[0, at]], both, preferred_element_type=jnp.float32
            )
            products.append(wide[:, :tile] + wide[:, tile:])
            targets.append(jnp.where(dead, NC, tasks_ref[2, at]))
        for product, target in zip(products, targets):
            total[target] += product
        return carry

    lax.fori_loop(0, (count + UNROLL - 1) // UNROLL, some, 0)
    out_ref[...] = total[:NC]


def contract(tasks, lefts, right, before):
    tile = right.shape[-1]
    n_tiles = sum(left.shape[0] for left in lefts)
    slots = tasks.shape[-1]
    vmem = pl.BlockSpec(memory_space=pltpu.VMEM)
    operands = [tasks, *lefts, right] + ([] if before is None else [before])
    return pl.pallas_call(
        functools.partial(contract_kernel, len(lefts), before is None, False),
        out_shape=jax.ShapeDtypeStruct((NC, tile, tile), jnp.float32),
        in_specs=[pl.BlockSpec(memory_space=pltpu.SMEM)] + [vmem] * (len(operands) - 1),
        out_specs=vmem,
        scratch_shapes=[
            pltpu.VMEM((n_tiles, tile, 2 * tile), jnp.bfloat16),
            pltpu.VMEM((NC + 1, tile, tile), jnp.float32),
            pltpu.SMEM((slots + UNROLL,), jnp.int32),
        ],
        compiler_params=pltpu.CompilerParams(vmem_limit_bytes=24 * 2**20),
        cost_estimate=pl.CostEstimate(
            flops=2 * 3 * slots * tile**3 // 4,
            bytes_accessed=4 * tile * tile * (n_tiles + right.shape[0] + 2 * NC),
            transcendentals=0,
        ),
    )(*operands)


def shift_pairs(count, by):
    return [(i, (i + by) % count) for i in range(count)]


def right_panels(own):
    panels, steps = lax.axis_size("blk"), own.shape[0]
    if steps != 4 or panels % 2:
        found = [own]
        for step in range(1, steps):
            found.append(lax.ppermute(own, "blk", shift_pairs(panels, step)))
        return found
    odd = lax.axis_index("blk") % 2 == 1
    two = lax.ppermute(own, "blk", shift_pairs(panels, 2))
    one = lax.ppermute(
        jnp.where(odd, two, own), "blk", [(i, i ^ 1) for i in range(panels)]
    )
    three = lax.ppermute(
        jnp.where(odd, own, two),
        "blk",
        [(i, (i + 3) % panels if i % 2 else i + 1) for i in range(panels)],
    )
    return [own, one, two, three]


def per_device(p_tiles, tasks):
    own = p_tiles[0, 0]
    lists = tasks[0, 0]
    steps, per, tile = own.shape[0], own.shape[1], own.shape[-1]
    slivers = lax.axis_size("rep")
    me = lax.axis_index("rep")

    away = lists[:, 0] // per - me
    spot = lists[:, 0] % per
    up_pairs = lambda far: [(i, i + 1) for i in range(far - 1, slivers - 1)]
    down_pairs = lambda far: [(i, i - 1) for i in range(slivers - far, 0, -1)]

    left = {}
    for step in range(steps):
        left[step, 0] = (own[step],)
    for far in range(1, slivers):
        for step in range(steps):
            before = left[step, far - 1]
            below = lax.ppermute(before[0], "rep", up_pairs(far))
            above = lax.ppermute(before[-1], "rep", down_pairs(far))
            left[step, far] = (below, above)

    right = [panel.reshape(-1, tile, tile) for panel in right_panels(own)]

    total = None
    for far in range(slivers):
        for step in range(steps):
            here = jnp.abs(away[step]) == far
            number = spot[step] + jnp.where(away[step] > 0, per, 0)
            stage = jnp.stack(
                [
                    jnp.where(here, number, 0),
                    lists[step, 1],
                    jnp.where(here, lists[step, 2], NC),
                ]
            )
            total = contract(stage, left[step, far], right[step], total)
    return total[None, None]


def solution(mesh):
    return jax.shard_map(
        per_device,
        mesh=mesh,
        in_specs=(P("blk", "rep", None, None, None, None), P("blk", "rep", None, None, None)),
        out_specs=P("blk", "rep", None, None, None),
        check_vma=False,
    )
```

time: 193 us -> 121 us (0.63)
  the two profiles are of different devices: /device:TPU:1 before, /device:TPU:18 now
where the time goes in v1:
time: 121 us; the launch traced here: 119 us
  starting transfers between devices  68 us (56%)
  Pallas kernels  30.1 us (25%)
  waiting for transfers between devices  17.7 us (15%)
  local copies, waits for them, and re-layouts  2.23 us (2%)
    ppermute x12, starting transfers between devices, per_device(): below = lax.ppermute(before[0], 'rep', up_pairs(far))  39.7 us
    pallas_call x16, Pallas kernels, contract(): pl.pallas_call(functools.partial(contract_kernel, len(lefts), before is N...  30.1 us
    ppermute x12, starting transfers between devices, per_device(): above = lax.ppermute(before[-1], 'rep', down_pairs(far))  26.2 us
    ppermute x12, waiting for transfers between devices, per_device(): below = lax.ppermute(before[0], 'rep', up_pairs(far))  9.11 us
    ppermute x12, waiting for transfers between devices, per_device(): above = lax.ppermute(before[-1], 'rep', down_pairs(far))  8.56 us
  transfers between devices with their start and end apart: 27, of which 9 were waited for; matrix products, arithmetic and copies ran while one was open for 2% of the time, Pallas kernels for 23%

profile of v1, /device:TPU:18, one launch (start us, length us, event | category | flops | bytes accessed | tf_op | source)
XLA Modules:
  0.0 118.9 jit_solution(5951617017901356176)
XLA Ops:
  1.5 2.2 %slice_bitcast_fusion = (f32[5,128,128]{2,1,0:T(8,128)}, f32[5,128,128]{2,1,0:T(8,128)}, f32[5,128,128]{2,1,0:T(8,128)S(1)}, f32[5,128,128]{2,1,0:T(8,128)S(1)}) fusion(f32[1,1,4,5,128,128]{5,4,3,2,1,0:T(8,128)} %param.2), kind=kLoop, calls=%fused_computation.2 | loop fusion | bytes 2621440 | tf_op jit(solution)/shard_map/squeeze | solution.py:141
  3.7 3.5 %collective-permute-start.21 = (f32[5,128,128]{2,1,0:T(8,128)}, f32[5,128,128]{2,1,0:T(8,128)}, u32[]{:S(2)}, u32[]{:S(2)}) collective-permute-start(f32[5,128,128]{2,1,0:T(8,128)} %get-tuple-element.17.refs_0_), channel_id=1, source_target_pairs={{0,1},{1,2},{2,3},{4,5},{5,6},{6,7},{8,9},{9,10},{10,11},{12,13},{... | collective-permute-start | bytes 983048 | tf_op jit(solution)/shard_map/ppermute | solution.py:145
  7.2 2.4 %collective-permute-start.24 = (f32[5,128,128]{2,1,0:T(8,128)}, f32[5,128,128]{2,1,0:T(8,128)}, u32[]{:S(2)}, u32[]{:S(2)}) collective-permute-start(f32[5,128,128]{2,1,0:T(8,128)} %get-tuple-element.17.refs_0_), channel_id=1, source_target_pairs={{3,2},{2,1},{1,0},{7,6},{6,5},{5,4},{11,10},{10,9},{9,8},{15,14},{... | collective-permute-start | bytes 983048 | tf_op jit(solution)/shard_map/ppermute | solution.py:146
  9.6 4.2 %collective-permute-start.14 = (f32[5,128,128]{2,1,0:T(8,128)}, f32[5,128,128]{2,1,0:T(8,128)}, u32[]{:S(2)}, u32[]{:S(2)}) collective-permute-start(f32[5,128,128]{2,1,0:T(8,128)} %get-tuple-element.18.refs_0_), channel_id=1, source_target_pairs={{0,1},{1,2},{2,3},{4,5},{5,6},{6,7},{8,9},{9,10},{10,11},{12,13},{... | collective-permute-start | bytes 983048 | tf_op jit(solution)/shard_map/ppermute | solution.py:145
  16.5 2.7 %collective-permute-start.11 = (f32[5,128,128]{2,1,0:T(8,128)S(1)}, f32[5,128,128]{2,1,0:T(8,128)}, u32[]{:S(2)}, u32[]{:S(2)}) collective-permute-start(f32[5,128,128]{2,1,0:T(8,128)S(1)} %get-tuple-element.19.refs_0_), channel_id=1, source_target_pairs={{3,2},{2,1},{1,0},{7,6},{6,5},{5,4},{11,10},{10,9},{9,8},{15,14},{... | collective-permute-start | bytes 983048 | tf_op jit(solution)/shard_map/ppermute | solution.py:146
  19.3 3.8 %collective-permute-start.8 = (f32[5,128,128]{2,1,0:T(8,128)S(1)}, f32[5,128,128]{2,1,0:T(8,128)S(1)}, u32[]{:S(2)}, u32[]{:S(2)}) collective-permute-start(f32[5,128,128]{2,1,0:T(8,128)S(1)} %get-tuple-element.19.refs_0_), channel_id=1, source_target_pairs={{0,1},{1,2},{2,3},{4,5},{5,6},{6,7},{8,9},{9,10},{10,11},{12,13},{... | collective-permute-start | bytes 983048 | tf_op jit(solution)/shard_map/ppermute | solution.py:145
  23.2 2.5 %collective-permute-start = (f32[5,128,128]{2,1,0:T(8,128)S(1)}, f32[5,128,128]{2,1,0:T(8,128)S(1)}, u32[]{:S(2)}, u32[]{:S(2)}) collective-permute-start(f32[5,128,128]{2,1,0:T(8,128)S(1)} %get-tuple-element.20.refs_0_), channel_id=1, source_target_pairs={{0,1},{1,2},{2,3},{4,5},{5,6},{6,7},{8,9},{9,10},{10,11},{12,13},{... | collective-permute-start | bytes 983048 | tf_op jit(solution)/shard_map/ppermute | solution.py:145
  26.6 2.4 %collective-permute-start.3 = (f32[5,128,128]{2,1,0:T(8,128)S(1)}, f32[5,128,128]{2,1,0:T(8,128)S(1)}, u32[]{:S(2)}, u32[]{:S(2)}) collective-permute-start(f32[5,128,128]{2,1,0:T(8,128)S(1)} %get-tuple-element.20.refs_0_), channel_id=1, source_target_pairs={{3,2},{2,1},{1,0},{7,6},{6,5},{5,4},{11,10},{10,9},{9,8},{15,14},{... | collective-permute-start | bytes 983048 | tf_op jit(solution)/shard_map/ppermute | solution.py:146
  29.1 4.6 %collective-permute-done.11.refs_1_ = f32[5,128,128]{2,1,0:T(8,128)} collective-permute-done((f32[5,128,128]{2,1,0:T(8,128)S(1)}, f32[5,128,128]{2,1,0:T(8,128)}, u32[]{:S(2)}, u32[]{:S(2)}) %collective-permute-start.11) | collective-permute-done | bytes 327712 | tf_op jit(solution)/shard_map/ppermute | solution.py:146
  35.6 4.0 %collective-permute-start.25 = (f32[5,128,128]{2,1,0:T(8,128)}, f32[5,128,128]{2,1,0:T(8,128)S(1)}, u32[]{:S(2)}, u32[]{:S(2)}) collective-permute-start(f32[5,128,128]{2,1,0:T(8,128)} %collective-permute-done.24.refs_1_), channel_id=1, source_target_pairs={{2,1},{1,0},{6,5},{5,4},{10,9},{9,8},{14,13},{13,12},{18,17},{17,1... | collective-permute-start | bytes 983048 | tf_op jit(solution)/shard_map/ppermute | solution.py:146
  41.7 4.0 %collective-permute-start.18 = (f32[5,128,128]{2,1,0:T(8,128)}, f32[5,128,128]{2,1,0:T(8,128)S(1)}, u32[]{:S(2)}, u32[]{:S(2)}) collective-permute-start(f32[5,128,128]{2,1,0:T(8,128)} %collective-permute-done.17.refs_1_), channel_id=1, source_target_pairs={{2,1},{1,0},{6,5},{5,4},{10,9},{9,8},{14,13},{13,12},{18,17},{17,1... | collective-permute-start | bytes 983048 | tf_op jit(solution)/shard_map/ppermute | solution.py:146
  50.1 3.5 %collective-permute-start.9 = (f32[5,128,128]{2,1,0:T(8,128)S(1)}, f32[5,128,128]{2,1,0:T(8,128)S(1)}, u32[]{:S(2)}, u32[]{:S(2)}) collective-permute-start(f32[5,128,128]{2,1,0:T(8,128)S(1)} %collective-permute-done.8.refs_0_), channel_id=1, source_target_pairs={{1,2},{2,3},{5,6},{6,7},{9,10},{10,11},{13,14},{14,15},{17,18},{18... | collective-permute-start | bytes 983048 | tf_op jit(solution)/shard_map/ppermute | solution.py:145
  56.0 2.4 %collective-permute-done.12.refs_1_ = f32[5,128,128]{2,1,0:T(8,128)S(1)} collective-permute-done((f32[5,128,128]{2,1,0:T(8,128)}, f32[5,128,128]{2,1,0:T(8,128)S(1)}, u32[]{:S(2)}, u32[]{:S(2)}) %collective-permute-start.12) | collective-permute-done | bytes 327712 | tf_op jit(solution)/shard_map/ppermute | solution.py:146
  58.5 4.3 %collective-permute-start.4 = (f32[5,128,128]{2,1,0:T(8,128)S(1)}, f32[5,128,128]{2,1,0:T(8,128)S(1)}, u32[]{:S(2)}, u32[]{:S(2)}) collective-permute-start(f32[5,128,128]{2,1,0:T(8,128)S(1)} %collective-permute-done.3.refs_1_), channel_id=1, source_target_pairs={{2,1},{1,0},{6,5},{5,4},{10,9},{9,8},{14,13},{13,12},{18,17},{17,1... | collective-permute-start | bytes 983048 | tf_op jit(solution)/shard_map/ppermute | solution.py:146
  62.8 3.3 %collective-permute-start.23 = (f32[5,128,128]{2,1,0:T(8,128)S(1)}, f32[5,128,128]{2,1,0:T(8,128)S(1)}, u32[]{:S(2)}, u32[]{:S(2)}) collective-permute-start(f32[5,128,128]{2,1,0:T(8,128)S(1)} %collective-permute-done.22.refs_0_), channel_id=1, source_target_pairs={{2,3},{6,7},{10,11},{14,15},{18,19},{22,23},{26,27},{30,31}} | collective-permute-start | bytes 983048 | tf_op jit(solution)/shard_map/ppermute | solution.py:145
  66.1 2.6 %collective-permute-done.1.refs_0_ = f32[5,128,128]{2,1,0:T(8,128)S(1)} collective-permute-done((f32[5,128,128]{2,1,0:T(8,128)S(1)}, f32[5,128,128]{2,1,0:T(8,128)S(1)}, u32[]{:S(2)}, u32[]{:S(2)}) %collective-permute-start.1) | collective-permute-done | bytes 327712 | tf_op jit(solution)/shard_map/ppermute | solution.py:145
  69.4 4.4 %collective-permute-start.16 = (f32[5,128,128]{2,1,0:T(8,128)S(1)}, f32[5,128,128]{2,1,0:T(8,128)S(1)}, u32[]{:S(2)}, u32[]{:S(2)}) collective-permute-start(f32[5,128,128]{2,1,0:T(8,128)S(1)} %collective-permute-done.15.refs_0_), channel_id=1, source_target_pairs={{2,3},{6,7},{10,11},{14,15},{18,19},{22,23},{26,27},{30,31}} | collective-permute-start | bytes 983048 | tf_op jit(solution)/shard_map/ppermute | solution.py:145
  76.4 4.4 %collective-permute-start.10 = (f32[5,128,128]{2,1,0:T(8,128)S(1)}, f32[5,128,128]{2,1,0:T(8,128)S(1)}, u32[]{:S(2)}, u32[]{:S(2)}) collective-permute-start(f32[5,128,128]{2,1,0:T(8,128)S(1)} %collective-permute-done.9.refs_0_), channel_id=1, source_target_pairs={{2,3},{6,7},{10,11},{14,15},{18,19},{22,23},{26,27},{30,31}} | collective-permute-start | bytes 983048 | tf_op jit(solution)/shard_map/ppermute | solution.py:145
  83.5 4.4 %collective-permute-start.2 = (f32[5,128,128]{2,1,0:T(8,128)S(1)}, f32[5,128,128]{2,1,0:T(8,128)S(1)}, u32[]{:S(2)}, u32[]{:S(2)}) collective-permute-start(f32[5,128,128]{2,1,0:T(8,128)S(1)} %collective-permute-done.1.refs_0_), channel_id=1, source_target_pairs={{2,3},{6,7},{10,11},{14,15},{18,19},{22,23},{26,27},{30,31}} | collective-permute-start | bytes 983048 | tf_op jit(solution)/shard_map/ppermute | solution.py:145
  88.6 2.1 %shard_map.28.refs_2_ = f32[16,128,128]{2,1,0:T(8,128)S(1)} custom-call(s32[3,48]{1,0:T(4,128)S(1)} %get-tuple-element.68.tasks_ref, f32[5,128,128]{2,1,0:T(8,128)} %get-tuple-element.17.refs_0_, f32[20,128,128]{2,1,0:T(8,128)S(1)} %bitcast.83), custom_call_target="tpu_custom_call" | custom-call | flops 150994944 | bytes 3735552 | tf_op jit(solution)/shard_map/pallas_call | solution.py:84
  95.8 2.5 %shard_map.32.refs_3_ = f32[16,128,128]{2,1,0:T(8,128)S(1)} custom-call(s32[3,48]{1,0:T(4,128)S(1)} %get-tuple-element.70.tasks_ref, f32[5,128,128]{2,1,0:T(8,128)} %collective-permute-done.21.refs_0_, f32[5,128,128]{2,1,0:T(8,128)} %collective-permute-done.24.refs_1_, f32[20,128,128]{2,1,0:T(8,128)S(1)} %bitcast.84, f32[16,128,128]{2,1,0:T(8,128)S(1)} %shard_map.31.refs_3_), custom_call_target="tpu_custom_call" | custom-call | flops 150994944 | bytes 4063232 | tf_op jit(solution)/shard_map/pallas_call | solution.py:84
  98.4 2.0 %shard_map.33.refs_3_ = f32[16,128,128]{2,1,0:T(8,128)S(1)} custom-call(s32[3,48]{1,0:T(4,128)S(1)} %get-tuple-element.74.tasks_ref, f32[5,128,128]{2,1,0:T(8,128)} %collective-permute-done.14.refs_0_, f32[5,128,128]{2,1,0:T(8,128)} %collective-permute-done.17.refs_1_, f32[20,128,128]{2,1,0:T(8,128)S(1)} %bitcast.96, f32[16,128,128]{2,1,0:T(8,128)S(1)} %shard_map.32.refs_3_), custom_call_target="tpu_custom_call" | custom-call | flops 150994944 | bytes 4063232 | tf_op jit(solution)/shard_map/pallas_call | solution.py:84
  100.4 2.9 %shard_map.34.refs_3_ = f32[16,128,128]{2,1,0:T(8,128)S(1)} custom-call(s32[3,48]{1,0:T(4,128)S(1)} %get-tuple-element.78.tasks_ref, f32[5,128,128]{2,1,0:T(8,128)S(1)} %collective-permute-done.8.refs_0_, f32[5,128,128]{2,1,0:T(8,128)} %collective-permute-done.11.refs_1_, f32[20,128,128]{2,1,0:T(8,128)S(1)} %bitcast.88, f32[16,128,128]{2,1,0:T(8,128)S(1)} %shard_map.33.refs_3_), custom_call_target="tpu_custom_call" | custom-call | flops 150994944 | bytes 4063232 | tf_op jit(solution)/shard_map/pallas_call | solution.py:84
  116.6 2.2 %shard_map.43 = f32[16,128,128]{2,1,0:T(8,128)} custom-call(s32[3,48]{1,0:T(4,128)S(1)} %get-tuple-element.83.tasks_ref, f32[5,128,128]{2,1,0:T(8,128)S(1)} %collective-permute-done.2.refs_0_, f32[5,128,128]{2,1,0:T(8,128)S(1)} %collective-permute-done.5.refs_1_, f32[20,128,128]{2,1,0:T(8,128)S(1)} %bitcast.94, f32[16,128,128]{2,1,0:T(8,128)S(1)} %shard_map.42.refs_3_), custom_call_target="tpu_custom_call" | custom-call | flops 150994944 | bytes 4063232 | tf_op jit(solution)/shard_map/pallas_call | solution.py:84
  (63 shorter events, 40.9 us)
Async XLA Ops:
  0.0 35.6 %collective-permute-start.6 = (f32[4,5,128,128]{3,2,1,0:T(8,128)}, f32[4,5,128,128]{3,2,1,0:T(8,128)S(1)}, u32[]{:S(2)}, u32[]{:S(2)}) collective-permute-start(f32[4,5,128,128]{3,2,1,0:T(8,128)} %bitcast.82), channel_id=1, source_target_pairs={{0,8},{4,12},{8,16},{12,20},{16,24},{20,28},{24,0},{28,4},{1,9},{5... | collective-permute-start | bytes 3932168 | tf_op jit(solution)/shard_map/ppermute | solution.py:115
  3.7 12.8 %collective-permute-start.21 = (f32[5,128,128]{2,1,0:T(8,128)}, f32[5,128,128]{2,1,0:T(8,128)}, u32[]{:S(2)}, u32[]{:S(2)}) collective-permute-start(f32[5,128,128]{2,1,0:T(8,128)} %get-tuple-element.17.refs_0_), channel_id=1, source_target_pairs={{0,1},{1,2},{2,3},{4,5},{5,6},{6,7},{8,9},{9,10},{10,11},{12,13},{... | collective-permute-start | bytes 983048 | tf_op jit(solution)/shard_map/ppermute | solution.py:145
  7.2 12.1 %collective-permute-start.24 = (f32[5,128,128]{2,1,0:T(8,128)}, f32[5,128,128]{2,1,0:T(8,128)}, u32[]{:S(2)}, u32[]{:S(2)}) collective-permute-start(f32[5,128,128]{2,1,0:T(8,128)} %get-tuple-element.17.refs_0_), channel_id=1, source_target_pairs={{3,2},{2,1},{1,0},{7,6},{6,5},{5,4},{11,10},{10,9},{9,8},{15,14},{... | collective-permute-start | bytes 983048 | tf_op jit(solution)/shard_map/ppermute | solution.py:146
  9.6 13.6 %collective-permute-start.14 = (f32[5,128,128]{2,1,0:T(8,128)}, f32[5,128,128]{2,1,0:T(8,128)}, u32[]{:S(2)}, u32[]{:S(2)}) collective-permute-start(f32[5,128,128]{2,1,0:T(8,128)} %get-tuple-element.18.refs_0_), channel_id=1, source_target_pairs={{0,1},{1,2},{2,3},{4,5},{5,6},{6,7},{8,9},{9,10},{10,11},{12,13},{... | collective-permute-start | bytes 983048 | tf_op jit(solution)/shard_map/ppermute | solution.py:145
  13.8 12.9 %collective-permute-start.17 = (f32[5,128,128]{2,1,0:T(8,128)}, f32[5,128,128]{2,1,0:T(8,128)}, u32[]{:S(2)}, u32[]{:S(2)}) collective-permute-start(f32[5,128,128]{2,1,0:T(8,128)} %get-tuple-element.18.refs_0_), channel_id=1, source_target_pairs={{3,2},{2,1},{1,0},{7,6},{6,5},{5,4},{11,10},{10,9},{9,8},{15,14},{... | collective-permute-start | bytes 983048 | tf_op jit(solution)/shard_map/ppermute | solution.py:146
  16.5 17.1 %collective-permute-start.11 = (f32[5,128,128]{2,1,0:T(8,128)S(1)}, f32[5,128,128]{2,1,0:T(8,128)}, u32[]{:S(2)}, u32[]{:S(2)}) collective-permute-start(f32[5,128,128]{2,1,0:T(8,128)S(1)} %get-tuple-element.19.refs_0_), channel_id=1, source_target_pairs={{3,2},{2,1},{1,0},{7,6},{6,5},{5,4},{11,10},{10,9},{9,8},{15,14},{... | collective-permute-start | bytes 983048 | tf_op jit(solution)/shard_map/ppermute | solution.py:146
  19.3 20.4 %collective-permute-start.8 = (f32[5,128,128]{2,1,0:T(8,128)S(1)}, f32[5,128,128]{2,1,0:T(8,128)S(1)}, u32[]{:S(2)}, u32[]{:S(2)}) collective-permute-start(f32[5,128,128]{2,1,0:T(8,128)S(1)} %get-tuple-element.19.refs_0_), channel_id=1, source_target_pairs={{0,1},{1,2},{2,3},{4,5},{5,6},{6,7},{8,9},{9,10},{10,11},{12,13},{... | collective-permute-start | bytes 983048 | tf_op jit(solution)/shard_map/ppermute | solution.py:145
  23.2 18.5 %collective-permute-start = (f32[5,128,128]{2,1,0:T(8,128)S(1)}, f32[5,128,128]{2,1,0:T(8,128)S(1)}, u32[]{:S(2)}, u32[]{:S(2)}) collective-permute-start(f32[5,128,128]{2,1,0:T(8,128)S(1)} %get-tuple-element.20.refs_0_), channel_id=1, source_target_pairs={{0,1},{1,2},{2,3},{4,5},{5,6},{6,7},{8,9},{9,10},{10,11},{12,13},{... | collective-permute-start | bytes 983048 | tf_op jit(solution)/shard_map/ppermute | solution.py:145
  26.6 19.0 %collective-permute-start.3 = (f32[5,128,128]{2,1,0:T(8,128)S(1)}, f32[5,128,128]{2,1,0:T(8,128)S(1)}, u32[]{:S(2)}, u32[]{:S(2)}) collective-permute-start(f32[5,128,128]{2,1,0:T(8,128)S(1)} %get-tuple-element.20.refs_0_), channel_id=1, source_target_pairs={{3,2},{2,1},{1,0},{7,6},{6,5},{5,4},{11,10},{10,9},{9,8},{15,14},{... | collective-permute-start | bytes 983048 | tf_op jit(solution)/shard_map/ppermute | solution.py:146
  33.7 14.0 %collective-permute-start.22 = (f32[5,128,128]{2,1,0:T(8,128)}, f32[5,128,128]{2,1,0:T(8,128)S(1)}, u32[]{:S(2)}, u32[]{:S(2)}) collective-permute-start(f32[5,128,128]{2,1,0:T(8,128)} %collective-permute-done.21.refs_0_), channel_id=1, source_target_pairs={{1,2},{2,3},{5,6},{6,7},{9,10},{10,11},{13,14},{14,15},{17,18},{18... | collective-permute-start | bytes 983048 | tf_op jit(solution)/shard_map/ppermute | solution.py:145
  35.6 12.1 %collective-permute-start.25 = (f32[5,128,128]{2,1,0:T(8,128)}, f32[5,128,128]{2,1,0:T(8,128)S(1)}, u32[]{:S(2)}, u32[]{:S(2)}) collective-permute-start(f32[5,128,128]{2,1,0:T(8,128)} %collective-permute-done.24.refs_1_), channel_id=1, source_target_pairs={{2,1},{1,0},{6,5},{5,4},{10,9},{9,8},{14,13},{13,12},{18,17},{17,1... | collective-permute-start | bytes 983048 | tf_op jit(solution)/shard_map/ppermute | solution.py:146
  41.7 12.4 %collective-permute-start.18 = (f32[5,128,128]{2,1,0:T(8,128)}, f32[5,128,128]{2,1,0:T(8,128)S(1)}, u32[]{:S(2)}, u32[]{:S(2)}) collective-permute-start(f32[5,128,128]{2,1,0:T(8,128)} %collective-permute-done.17.refs_1_), channel_id=1, source_target_pairs={{2,1},{1,0},{6,5},{5,4},{10,9},{9,8},{14,13},{13,12},{18,17},{17,1... | collective-permute-start | bytes 983048 | tf_op jit(solution)/shard_map/ppermute | solution.py:146
  45.7 12.8 %collective-permute-start.12 = (f32[5,128,128]{2,1,0:T(8,128)}, f32[5,128,128]{2,1,0:T(8,128)S(1)}, u32[]{:S(2)}, u32[]{:S(2)}) collective-permute-start(f32[5,128,128]{2,1,0:T(8,128)} %collective-permute-done.11.refs_1_), channel_id=1, source_target_pairs={{2,1},{1,0},{6,5},{5,4},{10,9},{9,8},{14,13},{13,12},{18,17},{17,1... | collective-permute-start | bytes 983048 | tf_op jit(solution)/shard_map/ppermute | solution.py:146
  47.6 35.8 %collective-permute-start.20 = (f32[4,5,128,128]{3,2,1,0:T(8,128)S(1)}, f32[4,5,128,128]{3,2,1,0:T(8,128)S(1)}, u32[]{:S(2)}, u32[]{:S(2)}) collective-permute-start(f32[4,5,128,128]{3,2,1,0:T(8,128)S(1)} %get-tuple-element.15), channel_id=1, source_target_pairs={{0,4},{4,0},{8,12},{12,8},{16,20},{20,16},{24,28},{28,24},{1,5},{5... | collective-permute-start | bytes 3932168 | tf_op jit(solution)/shard_map/ppermute | solution.py:116
  47.7 40.2 %collective-permute-start.7 = (f32[4,5,128,128]{3,2,1,0:T(8,128)S(1)}, f32[4,5,128,128]{3,2,1,0:T(8,128)S(1)}, u32[]{:S(2)}, u32[]{:S(2)}) collective-permute-start(f32[4,5,128,128]{3,2,1,0:T(8,128)S(1)} %get-tuple-element.16), channel_id=1, source_target_pairs={{0,4},{4,16},{8,12},{12,24},{16,20},{20,0},{24,28},{28,8},{1,5},{5... | collective-permute-start | bytes 3932168 | tf_op jit(solution)/shard_map/ppermute | solution.py:119
  50.1 12.7 %collective-permute-start.9 = (f32[5,128,128]{2,1,0:T(8,128)S(1)}, f32[5,128,128]{2,1,0:T(8,128)S(1)}, u32[]{:S(2)}, u32[]{:S(2)}) collective-permute-start(f32[5,128,128]{2,1,0:T(8,128)S(1)} %collective-permute-done.8.refs_0_), channel_id=1, source_target_pairs={{1,2},{2,3},{5,6},{6,7},{9,10},{10,11},{13,14},{14,15},{17,18},{18... | collective-permute-start | bytes 983048 | tf_op jit(solution)/shard_map/ppermute | solution.py:145
  54.1 14.6 %collective-permute-start.1 = (f32[5,128,128]{2,1,0:T(8,128)S(1)}, f32[5,128,128]{2,1,0:T(8,128)S(1)}, u32[]{:S(2)}, u32[]{:S(2)}) collective-permute-start(f32[5,128,128]{2,1,0:T(8,128)S(1)} %collective-permute-done.refs_0_), channel_id=1, source_target_pairs={{1,2},{2,3},{5,6},{6,7},{9,10},{10,11},{13,14},{14,15},{17,18},{18... | collective-permute-start | bytes 983048 | tf_op jit(solution)/shard_map/ppermute | solution.py:145
  62.8 12.9 %collective-permute-start.23 = (f32[5,128,128]{2,1,0:T(8,128)S(1)}, f32[5,128,128]{2,1,0:T(8,128)S(1)}, u32[]{:S(2)}, u32[]{:S(2)}) collective-permute-start(f32[5,128,128]{2,1,0:T(8,128)S(1)} %collective-permute-done.22.refs_0_), channel_id=1, source_target_pairs={{2,3},{6,7},{10,11},{14,15},{18,19},{22,23},{26,27},{30,31}} | collective-permute-start | bytes 983048 | tf_op jit(solution)/shard_map/ppermute | solution.py:145
  69.4 13.4 %collective-permute-start.16 = (f32[5,128,128]{2,1,0:T(8,128)S(1)}, f32[5,128,128]{2,1,0:T(8,128)S(1)}, u32[]{:S(2)}, u32[]{:S(2)}) collective-permute-start(f32[5,128,128]{2,1,0:T(8,128)S(1)} %collective-permute-done.15.refs_0_), channel_id=1, source_target_pairs={{2,3},{6,7},{10,11},{14,15},{18,19},{22,23},{26,27},{30,31}} | collective-permute-start | bytes 983048 | tf_op jit(solution)/shard_map/ppermute | solution.py:145
  75.8 38.3 %collective-permute-start.19 = (f32[5,128,128]{2,1,0:T(8,128)S(1)}, f32[5,128,128]{2,1,0:T(8,128)S(1)}, u32[]{:S(2)}, u32[]{:S(2)}) collective-permute-start(f32[5,128,128]{2,1,0:T(8,128)S(1)} %collective-permute-done.18.refs_1_), channel_id=1, source_target_pairs={{1,0},{5,4},{9,8},{13,12},{17,16},{21,20},{25,24},{29,28}} | collective-permute-start | bytes 983048 | tf_op jit(solution)/shard_map/ppermute | solution.py:146
  76.4 38.9 %collective-permute-start.10 = (f32[5,128,128]{2,1,0:T(8,128)S(1)}, f32[5,128,128]{2,1,0:T(8,128)S(1)}, u32[]{:S(2)}, u32[]{:S(2)}) collective-permute-start(f32[5,128,128]{2,1,0:T(8,128)S(1)} %collective-permute-done.9.refs_0_), channel_id=1, source_target_pairs={{2,3},{6,7},{10,11},{14,15},{18,19},{22,23},{26,27},{30,31}} | collective-permute-start | bytes 983048 | tf_op jit(solution)/shard_map/ppermute | solution.py:145
  82.8 32.5 %collective-permute-start.13 = (f32[5,128,128]{2,1,0:T(8,128)S(1)}, f32[5,128,128]{2,1,0:T(8,128)S(1)}, u32[]{:S(2)}, u32[]{:S(2)}) collective-permute-start(f32[5,128,128]{2,1,0:T(8,128)S(1)} %collective-permute-done.12.refs_1_), channel_id=1, source_target_pairs={{1,0},{5,4},{9,8},{13,12},{17,16},{21,20},{25,24},{29,28}} | collective-permute-start | bytes 983048 | tf_op jit(solution)/shard_map/ppermute | solution.py:146
  83.5 33.1 %collective-permute-start.2 = (f32[5,128,128]{2,1,0:T(8,128)S(1)}, f32[5,128,128]{2,1,0:T(8,128)S(1)}, u32[]{:S(2)}, u32[]{:S(2)}) collective-permute-start(f32[5,128,128]{2,1,0:T(8,128)S(1)} %collective-permute-done.1.refs_0_), channel_id=1, source_target_pairs={{2,3},{6,7},{10,11},{14,15},{18,19},{22,23},{26,27},{30,31}} | collective-permute-start | bytes 983048 | tf_op jit(solution)/shard_map/ppermute | solution.py:145
  87.9 28.7 %collective-permute-start.5 = (f32[5,128,128]{2,1,0:T(8,128)S(1)}, f32[5,128,128]{2,1,0:T(8,128)S(1)}, u32[]{:S(2)}, u32[]{:S(2)}) collective-permute-start(f32[5,128,128]{2,1,0:T(8,128)S(1)} %collective-permute-done.4.refs_1_), channel_id=1, source_target_pairs={{1,0},{5,4},{9,8},{13,12},{17,16},{21,20},{25,24},{29,28}} | collective-permute-start | bytes 983048 | tf_op jit(solution)/shard_map/ppermute | solution.py:146
  (5 other events, 87.8 us)

commit v2 on v1

v2 whole, which is shorter than its diff:
```python
import functools

import jax
import jax.numpy as jnp
from jax import lax
from jax.experimental import pallas as pl
from jax.experimental.pallas import tpu as pltpu
from jax.sharding import PartitionSpec as P

NC = 16
UNROLL = 4


def split(value):
    high = value.astype(jnp.bfloat16)
    low = (value - high.astype(jnp.float32)).astype(jnp.bfloat16)
    return high, low


def contract_kernel(n_left, n_right, first, tasks_ref, *refs):
    left_refs, right_refs = refs[:n_left], refs[n_left : n_left + n_right]
    rest = refs[n_left + n_right :]
    if first:
        out_ref, left_split, total, live = rest
    else:
        before_ref, out_ref, left_split, total, live = rest
    tile = right_refs[0].shape[-1]
    slots = tasks_ref.shape[-1]

    if first:
        total[...] = jnp.zeros_like(total)
    else:
        total[:NC] = before_ref[...]

    base = 0
    for ref in left_refs:
        for s in range(ref.shape[0]):
            for t in range(ref.shape[1]):
                high, low = split(ref[s, t])
                left_split[base, :, :tile] = high
                left_split[base, :, tile:] = low
                base += 1

    for s, right_ref in enumerate(right_refs):
        def pack(j, count):
            live[count] = j
            return count + jnp.where(tasks_ref[s, 2, j] < NC, 1, 0)

        count = lax.fori_loop(0, slots, pack, 0)
        for extra in range(UNROLL):
            live[count + extra] = slots

        def some(i, carry):
            products, targets = [], []
            for u in range(UNROLL):
                j = live[i * UNROLL + u]
                dead = j >= slots
                at = jnp.where(dead, 0, j)
                high, low = split(right_ref[tasks_ref[s, 1, at]])
                both = jnp.concatenate(
                    [
                        jnp.concatenate([high, low], axis=1),
                        jnp.concatenate([high, jnp.zeros_like(low)], axis=1),
                    ],
                    axis=0,
                )
                wide = jnp.dot(
                    left_split[tasks_ref[s, 0, at]], both, preferred_element_type=jnp.float32
                )
                products.append(wide[:, :tile] + wide[:, tile:])
                targets.append(jnp.where(dead, NC, tasks_ref[s, 2, at]))
            for product, target in zip(products, targets):
                total[target] += product
            return carry

        lax.fori_loop(0, (count + UNROLL - 1) // UNROLL, some, 0)
    out_ref[...] = total[:NC]


def contract(tasks, lefts, rights, before):
    tile = rights[0].shape[-1]
    n_tiles = sum(left.shape[0] * left.shape[1] for left in lefts)
    steps, _, slots = tasks.shape
    vmem = pl.BlockSpec(memory_space=pltpu.VMEM)
    operands = [tasks, *lefts, *rights] + ([] if before is None else [before])
    return pl.pallas_call(
        functools.partial(contract_kernel, len(lefts), len(rights), before is None),
        out_shape=jax.ShapeDtypeStruct((NC, tile, tile), jnp.float32),
        in_specs=[pl.BlockSpec(memory_space=pltpu.SMEM)] + [vmem] * (len(operands) - 1),
        out_specs=vmem,
        scratch_shapes=[
            pltpu.VMEM((n_tiles, tile, 2 * tile), jnp.bfloat16),
            pltpu.VMEM((NC + 1, tile, tile), jnp.float32),
            pltpu.SMEM((slots + UNROLL,), jnp.int32),
        ],
        compiler_params=pltpu.CompilerParams(vmem_limit_bytes=24 * 2**20),
        cost_estimate=pl.CostEstimate(
            flops=1150 * 10**6 * steps,
            bytes_accessed=4 * tile * tile * 2 * NC,
            transcendentals=0,
        ),
    )(*operands)


def shift_pairs(count, by):
    return [(i, (i + by) % count) for i in range(count)]


def right_panels(own):
    panels, steps = lax.axis_size("blk"), own.shape[0]
    if steps != 4 or panels % 2:
        found = [own]
        for step in range(1, steps):
            found.append(lax.ppermute(own, "blk", shift_pairs(panels, step)))
        return found
    odd = lax.axis_index("blk") % 2 == 1
    two = lax.ppermute(own, "blk", shift_pairs(panels, 2))
    one = lax.ppermute(
        jnp.where(odd, two, own), "blk", [(i, i ^ 1) for i in range(panels)]
    )
    three = lax.ppermute(
        jnp.where(odd, own, two),
        "blk",
        [(i, (i + 3) % panels if i % 2 else i + 1) for i in range(panels)],
    )
    return [own, one, two, three]


def gathered(own):
    slivers = lax.axis_size("rep")
    me = lax.axis_index("rep")
    if slivers != 4:
        whole = lax.all_gather(own, "rep", axis=0)
        return [([i], (whole[i],)) for i in range(slivers)]
    outer = [(0, 1), (1, 0), (2, 3), (3, 2)]
    inner = [(1, 2), (2, 1)]
    ends = [(1, 0), (2, 3)]
    side = lax.ppermute(own, "rep", outer)
    near = lax.ppermute(own, "rep", inner)
    far = lax.ppermute(side, "rep", inner)
    near_end = lax.ppermute(near, "rep", ends)
    far_end = lax.ppermute(far, "rep", ends)
    low = me < 2
    middle = (me == 1) | (me == 2)
    pick = lambda number: jnp.where(middle, number, -1), lambda number: jnp.where(middle, -1, number)
    inner_of_other, outer_of_other = jnp.where(low, 2, 1), jnp.where(low, 3, 0)
    return [
        ([me], (own,)),
        ([me ^ 1], (side,)),
        ([pick[0](inner_of_other), pick[1](inner_of_other)], (near, near_end)),
        ([pick[0](outer_of_other), pick[1](outer_of_other)], (far, far_end)),
    ]


def per_device(p_tiles, tasks):
    own = p_tiles[0, 0]
    lists = tasks[0, 0]
    steps, per, tile = own.shape[0], own.shape[1], own.shape[-1]
    right = [panel.reshape(-1, tile, tile) for panel in right_panels(own)]
    sliver, spot = lists[:, 0] // per, lists[:, 0] % per
    spot = spot + per * jnp.arange(steps, dtype=spot.dtype)[:, None]

    total = None
    for numbers, lefts in gathered(own):
        here, place = False, 0
        for i, number in enumerate(numbers):
            this = sliver == number
            here = here | this
            place = place + jnp.where(this, spot + i * steps * per, 0)
        stage = jnp.stack([place, lists[:, 1], jnp.where(here, lists[:, 2], NC)], axis=1)
        total = contract(stage, lefts, right, total)
    return total[None, None]


def solution(mesh):
    return jax.shard_map(
        per_device,
        mesh=mesh,
        in_specs=(P("blk", "rep", None, None, None, None), P("blk", "rep", None, None, None)),
        out_specs=P("blk", "rep", None, None, None),
        check_vma=False,
    )
```

time: 121 us -> 108 us (0.89)
  the two profiles are of different devices: /device:TPU:18 before, /device:TPU:1 now
where the time goes in v2:
time: 108 us; the launch traced here: 106 us
  waiting for transfers between devices  67.4 us (62%)
  Pallas kernels  23.3 us (22%)
  starting transfers between devices  12.2 us (11%)
  other arithmetic  3.22 us (3%)
    ppermute x1, waiting for transfers between devices, gathered(): side = lax.ppermute(own, 'rep', outer)  25.9 us
    pallas_call x4, Pallas kernels, contract(): pl.pallas_call(functools.partial(contract_kernel, len(lefts), len(rights)...  23.3 us
    ppermute x1, waiting for transfers between devices, gathered(): far_end = lax.ppermute(far, 'rep', ends)  20.9 us
    ppermute x1, waiting for transfers between devices, right_panels(): lax.ppermute(jnp.where(odd, own, two), 'blk', [(i, (i + 3) % panels if i...  12.1 us
    ppermute x1, waiting for transfers between devices, gathered(): near_end = lax.ppermute(near, 'rep', ends)  8.53 us
    select_n x1, other arithmetic, right_panels(): jnp.where(odd, own, two)  3.09 us
  transfers between devices with their start and end apart: 8, of which 4 were waited for; matrix products, arithmetic and copies ran while one was open for 3% of the time, Pallas kernels for 16%

profile of v2, /device:TPU:1, one launch (start us, length us, event | category | flops | bytes accessed | tf_op | source)
XLA Modules:
  0.0 106.2 jit_solution(456640449950538926)
XLA Ops:
  0.0 2.1 %collective-permute-start = (f32[4,5,128,128]{3,2,1,0:T(8,128)}, f32[4,5,128,128]{3,2,1,0:T(8,128)}, u32[]{:S(2)}, u32[]{:S(2)}) collective-permute-start(f32[4,5,128,128]{3,2,1,0:T(8,128)} %bitcast.11), channel_id=1, source_target_pairs={{0,1},{1,0},{2,3},{3,2},{4,5},{5,4},{6,7},{7,6},{8,9},{9,8},{10,11... | collective-permute-start | bytes 3932168 | tf_op jit(solution)/shard_map/ppermute | solution.py:138
  2.1 1.2 %collective-permute-start.3 = (f32[4,5,128,128]{3,2,1,0:T(8,128)}, f32[4,5,128,128]{3,2,1,0:T(8,128)S(1)}, u32[]{:S(2)}, u32[]{:S(2)}) collective-permute-start(f32[4,5,128,128]{3,2,1,0:T(8,128)} %bitcast.12), channel_id=1, source_target_pairs={{0,8},{4,12},{8,16},{12,20},{16,24},{20,28},{24,0},{28,4},{1,9},{5... | collective-permute-start | bytes 3932168 | tf_op jit(solution)/shard_map/ppermute | solution.py:117
  3.3 1.7 %collective-permute-start.6 = (f32[4,5,128,128]{3,2,1,0:T(8,128)}, f32[4,5,128,128]{3,2,1,0:T(8,128)}, u32[]{:S(2)}, u32[]{:S(2)}) collective-permute-start(f32[4,5,128,128]{3,2,1,0:T(8,128)} %bitcast.13), channel_id=1, source_target_pairs={{1,2},{2,1},{5,6},{6,5},{9,10},{10,9},{13,14},{14,13},{17,18},{18,... | collective-permute-start | bytes 3932168 | tf_op jit(solution)/shard_map/ppermute | solution.py:139
  5.1 25.9 %collective-permute-done.refs_0_ = f32[4,5,128,128]{3,2,1,0:T(8,128)} collective-permute-done((f32[4,5,128,128]{3,2,1,0:T(8,128)}, f32[4,5,128,128]{3,2,1,0:T(8,128)}, u32[]{:S(2)}, u32[]{:S(2)}) %collective-permute-start) | collective-permute-done | bytes 1310752 | tf_op jit(solution)/shard_map/ppermute | solution.py:138
  30.9 1.7 %collective-permute-start.1 = (f32[4,5,128,128]{3,2,1,0:T(8,128)}, f32[4,5,128,128]{3,2,1,0:T(8,128)}, u32[]{:S(2)}, u32[]{:S(2)}) collective-permute-start(f32[4,5,128,128]{3,2,1,0:T(8,128)} %collective-permute-done.refs_0_), channel_id=1, source_target_pairs={{1,2},{2,1},{5,6},{6,5},{9,10},{10,9},{13,14},{14,13},{17,18},{18,... | collective-permute-start | bytes 3932168 | tf_op jit(solution)/shard_map/ppermute | solution.py:140
  32.7 0.0 collective-permute-done.3
  32.7 3.1 %broadcast_select_fusion = (f32[4,5,128,128]{3,2,1,0:T(8,128)}, f32[4,5,128,128]{3,2,1,0:T(8,128)}) fusion(f32[4,5,128,128]{3,2,1,0:T(8,128)S(1)} %collective-permute-done.3, pred[]{:T(512)S(6)} %eq.67, f32[1,1,4,5,128,128]{5,4,3,2,1,0:T(8,128)} %param.2), kind=kLoop, calls=%fused_computation | loop fusion | flops 655360 | bytes 5242881 | tf_op jit(solution)/shard_map/jit(_where)/select_n | solution.py:122
  35.8 1.7 %collective-permute-start.4 = (f32[4,5,128,128]{3,2,1,0:T(8,128)}, f32[4,5,128,128]{3,2,1,0:T(8,128)}, u32[]{:S(2)}, u32[]{:S(2)}) collective-permute-start(f32[4,5,128,128]{3,2,1,0:T(8,128)} %get-tuple-element.9), channel_id=1, source_target_pairs={{0,4},{4,0},{8,12},{12,8},{16,20},{20,16},{24,28},{28,24},{1,5},{5... | collective-permute-start | bytes 3932168 | tf_op jit(solution)/shard_map/ppermute | solution.py:118
  37.5 1.1 %collective-permute-start.5 = (f32[4,5,128,128]{3,2,1,0:T(8,128)}, f32[4,5,128,128]{3,2,1,0:T(8,128)}, u32[]{:S(2)}, u32[]{:S(2)}) collective-permute-start(f32[4,5,128,128]{3,2,1,0:T(8,128)} %get-tuple-element.8), channel_id=1, source_target_pairs={{0,4},{4,16},{8,12},{12,24},{16,20},{20,0},{24,28},{28,8},{1,5},{5... | collective-permute-start | bytes 3932168 | tf_op jit(solution)/shard_map/ppermute | solution.py:121
  38.7 0.0 copy-done.1
  38.7 0.0 collective-permute-done.6.refs_0_
  38.7 1.3 %collective-permute-start.7 = (f32[4,5,128,128]{3,2,1,0:T(8,128)}, f32[4,5,128,128]{3,2,1,0:T(8,128)}, u32[]{:S(2)}, u32[]{:S(2)}) collective-permute-start(f32[4,5,128,128]{3,2,1,0:T(8,128)} %collective-permute-done.6.refs_0_), channel_id=1, source_target_pairs={{1,0},{2,3},{5,4},{6,7},{9,8},{10,11},{13,12},{14,15},{17,16},{18,... | collective-permute-start | bytes 3932168 | tf_op jit(solution)/shard_map/ppermute | solution.py:141
  40.0 0.1 compare_select_fusion.1
  40.1 0.0 collective-permute-done.1.refs_0_
  40.1 1.3 %collective-permute-start.2 = (f32[4,5,128,128]{3,2,1,0:T(8,128)}, f32[4,5,128,128]{3,2,1,0:T(8,128)S(1)}, u32[]{:S(2)}, u32[]{:S(2)}) collective-permute-start(f32[4,5,128,128]{3,2,1,0:T(8,128)} %collective-permute-done.1.refs_0_), channel_id=1, source_target_pairs={{1,0},{2,3},{5,4},{6,7},{9,8},{10,11},{13,12},{14,15},{17,16},{18,... | collective-permute-start | bytes 3932168 | tf_op jit(solution)/shard_map/ppermute | solution.py:142
  41.4 0.0 collective-permute-done.4
  41.4 12.1 %collective-permute-done.5 = f32[4,5,128,128]{3,2,1,0:T(8,128)} collective-permute-done((f32[4,5,128,128]{3,2,1,0:T(8,128)}, f32[4,5,128,128]{3,2,1,0:T(8,128)}, u32[]{:S(2)}, u32[]{:S(2)}) %collective-permute-start.5) | collective-permute-done | bytes 1310752 | tf_op jit(solution)/shard_map/ppermute | solution.py:121
  53.5 0.0 copy-done
  53.5 4.6 %shard_map.28.refs_5_ = f32[16,128,128]{2,1,0:T(8,128)S(1)} custom-call(s32[4,3,48]{2,1,0:T(4,128)S(1)} %get-tuple-element.18.tasks_ref, f32[4,5,128,128]{3,2,1,0:T(8,128)S(1)} %bitcast.14, f32[20,128,128]{2,1,0:T(8,128)S(1)} %bitcast.15, f32[20,128,128]{2,1,0:T(8,128)} %bitcast.3.refs_2_.refs_3_, f32[20,128,128]{2,1,0:T(8,128)S(1)} %bitcast.19, ...), custom_call_target="tpu_custom_call" | custom-call | flops 4600000000 | bytes 2097152 | tf_op jit(solution)/shard_map/pallas_call | solution.py:86
  58.1 5.5 %shard_map.29.refs_6_ = f32[16,128,128]{2,1,0:T(8,128)S(1)} custom-call(s32[4,3,48]{2,1,0:T(4,128)S(1)} %get-tuple-element.20.tasks_ref, f32[4,5,128,128]{3,2,1,0:T(8,128)} %collective-permute-done.refs_0_, f32[20,128,128]{2,1,0:T(8,128)S(1)} %bitcast.16, f32[20,128,128]{2,1,0:T(8,128)} %bitcast.3.refs_2_.refs_3_, f32[20,128,128]{2,1,0:T(8,128)S(1)} %bitcast.20, ...), custom_call_target="tpu_custom_call" | custom-call | flops 4600000000 | bytes 2097152 | tf_op jit(solution)/shard_map/pallas_call | solution.py:86
  63.6 8.5 %collective-permute-done.7.refs_1_ = f32[4,5,128,128]{3,2,1,0:T(8,128)} collective-permute-done((f32[4,5,128,128]{3,2,1,0:T(8,128)}, f32[4,5,128,128]{3,2,1,0:T(8,128)}, u32[]{:S(2)}, u32[]{:S(2)}) %collective-permute-start.7) | collective-permute-done | bytes 1310752 | tf_op jit(solution)/shard_map/ppermute | solution.py:141
  72.1 6.6 %shard_map.30.refs_6_ = f32[16,128,128]{2,1,0:T(8,128)S(1)} custom-call(s32[4,3,48]{2,1,0:T(4,128)S(1)} %get-tuple-element.19.tasks_ref, f32[4,5,128,128]{3,2,1,0:T(8,128)} %collective-permute-done.6.refs_0_, f32[4,5,128,128]{3,2,1,0:T(8,128)} %collective-permute-done.7.refs_1_, f32[20,128,128]{2,1,0:T(8,128)S(1)} %bitcast.17, ...), custom_call_target="tpu_custom_call" | custom-call | flops 4600000000 | bytes 2097152 | tf_op jit(solution)/shard_map/pallas_call | solution.py:86
  78.7 20.9 %collective-permute-done.2.refs_1_ = f32[4,5,128,128]{3,2,1,0:T(8,128)S(1)} collective-permute-done((f32[4,5,128,128]{3,2,1,0:T(8,128)}, f32[4,5,128,128]{3,2,1,0:T(8,128)S(1)}, u32[]{:S(2)}, u32[]{:S(2)}) %collective-permute-start.2) | collective-permute-done | bytes 1310752 | tf_op jit(solution)/shard_map/ppermute | solution.py:142
  99.6 6.7 %shard_map.31 = f32[16,128,128]{2,1,0:T(8,128)} custom-call(s32[4,3,48]{2,1,0:T(4,128)S(1)} %get-tuple-element.21.tasks_ref, f32[4,5,128,128]{3,2,1,0:T(8,128)} %collective-permute-done.1.refs_0_, f32[4,5,128,128]{3,2,1,0:T(8,128)S(1)} %collective-permute-done.2.refs_1_, f32[20,128,128]{2,1,0:T(8,128)S(1)} %bitcast.18, ...), custom_call_target="tpu_custom_call" | custom-call | flops 4600000000 | bytes 2097152 | tf_op jit(solution)/shard_map/pallas_call | solution.py:86
  (6 shorter events, 0.1 us)
Async XLA Ops:
  0.0 30.9 %collective-permute-start = (f32[4,5,128,128]{3,2,1,0:T(8,128)}, f32[4,5,128,128]{3,2,1,0:T(8,128)}, u32[]{:S(2)}, u32[]{:S(2)}) collective-permute-start(f32[4,5,128,128]{3,2,1,0:T(8,128)} %bitcast.11), channel_id=1, source_target_pairs={{0,1},{1,0},{2,3},{3,2},{4,5},{5,4},{6,7},{7,6},{8,9},{9,8},{10,11... | collective-permute-start | bytes 3932168 | tf_op jit(solution)/shard_map/ppermute | solution.py:138
  2.1 30.6 %collective-permute-start.3 = (f32[4,5,128,128]{3,2,1,0:T(8,128)}, f32[4,5,128,128]{3,2,1,0:T(8,128)S(1)}, u32[]{:S(2)}, u32[]{:S(2)}) collective-permute-start(f32[4,5,128,128]{3,2,1,0:T(8,128)} %bitcast.12), channel_id=1, source_target_pairs={{0,8},{4,12},{8,16},{12,20},{16,24},{20,28},{24,0},{28,4},{1,9},{5... | collective-permute-start | bytes 3932168 | tf_op jit(solution)/shard_map/ppermute | solution.py:117
  3.3 35.3 %collective-permute-start.6 = (f32[4,5,128,128]{3,2,1,0:T(8,128)}, f32[4,5,128,128]{3,2,1,0:T(8,128)}, u32[]{:S(2)}, u32[]{:S(2)}) collective-permute-start(f32[4,5,128,128]{3,2,1,0:T(8,128)} %bitcast.13), channel_id=1, source_target_pairs={{1,2},{2,1},{5,6},{6,5},{9,10},{10,9},{13,14},{14,13},{17,18},{18,... | collective-permute-start | bytes 3932168 | tf_op jit(solution)/shard_map/ppermute | solution.py:139
  5.1 33.6 %copy-start.1 = (s32[1,1,4,3,48]{4,2,3,1,0:T(4,128)S(1)}, s32[1,1,4,3,48]{4,2,3,1,0:T(4,128)}, u32[]{:S(2)}) copy-start(s32[1,1,4,3,48]{4,2,3,1,0:T(4,128)} %param.3) | copy-start | bytes 6916
  5.1 48.5 %copy-start = (f32[1,1,4,5,128,128]{5,4,3,2,1,0:T(8,128)S(1)}, f32[1,1,4,5,128,128]{5,4,3,2,1,0:T(8,128)}, u32[]{:S(2)}) copy-start(f32[1,1,4,5,128,128]{5,4,3,2,1,0:T(8,128)} %param.2) | copy-start | bytes 3932164
  30.9 9.1 %collective-permute-start.1 = (f32[4,5,128,128]{3,2,1,0:T(8,128)}, f32[4,5,128,128]{3,2,1,0:T(8,128)}, u32[]{:S(2)}, u32[]{:S(2)}) collective-permute-start(f32[4,5,128,128]{3,2,1,0:T(8,128)} %collective-permute-done.refs_0_), channel_id=1, source_target_pairs={{1,2},{2,1},{5,6},{6,5},{9,10},{10,9},{13,14},{14,13},{17,18},{18,... | collective-permute-start | bytes 3932168 | tf_op jit(solution)/shard_map/ppermute | solution.py:140
  35.8 5.6 %collective-permute-start.4 = (f32[4,5,128,128]{3,2,1,0:T(8,128)}, f32[4,5,128,128]{3,2,1,0:T(8,128)}, u32[]{:S(2)}, u32[]{:S(2)}) collective-permute-start(f32[4,5,128,128]{3,2,1,0:T(8,128)} %get-tuple-element.9), channel_id=1, source_target_pairs={{0,4},{4,0},{8,12},{12,8},{16,20},{20,16},{24,28},{28,24},{1,5},{5... | collective-permute-start | bytes 3932168 | tf_op jit(solution)/shard_map/ppermute | solution.py:118
  37.5 16.0 %collective-permute-start.5 = (f32[4,5,128,128]{3,2,1,0:T(8,128)}, f32[4,5,128,128]{3,2,1,0:T(8,128)}, u32[]{:S(2)}, u32[]{:S(2)}) collective-permute-start(f32[4,5,128,128]{3,2,1,0:T(8,128)} %get-tuple-element.8), channel_id=1, source_target_pairs={{0,4},{4,16},{8,12},{12,24},{16,20},{20,0},{24,28},{28,8},{1,5},{5... | collective-permute-start | bytes 3932168 | tf_op jit(solution)/shard_map/ppermute | solution.py:121
  38.7 33.4 %collective-permute-start.7 = (f32[4,5,128,128]{3,2,1,0:T(8,128)}, f32[4,5,128,128]{3,2,1,0:T(8,128)}, u32[]{:S(2)}, u32[]{:S(2)}) collective-permute-start(f32[4,5,128,128]{3,2,1,0:T(8,128)} %collective-permute-done.6.refs_0_), channel_id=1, source_target_pairs={{1,0},{2,3},{5,4},{6,7},{9,8},{10,11},{13,12},{14,15},{17,16},{18,... | collective-permute-start | bytes 3932168 | tf_op jit(solution)/shard_map/ppermute | solution.py:141
  40.1 59.5 %collective-permute-start.2 = (f32[4,5,128,128]{3,2,1,0:T(8,128)}, f32[4,5,128,128]{3,2,1,0:T(8,128)S(1)}, u32[]{:S(2)}, u32[]{:S(2)}) collective-permute-start(f32[4,5,128,128]{3,2,1,0:T(8,128)} %collective-permute-done.1.refs_0_), channel_id=1, source_target_pairs={{1,0},{2,3},{5,4},{6,7},{9,8},{10,11},{13,12},{14,15},{17,16},{18,... | collective-permute-start | bytes 3932168 | tf_op jit(solution)/shard_map/ppermute | solution.py:142

commit v3 on v0

v3 whole, which is shorter than its diff:
```python
import functools

import jax
import jax.numpy as jnp
from jax import lax
from jax.experimental import pallas as pl
from jax.experimental.pallas import tpu as pltpu
from jax.sharding import PartitionSpec as P

NC = 16
UNROLL = 8
LA, LB, LC = 30, 30, 30
VMEM = pl.BlockSpec(memory_space=pltpu.VMEM)
SMEM = pl.BlockSpec(memory_space=pltpu.SMEM)


def split(value):
    high = value.astype(jnp.bfloat16)
    low = (value - high.astype(jnp.float32)).astype(jnp.bfloat16)
    return high, low


def pack(words, keep, spare):
    slots = words.shape[-1]
    number = jnp.arange(slots + UNROLL)
    before = number[:slots, None] > number[None, :slots]
    rank = jnp.sum(keep[..., None, :] & before, axis=-1)
    count = jnp.sum(keep.astype(jnp.int32), axis=-1)
    chosen = keep[..., None, :] & (rank[..., None, :] == number[:, None])
    packed = jnp.sum(jnp.where(chosen, words[..., None, :] - spare, 0), axis=-1) + spare
    return packed, count


def contract_kernel(n_left, n_right, words_ref, counts_ref, *refs):
    left_refs, right_refs = refs[:n_left], refs[n_left : n_left + n_right]
    *before_ref, out_ref, left_split, total = refs[n_left + n_right :]
    tile = right_refs[0].shape[-1]

    some_live = counts_ref[0]
    for p in range(1, n_right):
        some_live = some_live + counts_ref[p]

    @pl.when(some_live > 0)
    def _():
        total[:NC] = before_ref[0][...] if before_ref else jnp.zeros_like(total[:NC])
        base = 0
        for ref in left_refs:
            for s in range(ref.shape[0]):

                def one(t, carry, ref=ref, s=s, base=base):
                    high, low = split(ref[s, t])
                    left_split[base + t, :, :tile] = high
                    left_split[base + t, :, tile:] = low
                    return carry

                lax.fori_loop(0, ref.shape[1], one, 0, unroll=True)
                base += ref.shape[1]

        for p, right_ref in enumerate(right_refs):

            def some(i, carry, p=p, right_ref=right_ref):
                products, targets = [], []
                for u in range(UNROLL):
                    word = words_ref[p, i * UNROLL + u]
                    high, low = split(right_ref[(word >> 8) & 255])
                    both = jnp.concatenate(
                        [
                            jnp.concatenate([high, low], axis=1),
                            jnp.concatenate([high, jnp.zeros_like(low)], axis=1),
                        ],
                        axis=0,
                    )
                    wide = jnp.dot(
                        left_split[word & 255], both, preferred_element_type=jnp.float32
                    )
                    products.append(wide[:, :tile] + wide[:, tile:])
                    targets.append(word >> 16)
                for product, target in zip(products, targets):
                    total[target] += product
                return carry

            lax.fori_loop(0, (counts_ref[p] + UNROLL - 1) // UNROLL, some, 0)
        out_ref[...] = total[:NC]

    @pl.when(some_live == 0)
    def _():
        out_ref[...] = before_ref[0][...] if before_ref else jnp.zeros_like(out_ref)


def contract(planned, lefts, rights, before=None, token=None):
    tile = rights[0].shape[-1]
    n_tiles = sum(left.shape[0] * left.shape[1] for left in lefts)
    if token is not None:
        planned, _ = lax.optimization_barrier((planned, token))
    operands = [*planned, *lefts, *rights] + ([] if before is None else [before])
    return pl.pallas_call(
        functools.partial(contract_kernel, len(lefts), len(rights)),
        out_shape=jax.ShapeDtypeStruct((NC, tile, tile), jnp.float32),
        in_specs=[SMEM] * 2 + [VMEM] * (len(operands) - 2),
        out_specs=VMEM,
        scratch_shapes=[
            pltpu.VMEM((n_tiles, tile, 2 * tile), jnp.bfloat16),
            pltpu.VMEM((NC + 1, tile, tile), jnp.float32),
        ],
        compiler_params=pltpu.CompilerParams(vmem_limit_bytes=24 * 2**20),
        cost_estimate=pl.CostEstimate(flops=1000, bytes_accessed=1000, transcendentals=0),
    )(*operands)


def later(seed, value, cost):
    seed, _ = lax.optimization_barrier((seed, value))

    def kernel(seed_ref, out_ref):
        out_ref[0] = seed_ref[0]

    return pl.pallas_call(
        kernel,
        out_shape=jax.ShapeDtypeStruct((1,), jnp.int32),
        in_specs=[SMEM],
        out_specs=SMEM,
        cost_estimate=pl.CostEstimate(flops=cost * 1150 * 10**6, bytes_accessed=0, transcendentals=0),
    )(seed)


def ring(count, by):
    return [(i, (i + by) % count) for i in range(count)]


def general(own, lists):
    steps, per, tile = own.shape[0], own.shape[1], own.shape[-1]
    panels, slivers = lax.axis_size("blk"), lax.axis_size("rep")
    whole = lax.all_gather(own, "rep", axis=0)
    total = None
    for step in range(steps):
        right = lax.ppermute(own, "blk", ring(panels, step)) if step else own
        left = whole[:, step]
        used = lists[step, 2] < NC
        word = lists[step, 0] | (lists[step, 1] << 8) | (lists[step, 2] << 16)
        total = contract(pack(word[None], used[None], NC << 16), [left], [right.reshape(-1, tile, tile)], total)
    return total


def helped(own, lists):
    steps, per, tile = own.shape[0], own.shape[1], own.shape[-1]
    panels, slivers = lax.axis_size("blk"), lax.axis_size("rep")
    blk, rep = lax.axis_index("blk"), lax.axis_index("rep")
    even, odd = range(0, panels, 2), range(1, panels, 2)
    every = range(panels)
    inward, outward, across = [(0, 1), (3, 2)], [(1, 0), (2, 3)], [(1, 2), (2, 1)]

    def send(value, *routes):
        pairs = [
            (b * slivers + source, (b + on) % panels * slivers + target)
            for these, ways, on in routes
            for b in these
            for source, target in ways
        ]
        return lax.ppermute(value, ("blk", "rep"), pairs)

    here = [(i, i) for i in range(slivers)]
    middle = [(1, 1), (2, 2)]
    flat = lambda x: x.reshape(-1, tile, tile)

    beyond = [(0, 2), (3, 1)]
    after = lambda value, *tokens: lax.optimization_barrier((value, *tokens))[0]

    side = send(own, (every, inward, 0), (even, outward, 0))
    near = send(own, (every, across, 0))
    two = send(own, (every, here, 2))
    their_lists = send(lists, (odd, inward, 0))
    side, near = lax.optimization_barrier((side, near))
    seed = jnp.zeros((1,), jnp.int32) + rep.astype(jnp.int32)

    far_even = send(side, (even, across, 0))
    near_end = send(near, (even, outward, 0))
    swapped = send(two, (even, here, 1), (odd, here, -1))
    theirs_two = send(side, (odd, middle, 2))
    theirs = [side, send(side, (even, middle, 1)), theirs_two, send(two, (even, inward, 1))]
    token = later(seed, (far_even, near_end), LA)
    alternate = send(after(own, theirs_two, token), (even, here, 1), (odd, here, 3))
    far_odd = send(after(side, theirs_two, token), (odd, across, 0))
    far_end = send(far_even, (even, outward, 0))
    late = later(seed, far_end, LC)

    is_odd = blk % 2 == 1
    is_middle = (rep == 1) | (rep == 2)
    block = steps * per

    def words(these, sliver_is, first):
        left = these[:, 0] % per + per * jnp.arange(steps)[:, None]
        for is_it, begin in zip(sliver_is, first):
            left = left + jnp.where(is_it, begin, 0)
        return left | (these[:, 1] << 8) | (these[:, 2] << 16)

    def slivers_of(these):
        sliver = these[:, 0] // per
        inner, outer = jnp.where(rep < 2, 2, 1), jnp.where(rep < 2, 3, 0)
        return [sliver == i for i in (rep, rep ^ 1, inner, outer)]

    def by_panel(these):
        return jnp.where(is_odd, these, jnp.stack([these[i] for i in (0, 3, 2, 1)]))

    spare = NC << 16
    live = lists[:, 2] < NC
    mine, beside, inner, outer = which = slivers_of(lists)
    full = is_middle | ~is_odd
    begin = jnp.where(is_middle, jnp.where(is_odd, 2 * block, block), 0)
    word = words(lists, which, [0, block, jnp.where(is_middle, 2 * block, 3 * block), begin])
    use_one = live & (mine | (full & (beside | inner)))
    use_two = live & outer & full
    mine, beside, inner, outer = which = slivers_of(their_lists)
    help_word = words(their_lists, which, [0, 0, block, 0])
    helping = (their_lists[:, 2] < NC) & is_middle & is_odd
    use_help = [helping & (mine | inner), helping & outer]

    panels_of = [flat(x) for x in theirs]
    part = contract(pack(help_word, use_help[0], spare), [own, near], panels_of)
    part = contract(pack(help_word, use_help[1], spare), [far_odd], panels_of, part)
    part = send(part, (odd, outward, 0))

    rights = [flat(x) for x in (own, alternate, two, swapped)]
    word = by_panel(word)
    total = contract(
        pack(word, by_panel(use_one), spare), [own, side, near, near_end], rights
    )
    total = contract(
        pack(word, by_panel(use_two), spare), [far_end, far_even, far_odd], rights, total, late
    )
    return total + part


def per_device(p_tiles, tasks):
    own, lists = p_tiles[0, 0], tasks[0, 0]
    small = lax.axis_size("rep") == 4 and own.shape[0] == 4 and lax.axis_size("blk") % 2 == 0
    return (helped if small else general)(own, lists)[None, None]


def solution(mesh):
    return jax.shard_map(
        per_device,
        mesh=mesh,
        in_specs=(P("blk", "rep", None, None, None, None), P("blk", "rep", None, None, None)),
        out_specs=P("blk", "rep", None, None, None),
        check_vma=False,
    )
```

time: 193 us -> 92.8 us (0.48)
  waiting for transfers between devices: 81 us -> 41.7 us
  matrix products: 31.1 us -> 0 us
  starting transfers between devices: 7.62 us -> 37.2 us
  local copies, waits for them, and re-layouts: 29 us -> 1.34 us
  other arithmetic: 29.2 us -> 5.37 us
  between operations: 13.5 us -> 0.32 us
  Pallas kernels: 0 us -> 6.36 us
    all_gather x1 -> x0, waiting for transfers between devices: 46.4 us -> none  [per_device(): whole_panel = lax.all_gather(own_tiles[None], 'rep', axis=0, tiled=True)]
    dot_general x4 -> x0, matrix products: 31.1 us -> none  [multiply_slots(): jnp.einsum('nij,njk->nik', left_pick, right_pick, precision=lax.Precision...]
    ppermute x3 -> x14, starting transfers between devices: 7.61 us -> 37.2 us  [send(): return lax.ppermute(value, ('blk', 'rep'), pairs)]
    scatter-add x4 -> x0, other arithmetic: 27.1 us -> none  [multiply_slots(): jax.ops.segment_sum(product, task_list[2, begin:finish], num_segments=tar...]
    gather x8 -> x0, local copies, waits for them, and re-layouts: 23.4 us -> none  [the longest x4 12.4 us: multiply_slots(): right_pick = right_tiles[task_list[1, begin:finish]]]
    ppermute x3 -> x14, waiting for transfers between devices: 33.9 us -> 41.7 us  [send(): return lax.ppermute(value, ('blk', 'rep'), pairs)]
    pallas_call x0 -> x4, Pallas kernels: none -> 6.36 us  [contract(): pl.pallas_call(functools.partial(contract_kernel, len(lefts), len(rights)...]
    slice x1, local copies, waits for them, and re-layouts: 4.47 us -> 0.01 us  [by_panel(): return jnp.where(is_odd, these, jnp.stack([these[i] for i in (0, 3, 2, 1)]))]
  transfers between devices with their start and end apart: 4 -> 14, of which waited for: 4 -> 4; matrix products, arithmetic and copies ran while one was open for 7% -> 5% of each run, Pallas kernels for 0% -> 7%
where the time goes in v3:
time: 92.8 us; the launch traced here: 92.4 us
  waiting for transfers between devices  41.7 us (45%)
  starting transfers between devices  37.2 us (40%)
  Pallas kernels  6.36 us (7%)
  other arithmetic  5.37 us (6%)
  local copies, waits for them, and re-layouts  1.34 us (1%)
    ppermute x14, waiting for transfers between devices, send(): return lax.ppermute(value, ('blk', 'rep'), pairs)  41.7 us
    ppermute x14, starting transfers between devices, send(): return lax.ppermute(value, ('blk', 'rep'), pairs)  37.2 us
    pallas_call x4, Pallas kernels, contract(): pl.pallas_call(functools.partial(contract_kernel, len(lefts), len(rights)...  6.36 us
  transfers between devices with their start and end apart: 14, of which 4 were waited for; matrix products, arithmetic and copies ran while one was open for 5% of the time, Pallas kernels for 7%

profile of v3, /device:TPU:1, one launch (start us, length us, event | category | flops | bytes accessed | tf_op | source)
XLA Modules:
  0.0 92.4 jit_solution(1015603999490249784)
XLA Ops:
  0.0 4.1 %collective-permute-start = (f32[4,5,128,128]{3,2,1,0:T(8,128)}, f32[4,5,128,128]{3,2,1,0:T(8,128)S(1)}, u32[]{:S(2)}, u32[]{:S(2)}) collective-permute-start(f32[4,5,128,128]{3,2,1,0:T(8,128)} %bitcast.123), channel_id=1, source_target_pairs={{0,1},{3,2},{4,5},{7,6},{8,9},{11,10},{12,13},{15,14},{16,17},{19,... | collective-permute-start | bytes 3932168 | tf_op jit(solution)/shard_map/ppermute | solution.py:158
  4.1 1.7 %collective-permute-start.1 = (f32[4,5,128,128]{3,2,1,0:T(8,128)}, f32[4,5,128,128]{3,2,1,0:T(8,128)}, u32[]{:S(2)}, u32[]{:S(2)}) collective-permute-start(f32[4,5,128,128]{3,2,1,0:T(8,128)} %bitcast.124), channel_id=1, source_target_pairs={{1,2},{2,1},{5,6},{6,5},{9,10},{10,9},{13,14},{14,13},{17,18},{18,... | collective-permute-start | bytes 3932168 | tf_op jit(solution)/shard_map/ppermute | solution.py:158
  5.8 1.2 %collective-permute-start.8 = (f32[4,5,128,128]{3,2,1,0:T(8,128)}, f32[4,5,128,128]{3,2,1,0:T(8,128)S(1)}, u32[]{:S(2)}, u32[]{:S(2)}) collective-permute-start(f32[4,5,128,128]{3,2,1,0:T(8,128)} %bitcast.125), channel_id=1, source_target_pairs={{0,8},{1,9},{2,10},{3,11},{4,12},{5,13},{6,14},{7,15},{8,16},{9,17... | collective-permute-start | bytes 3932168 | tf_op jit(solution)/shard_map/ppermute | solution.py:158
  7.1 2.7 %collective-permute-start.10 = (s32[4,3,48]{2,0,1:T(4,128)}, s32[4,3,48]{2,0,1:T(4,128)S(1)}, u32[]{:S(2)}, u32[]{:S(2)}) collective-permute-start(s32[4,3,48]{2,0,1:T(4,128)} %bitcast.145), channel_id=1, source_target_pairs={{4,5},{7,6},{12,13},{15,14},{20,21},{23,22},{28,29},{31,30}} | collective-permute-start | bytes 6920 | tf_op jit(solution)/shard_map/ppermute | solution.py:158
  9.8 21.9 %collective-permute-done.refs_1_ = f32[4,5,128,128]{3,2,1,0:T(8,128)S(1)} collective-permute-done((f32[4,5,128,128]{3,2,1,0:T(8,128)}, f32[4,5,128,128]{3,2,1,0:T(8,128)S(1)}, u32[]{:S(2)}, u32[]{:S(2)}) %collective-permute-start) | collective-permute-done | bytes 1310752 | tf_op jit(solution)/shard_map/ppermute | solution.py:158
  31.8 0.7 collective-permute-start.2
  32.5 0.7 collective-permute-start.5
  33.3 0.8 fusion.16
  34.9 0.7 collective-permute-start.4
  35.6 0.7 collective-permute-done.8
  36.4 0.7 collective-permute-start.11
  37.1 0.7 collective-permute-start.12
  37.9 0.7 collective-permute-start.6
  39.9 0.8 fusion.22
  40.9 19.8 %collective-permute-start.9 = (f32[4,5,128,128]{3,2,1,0:T(8,128)S(1)}, f32[4,5,128,128]{3,2,1,0:T(8,128)S(1)}, u32[]{:S(2)}, u32[]{:S(2)}) collective-permute-start(f32[4,5,128,128]{3,2,1,0:T(8,128)S(1)} %collective-permute-done.8), channel_id=1, source_target_pairs={{0,4},{1,5},{2,6},{3,7},{8,12},{9,13},{10,14},{11,15},{16,20},{17,... | collective-permute-start | bytes 3932168 | tf_op jit(solution)/shard_map/ppermute | solution.py:158
  60.7 1.2 %collective-permute-start.7 = (f32[4,5,128,128]{3,2,1,0:T(8,128)}, f32[4,5,128,128]{3,2,1,0:T(8,128)S(1)}, u32[]{:S(2)}, u32[]{:S(2)}) collective-permute-start(f32[4,5,128,128]{3,2,1,0:T(8,128)} %bitcast.126), channel_id=1, source_target_pairs={{0,4},{1,5},{2,6},{3,7},{8,12},{9,13},{10,14},{11,15},{16,20},{17,... | collective-permute-start | bytes 3932168 | tf_op jit(solution)/shard_map/ppermute | solution.py:158
  61.9 0.7 collective-permute-start.3
  62.7 1.3 %copy-done = f32[1,1,4,5,128,128]{5,4,3,2,1,0:T(8,128)S(1)} copy-done((f32[1,1,4,5,128,128]{5,4,3,2,1,0:T(8,128)S(1)}, f32[1,1,4,5,128,128]{5,4,3,2,1,0:T(8,128)}, u32[]{:S(2)}) %copy-start) | copy-done | bytes 1310744
  64.0 1.4 %shard_map.30.refs_5_ = f32[16,128,128]{2,1,0:T(8,128)S(1)} custom-call(s32[4,56]{1,0:T(4,128)S(1)} %broadcast_add_fusion.words_ref, s32[4]{0:T(128)S(1)} %get-tuple-element.19.counts_ref, f32[4,5,128,128]{3,2,1,0:T(8,128)S(1)} %bitcast.127, f32[4,5,128,128]{3,2,1,0:T(8,128)} %collective-permute-done.1.refs_2_.refs_1_, f32[20,128,128]{2,1,0:T(8,128)S(1)} %bitcast.131, ...), custom_call_target="tpu_custom_call" | custom-call | flops 1000 | bytes 1000 | tf_op jit(solution)/shard_map/pallas_call | solution.py:96
  66.1 1.3 %collective-permute-start.13 = (f32[16,128,128]{2,1,0:T(8,128)S(1)}, f32[16,128,128]{2,1,0:T(8,128)S(1)}, u32[]{:S(2)}, u32[]{:S(2)}) collective-permute-start(f32[16,128,128]{2,1,0:T(8,128)S(1)} %shard_map.31), channel_id=1, source_target_pairs={{5,4},{6,7},{13,12},{14,15},{21,20},{22,23},{29,28},{30,31}} | collective-permute-start | bytes 3145736 | tf_op jit(solution)/shard_map/ppermute | solution.py:158
  67.9 8.9 %collective-permute-done.7 = f32[4,5,128,128]{3,2,1,0:T(8,128)S(1)} collective-permute-done((f32[4,5,128,128]{3,2,1,0:T(8,128)}, f32[4,5,128,128]{3,2,1,0:T(8,128)S(1)}, u32[]{:S(2)}, u32[]{:S(2)}) %collective-permute-start.7) | collective-permute-done | bytes 1310752 | tf_op jit(solution)/shard_map/ppermute | solution.py:158
  76.8 3.7 %shard_map.28.refs_7_ = f32[16,128,128]{2,1,0:T(8,128)S(1)} custom-call(s32[4,56]{1,0:T(4,128)S(1)} %broadcast_add_fusion.2.words_ref, s32[4]{0:T(128)S(1)} %convert_reduce_fusion.6.counts_ref, f32[4,5,128,128]{3,2,1,0:T(8,128)S(1)} %bitcast.128, f32[4,5,128,128]{3,2,1,0:T(8,128)S(1)} %collective-permute-done.refs_1_, ...), custom_call_target="tpu_custom_call" | custom-call | flops 1000 | bytes 1000 | tf_op jit(solution)/shard_map/pallas_call | solution.py:96
  81.1 10.2 %collective-permute-done.13 = f32[16,128,128]{2,1,0:T(8,128)S(1)} collective-permute-done((f32[16,128,128]{2,1,0:T(8,128)S(1)}, f32[16,128,128]{2,1,0:T(8,128)S(1)}, u32[]{:S(2)}, u32[]{:S(2)}) %collective-permute-start.13) | collective-permute-done | bytes 1048608 | tf_op jit(solution)/shard_map/ppermute | solution.py:158
  91.3 1.1 %add_bitcast_fusion = f32[1,1,16,128,128]{4,3,2,1,0:T(8,128)} fusion(f32[16,128,128]{2,1,0:T(8,128)S(1)} %shard_map.29, f32[16,128,128]{2,1,0:T(8,128)S(1)} %collective-permute-done.13), kind=kLoop, calls=%fused_computation | loop fusion | flops 262144 | bytes 3145728 | tf_op jit(solution)/shard_map/broadcast_in_dim | solution.py:235
  (34 shorter events, 4.1 us)
Async XLA Ops:
  0.0 31.8 %collective-permute-start = (f32[4,5,128,128]{3,2,1,0:T(8,128)}, f32[4,5,128,128]{3,2,1,0:T(8,128)S(1)}, u32[]{:S(2)}, u32[]{:S(2)}) collective-permute-start(f32[4,5,128,128]{3,2,1,0:T(8,128)} %bitcast.123), channel_id=1, source_target_pairs={{0,1},{3,2},{4,5},{7,6},{8,9},{11,10},{12,13},{15,14},{16,17},{19,... | collective-permute-start | bytes 3932168 | tf_op jit(solution)/shard_map/ppermute | solution.py:158
  4.1 27.7 %collective-permute-start.1 = (f32[4,5,128,128]{3,2,1,0:T(8,128)}, f32[4,5,128,128]{3,2,1,0:T(8,128)}, u32[]{:S(2)}, u32[]{:S(2)}) collective-permute-start(f32[4,5,128,128]{3,2,1,0:T(8,128)} %bitcast.124), channel_id=1, source_target_pairs={{1,2},{2,1},{5,6},{6,5},{9,10},{10,9},{13,14},{14,13},{17,18},{18,... | collective-permute-start | bytes 3932168 | tf_op jit(solution)/shard_map/ppermute | solution.py:158
  5.8 30.5 %collective-permute-start.8 = (f32[4,5,128,128]{3,2,1,0:T(8,128)}, f32[4,5,128,128]{3,2,1,0:T(8,128)S(1)}, u32[]{:S(2)}, u32[]{:S(2)}) collective-permute-start(f32[4,5,128,128]{3,2,1,0:T(8,128)} %bitcast.125), channel_id=1, source_target_pairs={{0,8},{1,9},{2,10},{3,11},{4,12},{5,13},{6,14},{7,15},{8,16},{9,17... | collective-permute-start | bytes 3932168 | tf_op jit(solution)/shard_map/ppermute | solution.py:158
  7.1 32.3 %collective-permute-start.10 = (s32[4,3,48]{2,0,1:T(4,128)}, s32[4,3,48]{2,0,1:T(4,128)S(1)}, u32[]{:S(2)}, u32[]{:S(2)}) collective-permute-start(s32[4,3,48]{2,0,1:T(4,128)} %bitcast.145), channel_id=1, source_target_pairs={{4,5},{7,6},{12,13},{15,14},{20,21},{23,22},{28,29},{31,30}} | collective-permute-start | bytes 6920 | tf_op jit(solution)/shard_map/ppermute | solution.py:158
  31.8 5.3 %collective-permute-start.2 = (f32[4,5,128,128]{3,2,1,0:T(8,128)S(1)}, f32[4,5,128,128]{3,2,1,0:T(8,128)S(1)}, u32[]{:S(2)}, u32[]{:S(2)}) collective-permute-start(f32[4,5,128,128]{3,2,1,0:T(8,128)S(1)} %collective-permute-done.refs_1_), channel_id=1, source_target_pairs={{1,2},{2,1},{9,10},{10,9},{17,18},{18,17},{25,26},{26,25}} | collective-permute-start | bytes 3932168 | tf_op jit(solution)/shard_map/ppermute | solution.py:158
  32.5 5.4 %collective-permute-start.5 = (f32[4,5,128,128]{3,2,1,0:T(8,128)}, f32[4,5,128,128]{3,2,1,0:T(8,128)S(1)}, u32[]{:S(2)}, u32[]{:S(2)}) collective-permute-start(f32[4,5,128,128]{3,2,1,0:T(8,128)} %collective-permute-done.1.refs_2_.refs_1_), channel_id=1, source_target_pairs={{1,0},{2,3},{9,8},{10,11},{17,16},{18,19},{25,24},{26,27}} | collective-permute-start | bytes 3932168 | tf_op jit(solution)/shard_map/ppermute | solution.py:158
  34.9 3.0 %collective-permute-start.4 = (f32[4,5,128,128]{3,2,1,0:T(8,128)S(1)}, f32[4,5,128,128]{3,2,1,0:T(8,128)S(1)}, u32[]{:S(2)}, u32[]{:S(2)}) collective-permute-start(f32[4,5,128,128]{3,2,1,0:T(8,128)S(1)} %collective-permute-done.refs_1_), channel_id=1, source_target_pairs={{5,13},{6,14},{13,21},{14,22},{21,29},{22,30},{29,5},{30,6}} | collective-permute-start | bytes 3932168 | tf_op jit(solution)/shard_map/ppermute | solution.py:158
  36.4 25.6 %collective-permute-start.11 = (f32[4,5,128,128]{3,2,1,0:T(8,128)S(1)}, f32[4,5,128,128]{3,2,1,0:T(8,128)S(1)}, u32[]{:S(2)}, u32[]{:S(2)}) collective-permute-start(f32[4,5,128,128]{3,2,1,0:T(8,128)S(1)} %collective-permute-done.refs_1_), channel_id=1, source_target_pairs={{1,5},{2,6},{9,13},{10,14},{17,21},{18,22},{25,29},{26,30}} | collective-permute-start | bytes 3932168 | tf_op jit(solution)/shard_map/ppermute | solution.py:158
  37.1 25.6 %collective-permute-start.12 = (f32[4,5,128,128]{3,2,1,0:T(8,128)S(1)}, f32[4,5,128,128]{3,2,1,0:T(8,128)S(1)}, u32[]{:S(2)}, u32[]{:S(2)}) collective-permute-start(f32[4,5,128,128]{3,2,1,0:T(8,128)S(1)} %collective-permute-done.8), channel_id=1, source_target_pairs={{0,5},{3,6},{8,13},{11,14},{16,21},{19,22},{24,29},{27,30}} | collective-permute-start | bytes 3932168 | tf_op jit(solution)/shard_map/ppermute | solution.py:158
  37.9 27.5 %collective-permute-start.6 = (f32[4,5,128,128]{3,2,1,0:T(8,128)S(1)}, f32[4,5,128,128]{3,2,1,0:T(8,128)S(1)}, u32[]{:S(2)}, u32[]{:S(2)}) collective-permute-start(f32[4,5,128,128]{3,2,1,0:T(8,128)S(1)} %collective-permute-done.refs_1_), channel_id=1, source_target_pairs={{5,6},{6,5},{13,14},{14,13},{21,22},{22,21},{29,30},{30,29}} | collective-permute-start | bytes 3932168 | tf_op jit(solution)/shard_map/ppermute | solution.py:158
  40.9 27.0 %collective-permute-start.9 = (f32[4,5,128,128]{3,2,1,0:T(8,128)S(1)}, f32[4,5,128,128]{3,2,1,0:T(8,128)S(1)}, u32[]{:S(2)}, u32[]{:S(2)}) collective-permute-start(f32[4,5,128,128]{3,2,1,0:T(8,128)S(1)} %collective-permute-done.8), channel_id=1, source_target_pairs={{0,4},{1,5},{2,6},{3,7},{8,12},{9,13},{10,14},{11,15},{16,20},{17,... | collective-permute-start | bytes 3932168 | tf_op jit(solution)/shard_map/ppermute | solution.py:158
  60.7 16.1 %collective-permute-start.7 = (f32[4,5,128,128]{3,2,1,0:T(8,128)}, f32[4,5,128,128]{3,2,1,0:T(8,128)S(1)}, u32[]{:S(2)}, u32[]{:S(2)}) collective-permute-start(f32[4,5,128,128]{3,2,1,0:T(8,128)} %bitcast.126), channel_id=1, source_target_pairs={{0,4},{1,5},{2,6},{3,7},{8,12},{9,13},{10,14},{11,15},{16,20},{17,... | collective-permute-start | bytes 3932168 | tf_op jit(solution)/shard_map/ppermute | solution.py:158
  61.9 18.5 %collective-permute-start.3 = (f32[4,5,128,128]{3,2,1,0:T(8,128)S(1)}, f32[4,5,128,128]{3,2,1,0:T(8,128)S(1)}, u32[]{:S(2)}, u32[]{:S(2)}) collective-permute-start(f32[4,5,128,128]{3,2,1,0:T(8,128)S(1)} %collective-permute-done.2.refs_1_), channel_id=1, source_target_pairs={{1,0},{2,3},{9,8},{10,11},{17,16},{18,19},{25,24},{26,27}} | collective-permute-start | bytes 3932168 | tf_op jit(solution)/shard_map/ppermute | solution.py:158
  62.7 1.3 %copy-start = (f32[1,1,4,5,128,128]{5,4,3,2,1,0:T(8,128)S(1)}, f32[1,1,4,5,128,128]{5,4,3,2,1,0:T(8,128)}, u32[]{:S(2)}) copy-start(f32[1,1,4,5,128,128]{5,4,3,2,1,0:T(8,128)} %param.2) | copy-start | bytes 3932164
  65.4 11.4 %copy-start.1 = (f32[1,1,4,5,128,128]{5,4,3,2,1,0:T(8,128)S(1)}, f32[1,1,4,5,128,128]{5,4,3,2,1,0:T(8,128)}, u32[]{:S(2)}) copy-start(f32[1,1,4,5,128,128]{5,4,3,2,1,0:T(8,128)} %param.2) | copy-start | bytes 3932164
  66.1 25.2 %collective-permute-start.13 = (f32[16,128,128]{2,1,0:T(8,128)S(1)}, f32[16,128,128]{2,1,0:T(8,128)S(1)}, u32[]{:S(2)}, u32[]{:S(2)}) collective-permute-start(f32[16,128,128]{2,1,0:T(8,128)S(1)} %shard_map.31), channel_id=1, source_target_pairs={{5,4},{6,7},{13,12},{14,15},{21,20},{22,23},{29,28},{30,31}} | collective-permute-start | bytes 3145736 | tf_op jit(solution)/shard_map/ppermute | solution.py:158

commit v4 on v0

v4 whole, which is shorter than its diff:
```python
import functools

import jax
import jax.numpy as jnp
from jax import lax
from jax.experimental import pallas as pl
from jax.experimental.pallas import tpu as pltpu
from jax.sharding import PartitionSpec as P

NC = 16
UNROLL = 16
VMEM = pl.BlockSpec(memory_space=pltpu.VMEM)
SMEM = pl.BlockSpec(memory_space=pltpu.SMEM)
ANY = pl.BlockSpec(memory_space=pl.ANY)


def split(value):
    high = value.astype(jnp.bfloat16)
    low = (value - high.astype(jnp.float32)).astype(jnp.bfloat16)
    return high, low


def pack(words, keep):
    words, keep = words.reshape(-1), keep.reshape(-1)
    slots = words.shape[0]
    spare = NC << 16
    number = jnp.arange(slots + UNROLL)
    rank = jnp.sum(keep[None, :] & (number[:slots, None] > number[None, :slots]), axis=1)
    count = jnp.sum(keep.astype(jnp.int32), keepdims=True)
    chosen = keep[None, :] & (rank[None, :] == number[:, None])
    packed = jnp.sum(jnp.where(chosen, words[None, :] - spare, 0), axis=1) + spare
    return jnp.concatenate([packed, count])


def contract_kernel(placed, n_left, n_right, words_ref, *refs):
    left_refs, right_refs = refs[:n_left], refs[n_left : n_left + n_right]
    *before_ref, out_ref, left_raw, right_raw, total, sems = refs[n_left + n_right :]
    block, tile = right_refs[0].shape[0], right_refs[0].shape[-1]
    count, kind = (words_ref[words_ref.shape[0] - i] for i in (2, 1))

    @pl.when(count > 0)
    def _():
        blocks = left_raw.shape[0] // block

        def lefts(act):
            for b, places in enumerate(placed):
                for at in sorted(set(places) - {None}):
                    here = functools.reduce(
                        jnp.logical_or, [kind == c for c, place in enumerate(places) if place == at]
                    )
                    copy = pltpu.make_async_copy(
                        left_refs[b], left_raw.at[pl.ds(at * block, block)], sems.at[at]
                    )
                    pl.when(here)(functools.partial(act, copy))

        rights = [
            pltpu.make_async_copy(ref, right_raw.at[pl.ds(k * block, block)], sems.at[blocks + k])
            for k, ref in enumerate(right_refs)
        ]
        lefts(lambda copy: copy.start())
        for copy in rights:
            copy.start()
        total[:NC] = before_ref[0][...] if before_ref else jnp.zeros_like(total[:NC])
        lefts(lambda copy: copy.wait())

        for copy in rights:
            copy.wait()

        def some(i, carry):
            products, targets = [], []
            for u in range(UNROLL):
                word = words_ref[i * UNROLL + u]
                high, low = split(right_raw[(word >> 8) & 255])
                both = jnp.concatenate(
                    [
                        jnp.concatenate([high, low], axis=1),
                        jnp.concatenate([high, jnp.zeros_like(low)], axis=1),
                    ],
                    axis=0,
                )
                pair = jnp.concatenate(split(left_raw[word & 255]), axis=1)
                wide = jnp.dot(pair, both, preferred_element_type=jnp.float32)
                products.append(wide[:, :tile] + wide[:, tile:])
                targets.append(word >> 16)
            for product, target in zip(products, targets):
                total[target] += product
            return carry

        lax.fori_loop(0, (count + UNROLL - 1) // UNROLL, some, 0)
        out_ref[...] = total[:NC]

    @pl.when(count == 0)
    def _():
        out_ref[...] = before_ref[0][...] if before_ref else jnp.zeros_like(out_ref)


def contract(planned, lefts, rights, before=None, placed=None, kind=0):
    block, tile = rights[0].shape[0], rights[0].shape[-1]
    placed = placed or [(b,) for b in range(len(lefts))]
    blocks = 1 + max(place for places in placed for place in places if place is not None)
    planned = jnp.append(planned, jnp.int32(kind))
    lefts, rights = [
        [pltpu.with_memory_space_constraint(x, pltpu.HBM) for x in xs] for xs in (lefts, rights)
    ]
    operands = [planned, *lefts, *rights] + ([] if before is None else [before])
    size = (blocks * block + len(rights) * block + 3 * NC + 1) * tile * tile
    return pl.pallas_call(
        functools.partial(contract_kernel, placed, len(lefts), len(rights)),
        out_shape=pltpu.VMEM((NC, tile, tile), jnp.float32),
        in_specs=[SMEM] + [ANY] * (len(lefts) + len(rights)) + [VMEM] * (before is not None),
        out_specs=VMEM,
        scratch_shapes=[
            pltpu.VMEM((blocks * block, tile, tile), jnp.float32),
            pltpu.VMEM((len(rights) * block, tile, tile), jnp.float32),
            pltpu.VMEM((NC + 1, tile, tile), jnp.float32),
            pltpu.SemaphoreType.DMA((blocks + len(rights),)),
        ],
        compiler_params=pltpu.CompilerParams(vmem_limit_bytes=4 * size + 4 * 2**20),
        cost_estimate=pl.CostEstimate(flops=1000, bytes_accessed=1000, transcendentals=0),
    )(*operands)


def probe(value):
    corner = value[(0,) * (value.ndim - 2) + (slice(0, 1), slice(0, 1))].reshape(1)
    return jnp.minimum(jnp.abs(corner), 0).astype(jnp.int32)


def ring(count, by):
    return [(i, (i + by) % count) for i in range(count)]


def general(own, lists):
    steps, tile = own.shape[0], own.shape[-1]
    panels = lax.axis_size("blk")
    whole = lax.all_gather(own, "rep", axis=0)
    total = None
    for step in range(steps):
        right = lax.ppermute(own, "blk", ring(panels, step)) if step else own
        word = lists[step, 0] | (lists[step, 1] << 8) | (lists[step, 2] << 16)
        total = contract(
            pack(word, lists[step, 2] < NC),
            [whole[:, step].reshape(-1, tile, tile)],
            [right.reshape(-1, tile, tile)],
            total,
        )
    return total


def on_a_line(own, lists):
    steps, per, tile = own.shape[0], own.shape[1], own.shape[-1]
    panels, slivers = lax.axis_size("blk"), lax.axis_size("rep")
    blk, rep = lax.axis_index("blk"), lax.axis_index("rep")
    even, odd, every = range(0, panels, 2), range(1, panels, 2), range(panels)
    inward, outward, across, beyond = [(0, 1), (3, 2)], [(1, 0), (2, 3)], [(1, 2), (2, 1)], [(0, 2), (3, 1)]
    here = [(i, i) for i in range(slivers)]
    middle = [(1, 1), (2, 2)]
    block = steps * per

    def send(value, *routes):
        pairs = [
            (b * slivers + source, (b + on) % panels * slivers + target)
            for these, ways, on in routes
            for b in these
            for source, target in ways
        ]
        return lax.ppermute(value, ("blk", "rep"), pairs)

    is_odd, is_middle = blk % 2 == 1, (rep == 1) | (rep == 2)
    full = is_middle | ~is_odd
    kind = 2 * is_odd.astype(jnp.int32) + 1 - is_middle.astype(jnp.int32)

    sliver = lists[:, 0] // per
    steps_of = jnp.arange(steps)[:, None]
    place = lists[:, 0] % per + per * steps_of + (lists[:, 1] << 8) + (lists[:, 2] << 16)
    live = lists[:, 2] < NC
    mine, beside, inner, outer = [
        sliver == i for i in (rep, rep ^ 1, jnp.where(rep < 2, 2, 1), jnp.where(rep < 2, 3, 0))
    ]

    def words(panel, *firsts):
        word = place + ((panel * block) << 8)
        for is_it, first in zip((mine, beside, inner, outer), firsts):
            word = word + jnp.where(is_it, first, 0)
        return word

    panel = jnp.where(is_odd, steps_of, jnp.array([0, 3, 2, 1])[:, None])
    own_words = pack(words(panel, 0, block, 2 * block, 3 * block), live & (mine | full))
    their_words = pack(words(steps_of, 0, 0, block, 2 * block), live & is_odd & ~is_middle & ~mine)

    p1 = send(own, (even, beyond + outward, 0))
    p2 = send(own, (even, across, 0), (odd, inward, 0))
    p3 = send(own, (even, inward, 0), (odd, across, 0))
    two = send(own, (every, here, 2))
    their_words = send(their_words, (odd, inward, 0))
    alternate = send(own, (even, here, 1), (odd, here, 3))
    q1 = send(p2, (even, outward, 0), (odd, across, 0))
    q2 = send(jnp.where(is_middle, p1, two), (even, outward, 0), (even, inward, 1))
    h2 = send(p2, (odd, middle, 2))
    h1 = send(p3, (even, middle, 1))
    swapped = send(two, (even, here, 1), (odd, here, -1))

    own, p1, p2, p3, q1, q2, h1, h2, two, alternate, swapped = [
        x.reshape(-1, tile, tile) for x in (own, p1, p2, p3, q1, q2, h1, h2, two, alternate, swapped)
    ]
    part = contract(their_words + probe(alternate), [own, p3, q1], [p2, h1, h2, q2])
    part = send(part, (odd, outward, 0))

    lefts = [own, p1, p2, p3, q1, q2]
    placed = [
        (0, 0, 0, 0),
        (3, 1, None, None),
        (2, None, 1, None),
        (1, None, 2, None),
        (None, 2, 3, None),
        (None, 3, None, None),
    ]
    total = contract(own_words, lefts, [own, alternate, two, swapped], None, placed, kind)
    return total + part


def per_device(p_tiles, tasks):
    own, lists = p_tiles[0, 0], tasks[0, 0]
    small = lax.axis_size("rep") == 4 and own.shape[0] == 4 and lax.axis_size("blk") % 2 == 0
    return (on_a_line if small else general)(own, lists)[None, None]


def solution(mesh):
    return jax.shard_map(
        per_device,
        mesh=mesh,
        in_specs=(P("blk", "rep", None, None, None, None), P("blk", "rep", None, None, None)),
        out_specs=P("blk", "rep", None, None, None),
        check_vma=False,
    )
```

time: 193 us -> 90.7 us (0.47)
  waiting for transfers between devices: 81 us -> 36 us
  matrix products: 31.1 us -> 0 us
  starting transfers between devices: 7.62 us -> 37.3 us
  local copies, waits for them, and re-layouts: 29 us -> 4.43 us
  other arithmetic: 29.2 us -> 6.7 us
  between operations: 13.5 us -> 0.91 us
  Pallas kernels: 0 us -> 5.23 us
    all_gather x1 -> x0, waiting for transfers between devices: 46.4 us -> none  [per_device(): whole_panel = lax.all_gather(own_tiles[None], 'rep', axis=0, tiled=True)]
    dot_general x4 -> x0, matrix products: 31.1 us -> none  [multiply_slots(): jnp.einsum('nij,njk->nik', left_pick, right_pick, precision=lax.Precision...]
    ppermute x3 -> x12, starting transfers between devices: 7.61 us -> 37.3 us  [send(): return lax.ppermute(value, ('blk', 'rep'), pairs)]
    scatter-add x4 -> x0, other arithmetic: 27.1 us -> none  [multiply_slots(): jax.ops.segment_sum(product, task_list[2, begin:finish], num_segments=tar...]
    gather x8 -> x0, local copies, waits for them, and re-layouts: 23.4 us -> none  [the longest x4 12.4 us: multiply_slots(): right_pick = right_tiles[task_list[1, begin:finish]]]
    pallas_call x0 -> x2, Pallas kernels: none -> 5.23 us  [contract(): pl.pallas_call(functools.partial(contract_kernel, placed, len(lefts), len...]
    slice x1, local copies, waits for them, and re-layouts: 4.47 us -> 1.2 us  [probe(): value[(0,) * (value.ndim - 2) + (slice(0, 1), slice(0, 1))].reshape(1)]
    unnamed x4 -> x10, local copies, waits for them, and re-layouts: 0.01 us -> 2.26 us
  transfers between devices with their start and end apart: 4 -> 12, of which waited for: 4 -> 4; matrix products, arithmetic and copies ran while one was open for 7% -> 9% of each run, Pallas kernels for 0% -> 6%
where the time goes in v4:
time: 90.7 us; the launch traced here: 90.5 us
  starting transfers between devices  37.3 us (41%)
  waiting for transfers between devices  36 us (40%)
  other arithmetic  6.7 us (7%)
  Pallas kernels  5.23 us (6%)
  local copies, waits for them, and re-layouts  4.43 us (5%)
  between operations  0.91 us (1%)
    ppermute x12, starting transfers between devices, send(): return lax.ppermute(value, ('blk', 'rep'), pairs)  37.3 us
    ppermute x12, waiting for transfers between devices, send(): return lax.ppermute(value, ('blk', 'rep'), pairs)  36 us
    pallas_call x2, Pallas kernels, contract(): pl.pallas_call(functools.partial(contract_kernel, placed, len(lefts), len...  5.23 us
    unnamed x10, local copies, waits for them, and re-layouts  2.26 us
  transfers between devices with their start and end apart: 12, of which 4 were waited for; matrix products, arithmetic and copies ran while one was open for 9% of the time, Pallas kernels for 6%

profile of v4, /device:TPU:1, one launch (start us, length us, event | category | flops | bytes accessed | tf_op | source)
XLA Modules:
  0.0 90.5 jit_solution(10522025576774548372)
XLA Ops:
  0.0 0.7 collective-permute-start
  0.7 2.1 %collective-permute-start.4 = (f32[4,5,128,128]{3,2,1,0:T(8,128)}, f32[4,5,128,128]{3,2,1,0:T(8,128)}, u32[]{:S(2)}, u32[]{:S(2)}) collective-permute-start(f32[4,5,128,128]{3,2,1,0:T(8,128)} %bitcast.33), channel_id=1, source_target_pairs={{0,8},{1,9},{2,10},{3,11},{4,12},{5,13},{6,14},{7,15},{8,16},{9,17... | collective-permute-start | bytes 3932168 | tf_op jit(solution)/shard_map/ppermute | solution.py:166
  2.8 4.3 %collective-permute-start.1 = (f32[4,5,128,128]{3,2,1,0:T(8,128)}, f32[4,5,128,128]{3,2,1,0:T(8,128)}, u32[]{:S(2)}, u32[]{:S(2)}) collective-permute-start(f32[4,5,128,128]{3,2,1,0:T(8,128)} %bitcast.34), channel_id=1, source_target_pairs={{1,2},{2,1},{9,10},{10,9},{17,18},{18,17},{25,26},{26,25},{4,5},{7... | collective-permute-start | bytes 3932168 | tf_op jit(solution)/shard_map/ppermute | solution.py:166
  7.1 1.7 %collective-permute-start.2 = (f32[4,5,128,128]{3,2,1,0:T(8,128)}, f32[4,5,128,128]{3,2,1,0:T(8,128)}, u32[]{:S(2)}, u32[]{:S(2)}) collective-permute-start(f32[4,5,128,128]{3,2,1,0:T(8,128)} %bitcast.35), channel_id=1, source_target_pairs={{0,1},{3,2},{8,9},{11,10},{16,17},{19,18},{24,25},{27,26},{5,6},{6... | collective-permute-start | bytes 3932168 | tf_op jit(solution)/shard_map/ppermute | solution.py:166
  8.8 6.9 %collective-permute-start.6 = (f32[4,5,128,128]{3,2,1,0:T(8,128)}, f32[4,5,128,128]{3,2,1,0:T(8,128)}, u32[]{:S(2)}, u32[]{:S(2)}) collective-permute-start(f32[4,5,128,128]{3,2,1,0:T(8,128)} %bitcast.36), channel_id=1, source_target_pairs={{0,4},{1,5},{2,6},{3,7},{8,12},{9,13},{10,14},{11,15},{16,20},{17,... | collective-permute-start | bytes 3932168 | tf_op jit(solution)/shard_map/ppermute | solution.py:166
  15.9 0.7 fusion.2
  16.6 1.4 %slice_divide_fusion = (s32[4,1,48]{2,0,1:T(4,128)S(1)}, s32[4,1,48]{2,0,1:T(4,128)S(1)}, s32[4,1,48]{2,0,1:T(4,128)S(1)}, s32[4,1,48]{2,0,1:T(4,128)S(1)}, s32[...) fusion(s32[4,3,48]{2,0,1:T(4,128)} %bitcast.48, pred[4,1,48]{2,0,1:T(4,128)(4,1)S(1)} %get-tuple-element.13, ...), kind=kLoop, calls=%fused_computation.25 | loop fusion | flops 2878 | bytes 5771 | tf_op jit(solution)/shard_map/jit(floor_divide)/div | solution.py:172
  18.9 9.5 %collective-permute-done.4 = f32[4,5,128,128]{3,2,1,0:T(8,128)} collective-permute-done((f32[4,5,128,128]{3,2,1,0:T(8,128)}, f32[4,5,128,128]{3,2,1,0:T(8,128)}, u32[]{:S(2)}, u32[]{:S(2)}) %collective-permute-start.4) | collective-permute-done | bytes 1310752 | tf_op jit(solution)/shard_map/ppermute | solution.py:166
  28.3 1.5 %broadcast_select_fusion = f32[4,5,128,128]{3,2,1,0:T(8,128)S(1)} fusion(f32[4,5,128,128]{3,2,1,0:T(8,128)S(1)} %collective-permute-done, f32[4,5,128,128]{3,2,1,0:T(8,128)} %collective-permute-done.4, pred[]{:T(512)S(6)} %or.22), kind=kLoop, calls=%fused_computation.1 | loop fusion | flops 327680 | bytes 3932161 | tf_op jit(solution)/shard_map/jit(_where)/select_n | solution.py:197
  29.8 0.7 collective-permute-start.5
  30.6 4.2 %collective-permute-done.1 = f32[4,5,128,128]{3,2,1,0:T(8,128)} collective-permute-done((f32[4,5,128,128]{3,2,1,0:T(8,128)}, f32[4,5,128,128]{3,2,1,0:T(8,128)}, u32[]{:S(2)}, u32[]{:S(2)}) %collective-permute-start.1) | collective-permute-done | bytes 1310752 | tf_op jit(solution)/shard_map/ppermute | solution.py:166
  34.8 0.7 collective-permute-start.3
  35.5 0.7 collective-permute-start.10
  36.3 0.7 collective-permute-start.9
  37.6 0.7 pad_add_fusion.1
  38.3 8.4 %collective-permute-done.6 = f32[4,5,128,128]{3,2,1,0:T(8,128)} collective-permute-done((f32[4,5,128,128]{3,2,1,0:T(8,128)}, f32[4,5,128,128]{3,2,1,0:T(8,128)}, u32[]{:S(2)}, u32[]{:S(2)}) %collective-permute-start.6) | collective-permute-done | bytes 1310752 | tf_op jit(solution)/shard_map/ppermute | solution.py:166
  46.7 17.2 %collective-permute-start.8 = (s32[209]{0:T(256)S(1)}, s32[209]{0:T(256)S(1)}, u32[]{:S(2)}, u32[]{:S(2)}) collective-permute-start(s32[209]{0:T(256)S(1)} %pad_add_fusion.1), channel_id=1, source_target_pairs={{4,5},{7,6},{12,13},{15,14},{20,21},{23,22},{28,29},{31,30}} | collective-permute-start | bytes 2516 | tf_op jit(solution)/shard_map/ppermute | solution.py:166
  64.0 1.2 %slice.30 = f32[1,1,1]{2,1,0:T(1,128)} slice(f32[20,128,128]{2,1,0:T(8,128)} %bitcast.10.refs_7_), slice={[0:1], [0:1], [0:1]} | slice | bytes 8 | tf_op jit(solution)/shard_map/slice | solution.py:124
  66.1 1.0 %copy-done.2 = f32[4,5,128,128]{3,2,1,0:T(8,128)} copy-done((f32[4,5,128,128]{3,2,1,0:T(8,128)}, f32[4,5,128,128]{3,2,1,0:T(8,128)S(1)}, u32[]{:S(2)}) %copy-start.2) | copy-done | bytes 1310744
  69.0 1.3 %collective-permute-start.11 = (f32[16,128,128]{2,1,0:T(8,128)S(1)}, f32[16,128,128]{2,1,0:T(8,128)S(1)}, u32[]{:S(2)}, u32[]{:S(2)}) collective-permute-start(f32[16,128,128]{2,1,0:T(8,128)S(1)} %shard_map.38), channel_id=1, source_target_pairs={{5,4},{6,7},{13,12},{14,15},{21,20},{22,23},{29,28},{30,31}} | collective-permute-start | bytes 3145736 | tf_op jit(solution)/shard_map/ppermute | solution.py:166
  70.3 0.7 pad_add_fusion.words_ref
  71.0 4.5 %shard_map.37 = f32[16,128,128]{2,1,0:T(8,128)S(1)} custom-call(s32[210]{0:T(256)S(1)} %pad_add_fusion.words_ref, f32[20,128,128]{2,1,0:T(8,128)} %bitcast.38, f32[20,128,128]{2,1,0:T(8,128)} %bitcast.40, f32[20,128,128]{2,1,0:T(8,128)} %bitcast.6.refs_2_.refs_3_, f32[20,128,128]{2,1,0:T(8,128)} %bitcast.7.refs_3_.refs_1_, f32[20,128,128]{2,1,0:T(8,128)} %bitcast.44, ...), custom_call_target="tpu_custom_call" | custom-call | flops 1000 | bytes 1000 | tf_op jit(solution)/shard_map/pallas_call | solution.py:107
  75.6 13.9 %collective-permute-done.11 = f32[16,128,128]{2,1,0:T(8,128)S(1)} collective-permute-done((f32[16,128,128]{2,1,0:T(8,128)S(1)}, f32[16,128,128]{2,1,0:T(8,128)S(1)}, u32[]{:S(2)}, u32[]{:S(2)}) %collective-permute-start.11) | collective-permute-done | bytes 1048608 | tf_op jit(solution)/shard_map/ppermute | solution.py:166
  89.4 1.1 %add_bitcast_fusion = f32[1,1,16,128,128]{4,3,2,1,0:T(8,128)} fusion(f32[16,128,128]{2,1,0:T(8,128)S(1)} %shard_map.37, f32[16,128,128]{2,1,0:T(8,128)S(1)} %collective-permute-done.11), kind=kLoop, calls=%fused_computation | loop fusion | flops 262144 | bytes 3145728 | tf_op jit(solution)/shard_map/broadcast_in_dim | solution.py:224
  (44 shorter events, 3.6 us)
Async XLA Ops:
  0.0 18.8 %collective-permute-start = (f32[4,5,128,128]{3,2,1,0:T(8,128)}, f32[4,5,128,128]{3,2,1,0:T(8,128)S(1)}, u32[]{:S(2)}, u32[]{:S(2)}) collective-permute-start(f32[4,5,128,128]{3,2,1,0:T(8,128)} %bitcast.32), channel_id=1, source_target_pairs={{0,2},{3,1},{1,0},{2,3},{8,10},{11,9},{9,8},{10,11},{16,18},{19,17... | collective-permute-start | bytes 3932168 | tf_op jit(solution)/shard_map/ppermute | solution.py:166
  0.7 27.6 %collective-permute-start.4 = (f32[4,5,128,128]{3,2,1,0:T(8,128)}, f32[4,5,128,128]{3,2,1,0:T(8,128)}, u32[]{:S(2)}, u32[]{:S(2)}) collective-permute-start(f32[4,5,128,128]{3,2,1,0:T(8,128)} %bitcast.33), channel_id=1, source_target_pairs={{0,8},{1,9},{2,10},{3,11},{4,12},{5,13},{6,14},{7,15},{8,16},{9,17... | collective-permute-start | bytes 3932168 | tf_op jit(solution)/shard_map/ppermute | solution.py:166
  2.8 32.0 %collective-permute-start.1 = (f32[4,5,128,128]{3,2,1,0:T(8,128)}, f32[4,5,128,128]{3,2,1,0:T(8,128)}, u32[]{:S(2)}, u32[]{:S(2)}) collective-permute-start(f32[4,5,128,128]{3,2,1,0:T(8,128)} %bitcast.34), channel_id=1, source_target_pairs={{1,2},{2,1},{9,10},{10,9},{17,18},{18,17},{25,26},{26,25},{4,5},{7... | collective-permute-start | bytes 3932168 | tf_op jit(solution)/shard_map/ppermute | solution.py:166
  7.1 29.2 %collective-permute-start.2 = (f32[4,5,128,128]{3,2,1,0:T(8,128)}, f32[4,5,128,128]{3,2,1,0:T(8,128)}, u32[]{:S(2)}, u32[]{:S(2)}) collective-permute-start(f32[4,5,128,128]{3,2,1,0:T(8,128)} %bitcast.35), channel_id=1, source_target_pairs={{0,1},{3,2},{8,9},{11,10},{16,17},{19,18},{24,25},{27,26},{5,6},{6... | collective-permute-start | bytes 3932168 | tf_op jit(solution)/shard_map/ppermute | solution.py:166
  8.8 37.9 %collective-permute-start.6 = (f32[4,5,128,128]{3,2,1,0:T(8,128)}, f32[4,5,128,128]{3,2,1,0:T(8,128)}, u32[]{:S(2)}, u32[]{:S(2)}) collective-permute-start(f32[4,5,128,128]{3,2,1,0:T(8,128)} %bitcast.36), channel_id=1, source_target_pairs={{0,4},{1,5},{2,6},{3,7},{8,12},{9,13},{10,14},{11,15},{16,20},{17,... | collective-permute-start | bytes 3932168 | tf_op jit(solution)/shard_map/ppermute | solution.py:166
  18.9 11.0 %copy-start = (f32[4,5,128,128]{3,2,1,0:T(8,128)}, f32[4,5,128,128]{3,2,1,0:T(8,128)S(1)}, u32[]{:S(2)}) copy-start(f32[4,5,128,128]{3,2,1,0:T(8,128)S(1)} %collective-permute-done) | copy-start | bytes 3932164
  29.8 36.2 %collective-permute-start.5 = (f32[4,5,128,128]{3,2,1,0:T(8,128)S(1)}, f32[4,5,128,128]{3,2,1,0:T(8,128)S(1)}, u32[]{:S(2)}, u32[]{:S(2)}) collective-permute-start(f32[4,5,128,128]{3,2,1,0:T(8,128)S(1)} %broadcast_select_fusion), channel_id=1, source_target_pairs={{1,0},{2,3},{9,8},{10,11},{17,16},{18,19},{25,24},{26,27},{0,5},{3... | collective-permute-start | bytes 3932168 | tf_op jit(solution)/shard_map/ppermute | solution.py:166
  34.8 31.2 %collective-permute-start.3 = (f32[4,5,128,128]{3,2,1,0:T(8,128)}, f32[4,5,128,128]{3,2,1,0:T(8,128)S(1)}, u32[]{:S(2)}, u32[]{:S(2)}) collective-permute-start(f32[4,5,128,128]{3,2,1,0:T(8,128)} %collective-permute-done.1), channel_id=1, source_target_pairs={{1,0},{2,3},{9,8},{10,11},{17,16},{18,19},{25,24},{26,27},{5,6},{6... | collective-permute-start | bytes 3932168 | tf_op jit(solution)/shard_map/ppermute | solution.py:166
  35.5 30.5 %collective-permute-start.10 = (f32[4,5,128,128]{3,2,1,0:T(8,128)}, f32[4,5,128,128]{3,2,1,0:T(8,128)S(1)}, u32[]{:S(2)}, u32[]{:S(2)}) collective-permute-start(f32[4,5,128,128]{3,2,1,0:T(8,128)} %collective-permute-done.1), channel_id=1, source_target_pairs={{5,13},{6,14},{13,21},{14,22},{21,29},{22,30},{29,5},{30,6}} | collective-permute-start | bytes 3932168 | tf_op jit(solution)/shard_map/ppermute | solution.py:166
  36.3 29.7 %collective-permute-start.9 = (f32[4,5,128,128]{3,2,1,0:T(8,128)}, f32[4,5,128,128]{3,2,1,0:T(8,128)S(1)}, u32[]{:S(2)}, u32[]{:S(2)}) collective-permute-start(f32[4,5,128,128]{3,2,1,0:T(8,128)} %collective-permute-done.2), channel_id=1, source_target_pairs={{1,5},{2,6},{9,13},{10,14},{17,21},{18,22},{25,29},{26,30}} | collective-permute-start | bytes 3932168 | tf_op jit(solution)/shard_map/ppermute | solution.py:166
  46.7 19.1 %collective-permute-start.8 = (s32[209]{0:T(256)S(1)}, s32[209]{0:T(256)S(1)}, u32[]{:S(2)}, u32[]{:S(2)}) collective-permute-start(s32[209]{0:T(256)S(1)} %pad_add_fusion.1), channel_id=1, source_target_pairs={{4,5},{7,6},{12,13},{15,14},{20,21},{23,22},{28,29},{31,30}} | collective-permute-start | bytes 2516 | tf_op jit(solution)/shard_map/ppermute | solution.py:166
  65.8 5.2 %collective-permute-start.7 = (f32[4,5,128,128]{3,2,1,0:T(8,128)}, f32[4,5,128,128]{3,2,1,0:T(8,128)}, u32[]{:S(2)}, u32[]{:S(2)}) collective-permute-start(f32[4,5,128,128]{3,2,1,0:T(8,128)} %collective-permute-done.4), channel_id=1, source_target_pairs={{0,4},{1,5},{2,6},{3,7},{8,12},{9,13},{10,14},{11,15},{16,20},{17,... | collective-permute-start | bytes 3932168 | tf_op jit(solution)/shard_map/ppermute | solution.py:166
  66.0 1.1 %copy-start.2 = (f32[4,5,128,128]{3,2,1,0:T(8,128)}, f32[4,5,128,128]{3,2,1,0:T(8,128)S(1)}, u32[]{:S(2)}) copy-start(f32[4,5,128,128]{3,2,1,0:T(8,128)S(1)} %collective-permute-done.3) | copy-start | bytes 3932164
  66.0 1.5 %copy-start.1 = (f32[4,5,128,128]{3,2,1,0:T(8,128)}, f32[4,5,128,128]{3,2,1,0:T(8,128)S(1)}, u32[]{:S(2)}) copy-start(f32[4,5,128,128]{3,2,1,0:T(8,128)S(1)} %collective-permute-done.5) | copy-start | bytes 3932164
  66.0 1.9 %copy-start.4 = (f32[4,5,128,128]{3,2,1,0:T(8,128)}, f32[4,5,128,128]{3,2,1,0:T(8,128)S(1)}, u32[]{:S(2)}) copy-start(f32[4,5,128,128]{3,2,1,0:T(8,128)S(1)} %collective-permute-done.9) | copy-start | bytes 3932164
  66.0 2.3 %copy-start.3 = (f32[4,5,128,128]{3,2,1,0:T(8,128)}, f32[4,5,128,128]{3,2,1,0:T(8,128)S(1)}, u32[]{:S(2)}) copy-start(f32[4,5,128,128]{3,2,1,0:T(8,128)S(1)} %collective-permute-done.10) | copy-start | bytes 3932164
  69.0 20.4 %collective-permute-start.11 = (f32[16,128,128]{2,1,0:T(8,128)S(1)}, f32[16,128,128]{2,1,0:T(8,128)S(1)}, u32[]{:S(2)}, u32[]{:S(2)}) collective-permute-start(f32[16,128,128]{2,1,0:T(8,128)S(1)} %shard_map.38), channel_id=1, source_target_pairs={{5,4},{6,7},{13,12},{14,15},{21,20},{22,23},{29,28},{30,31}} | collective-permute-start | bytes 3145736 | tf_op jit(solution)/shard_map/ppermute | solution.py:166

commit v5 on v4

--- a/solution.py
+++ b/solution.py
@@ -63,13 +63,14 @@
         total[:NC] = before_ref[0][...] if before_ref else jnp.zeros_like(total[:NC])
         lefts(lambda copy: copy.wait())
 
-        for copy in rights:
-            copy.wait()
-
-        def some(i, carry):
+
+        def some(i, ready):
+            numbers = [words_ref[i * UNROLL + u] for u in range(UNROLL)]
+            most = functools.reduce(jnp.maximum, [(word >> 8) & 255 for word in numbers])
+            for k, copy in enumerate(rights):
+                pl.when((ready <= k) & (most >= k * block))(copy.wait)
             products, targets = [], []
-            for u in range(UNROLL):
-                word = words_ref[i * UNROLL + u]
+            for word in numbers:
                 high, low = split(right_raw[(word >> 8) & 255])
                 both = jnp.concatenate(
                     [
@@ -84,9 +85,11 @@
                 targets.append(word >> 16)
             for product, target in zip(products, targets):
                 total[target] += product
-            return carry
-
-        lax.fori_loop(0, (count + UNROLL - 1) // UNROLL, some, 0)
+            return jnp.maximum(ready, sum(jnp.where(most >= k * block, 1, 0) for k in range(n_right)))
+
+        ready = lax.fori_loop(0, (count + UNROLL - 1) // UNROLL, some, 0)
+        for k, copy in enumerate(rights):
+            pl.when(ready <= k)(copy.wait)
         out_ref[...] = total[:NC]
 
     @pl.when(count == 0)

time: 90.7 us -> 89.1 us (0.982)
  waiting for transfers between devices: 36 us -> 34.5 us
    ppermute x12, waiting for transfers between devices: 36 us -> 34.5 us  [send(): return lax.ppermute(value, ('blk', 'rep'), pairs)]
where the time goes in v5:
time: 89.1 us; the launch traced here: 89 us
  starting transfers between devices  37.3 us (42%)
  waiting for transfers between devices  34.5 us (39%)
  other arithmetic  6.7 us (8%)
  Pallas kernels  5.19 us (6%)
  local copies, waits for them, and re-layouts  4.43 us (5%)
  between operations  0.91 us (1%)
    ppermute x12, starting transfers between devices, send(): return lax.ppermute(value, ('blk', 'rep'), pairs)  37.3 us
    ppermute x12, waiting for transfers between devices, send(): return lax.ppermute(value, ('blk', 'rep'), pairs)  34.5 us
    pallas_call x2, Pallas kernels, contract(): pl.pallas_call(functools.partial(contract_kernel, placed, len(lefts), len...  5.19 us
    unnamed x10, local copies, waits for them, and re-layouts  2.26 us
  transfers between devices with their start and end apart: 12, of which 4 were waited for; matrix products, arithmetic and copies ran while one was open for 9% of the time, Pallas kernels for 6%

profile of v5, /device:TPU:1, one launch (start us, length us, event | category | flops | bytes accessed | tf_op | source)
XLA Modules:
  0.0 89.0 jit_solution(7389333023379737710)
XLA Ops:
  0.0 0.7 collective-permute-start
  0.7 2.1 %collective-permute-start.4 = (f32[4,5,128,128]{3,2,1,0:T(8,128)}, f32[4,5,128,128]{3,2,1,0:T(8,128)}, u32[]{:S(2)}, u32[]{:S(2)}) collective-permute-start(f32[4,5,128,128]{3,2,1,0:T(8,128)} %bitcast.33), channel_id=1, source_target_pairs={{0,8},{1,9},{2,10},{3,11},{4,12},{5,13},{6,14},{7,15},{8,16},{9,17... | collective-permute-start | bytes 3932168 | tf_op jit(solution)/shard_map/ppermute | solution.py:169
  2.8 4.3 %collective-permute-start.1 = (f32[4,5,128,128]{3,2,1,0:T(8,128)}, f32[4,5,128,128]{3,2,1,0:T(8,128)}, u32[]{:S(2)}, u32[]{:S(2)}) collective-permute-start(f32[4,5,128,128]{3,2,1,0:T(8,128)} %bitcast.34), channel_id=1, source_target_pairs={{1,2},{2,1},{9,10},{10,9},{17,18},{18,17},{25,26},{26,25},{4,5},{7... | collective-permute-start | bytes 3932168 | tf_op jit(solution)/shard_map/ppermute | solution.py:169
  7.1 1.7 %collective-permute-start.2 = (f32[4,5,128,128]{3,2,1,0:T(8,128)}, f32[4,5,128,128]{3,2,1,0:T(8,128)}, u32[]{:S(2)}, u32[]{:S(2)}) collective-permute-start(f32[4,5,128,128]{3,2,1,0:T(8,128)} %bitcast.35), channel_id=1, source_target_pairs={{0,1},{3,2},{8,9},{11,10},{16,17},{19,18},{24,25},{27,26},{5,6},{6... | collective-permute-start | bytes 3932168 | tf_op jit(solution)/shard_map/ppermute | solution.py:169
  8.8 6.9 %collective-permute-start.6 = (f32[4,5,128,128]{3,2,1,0:T(8,128)}, f32[4,5,128,128]{3,2,1,0:T(8,128)}, u32[]{:S(2)}, u32[]{:S(2)}) collective-permute-start(f32[4,5,128,128]{3,2,1,0:T(8,128)} %bitcast.36), channel_id=1, source_target_pairs={{0,4},{1,5},{2,6},{3,7},{8,12},{9,13},{10,14},{11,15},{16,20},{17,... | collective-permute-start | bytes 3932168 | tf_op jit(solution)/shard_map/ppermute | solution.py:169
  15.9 0.7 fusion.2
  16.6 1.4 %slice_divide_fusion = (s32[4,1,48]{2,0,1:T(4,128)S(1)}, s32[4,1,48]{2,0,1:T(4,128)S(1)}, s32[4,1,48]{2,0,1:T(4,128)S(1)}, s32[4,1,48]{2,0,1:T(4,128)S(1)}, s32[...) fusion(s32[4,3,48]{2,0,1:T(4,128)} %bitcast.48, pred[4,1,48]{2,0,1:T(4,128)(4,1)S(1)} %get-tuple-element.13, ...), kind=kLoop, calls=%fused_computation.25 | loop fusion | flops 2878 | bytes 5771 | tf_op jit(solution)/shard_map/jit(floor_divide)/div | solution.py:175
  18.9 9.5 %collective-permute-done.4 = f32[4,5,128,128]{3,2,1,0:T(8,128)} collective-permute-done((f32[4,5,128,128]{3,2,1,0:T(8,128)}, f32[4,5,128,128]{3,2,1,0:T(8,128)}, u32[]{:S(2)}, u32[]{:S(2)}) %collective-permute-start.4) | collective-permute-done | bytes 1310752 | tf_op jit(solution)/shard_map/ppermute | solution.py:169
  28.3 1.5 %broadcast_select_fusion = f32[4,5,128,128]{3,2,1,0:T(8,128)S(1)} fusion(f32[4,5,128,128]{3,2,1,0:T(8,128)S(1)} %collective-permute-done, f32[4,5,128,128]{3,2,1,0:T(8,128)} %collective-permute-done.4, pred[]{:T(512)S(6)} %or.22), kind=kLoop, calls=%fused_computation.1 | loop fusion | flops 327680 | bytes 3932161 | tf_op jit(solution)/shard_map/jit(_where)/select_n | solution.py:200
  29.8 0.7 collective-permute-start.5
  30.6 4.2 %collective-permute-done.1 = f32[4,5,128,128]{3,2,1,0:T(8,128)} collective-permute-done((f32[4,5,128,128]{3,2,1,0:T(8,128)}, f32[4,5,128,128]{3,2,1,0:T(8,128)}, u32[]{:S(2)}, u32[]{:S(2)}) %collective-permute-start.1) | collective-permute-done | bytes 1310752 | tf_op jit(solution)/shard_map/ppermute | solution.py:169
  34.8 0.7 collective-permute-start.3
  35.5 0.7 collective-permute-start.10
  36.3 0.7 collective-permute-start.9
  37.6 0.7 pad_add_fusion.1
  38.3 8.4 %collective-permute-done.6 = f32[4,5,128,128]{3,2,1,0:T(8,128)} collective-permute-done((f32[4,5,128,128]{3,2,1,0:T(8,128)}, f32[4,5,128,128]{3,2,1,0:T(8,128)}, u32[]{:S(2)}, u32[]{:S(2)}) %collective-permute-start.6) | collective-permute-done | bytes 1310752 | tf_op jit(solution)/shard_map/ppermute | solution.py:169
  46.7 17.2 %collective-permute-start.8 = (s32[209]{0:T(256)S(1)}, s32[209]{0:T(256)S(1)}, u32[]{:S(2)}, u32[]{:S(2)}) collective-permute-start(s32[209]{0:T(256)S(1)} %pad_add_fusion.1), channel_id=1, source_target_pairs={{4,5},{7,6},{12,13},{15,14},{20,21},{23,22},{28,29},{31,30}} | collective-permute-start | bytes 2516 | tf_op jit(solution)/shard_map/ppermute | solution.py:169
  64.0 1.2 %slice.30 = f32[1,1,1]{2,1,0:T(1,128)} slice(f32[20,128,128]{2,1,0:T(8,128)} %bitcast.10.refs_7_), slice={[0:1], [0:1], [0:1]} | slice | bytes 8 | tf_op jit(solution)/shard_map/slice | solution.py:127
  66.1 1.0 %copy-done.2 = f32[4,5,128,128]{3,2,1,0:T(8,128)} copy-done((f32[4,5,128,128]{3,2,1,0:T(8,128)}, f32[4,5,128,128]{3,2,1,0:T(8,128)S(1)}, u32[]{:S(2)}) %copy-start.2) | copy-done | bytes 1310744
  69.0 1.3 %collective-permute-start.11 = (f32[16,128,128]{2,1,0:T(8,128)S(1)}, f32[16,128,128]{2,1,0:T(8,128)S(1)}, u32[]{:S(2)}, u32[]{:S(2)}) collective-permute-start(f32[16,128,128]{2,1,0:T(8,128)S(1)} %shard_map.38), channel_id=1, source_target_pairs={{5,4},{6,7},{13,12},{14,15},{21,20},{22,23},{29,28},{30,31}} | collective-permute-start | bytes 3145736 | tf_op jit(solution)/shard_map/ppermute | solution.py:169
  70.3 0.7 pad_add_fusion.words_ref
  71.0 4.5 %shard_map.37 = f32[16,128,128]{2,1,0:T(8,128)S(1)} custom-call(s32[210]{0:T(256)S(1)} %pad_add_fusion.words_ref, f32[20,128,128]{2,1,0:T(8,128)} %bitcast.38, f32[20,128,128]{2,1,0:T(8,128)} %bitcast.40, f32[20,128,128]{2,1,0:T(8,128)} %bitcast.6.refs_2_.refs_3_, f32[20,128,128]{2,1,0:T(8,128)} %bitcast.7.refs_3_.refs_1_, f32[20,128,128]{2,1,0:T(8,128)} %bitcast.44, ...), custom_call_target="tpu_custom_call" | custom-call | flops 1000 | bytes 1000 | tf_op jit(solution)/shard_map/pallas_call | solution.py:110
  75.5 12.3 %collective-permute-done.11 = f32[16,128,128]{2,1,0:T(8,128)S(1)} collective-permute-done((f32[16,128,128]{2,1,0:T(8,128)S(1)}, f32[16,128,128]{2,1,0:T(8,128)S(1)}, u32[]{:S(2)}, u32[]{:S(2)}) %collective-permute-start.11) | collective-permute-done | bytes 1048608 | tf_op jit(solution)/shard_map/ppermute | solution.py:169
  87.9 1.1 %add_bitcast_fusion = f32[1,1,16,128,128]{4,3,2,1,0:T(8,128)} fusion(f32[16,128,128]{2,1,0:T(8,128)S(1)} %shard_map.37, f32[16,128,128]{2,1,0:T(8,128)S(1)} %collective-permute-done.11), kind=kLoop, calls=%fused_computation | loop fusion | flops 262144 | bytes 3145728 | tf_op jit(solution)/shard_map/broadcast_in_dim | solution.py:227
  (44 shorter events, 3.6 us)
Async XLA Ops:
  0.0 18.8 %collective-permute-start = (f32[4,5,128,128]{3,2,1,0:T(8,128)}, f32[4,5,128,128]{3,2,1,0:T(8,128)S(1)}, u32[]{:S(2)}, u32[]{:S(2)}) collective-permute-start(f32[4,5,128,128]{3,2,1,0:T(8,128)} %bitcast.32), channel_id=1, source_target_pairs={{0,2},{3,1},{1,0},{2,3},{8,10},{11,9},{9,8},{10,11},{16,18},{19,17... | collective-permute-start | bytes 3932168 | tf_op jit(solution)/shard_map/ppermute | solution.py:169
  0.7 27.6 %collective-permute-start.4 = (f32[4,5,128,128]{3,2,1,0:T(8,128)}, f32[4,5,128,128]{3,2,1,0:T(8,128)}, u32[]{:S(2)}, u32[]{:S(2)}) collective-permute-start(f32[4,5,128,128]{3,2,1,0:T(8,128)} %bitcast.33), channel_id=1, source_target_pairs={{0,8},{1,9},{2,10},{3,11},{4,12},{5,13},{6,14},{7,15},{8,16},{9,17... | collective-permute-start | bytes 3932168 | tf_op jit(solution)/shard_map/ppermute | solution.py:169
  2.8 32.0 %collective-permute-start.1 = (f32[4,5,128,128]{3,2,1,0:T(8,128)}, f32[4,5,128,128]{3,2,1,0:T(8,128)}, u32[]{:S(2)}, u32[]{:S(2)}) collective-permute-start(f32[4,5,128,128]{3,2,1,0:T(8,128)} %bitcast.34), channel_id=1, source_target_pairs={{1,2},{2,1},{9,10},{10,9},{17,18},{18,17},{25,26},{26,25},{4,5},{7... | collective-permute-start | bytes 3932168 | tf_op jit(solution)/shard_map/ppermute | solution.py:169
  7.1 29.2 %collective-permute-start.2 = (f32[4,5,128,128]{3,2,1,0:T(8,128)}, f32[4,5,128,128]{3,2,1,0:T(8,128)}, u32[]{:S(2)}, u32[]{:S(2)}) collective-permute-start(f32[4,5,128,128]{3,2,1,0:T(8,128)} %bitcast.35), channel_id=1, source_target_pairs={{0,1},{3,2},{8,9},{11,10},{16,17},{19,18},{24,25},{27,26},{5,6},{6... | collective-permute-start | bytes 3932168 | tf_op jit(solution)/shard_map/ppermute | solution.py:169
  8.8 37.9 %collective-permute-start.6 = (f32[4,5,128,128]{3,2,1,0:T(8,128)}, f32[4,5,128,128]{3,2,1,0:T(8,128)}, u32[]{:S(2)}, u32[]{:S(2)}) collective-permute-start(f32[4,5,128,128]{3,2,1,0:T(8,128)} %bitcast.36), channel_id=1, source_target_pairs={{0,4},{1,5},{2,6},{3,7},{8,12},{9,13},{10,14},{11,15},{16,20},{17,... | collective-permute-start | bytes 3932168 | tf_op jit(solution)/shard_map/ppermute | solution.py:169
  18.9 11.0 %copy-start = (f32[4,5,128,128]{3,2,1,0:T(8,128)}, f32[4,5,128,128]{3,2,1,0:T(8,128)S(1)}, u32[]{:S(2)}) copy-start(f32[4,5,128,128]{3,2,1,0:T(8,128)S(1)} %collective-permute-done) | copy-start | bytes 3932164
  29.8 36.2 %collective-permute-start.5 = (f32[4,5,128,128]{3,2,1,0:T(8,128)S(1)}, f32[4,5,128,128]{3,2,1,0:T(8,128)S(1)}, u32[]{:S(2)}, u32[]{:S(2)}) collective-permute-start(f32[4,5,128,128]{3,2,1,0:T(8,128)S(1)} %broadcast_select_fusion), channel_id=1, source_target_pairs={{1,0},{2,3},{9,8},{10,11},{17,16},{18,19},{25,24},{26,27},{0,5},{3... | collective-permute-start | bytes 3932168 | tf_op jit(solution)/shard_map/ppermute | solution.py:169
  34.8 31.2 %collective-permute-start.3 = (f32[4,5,128,128]{3,2,1,0:T(8,128)}, f32[4,5,128,128]{3,2,1,0:T(8,128)S(1)}, u32[]{:S(2)}, u32[]{:S(2)}) collective-permute-start(f32[4,5,128,128]{3,2,1,0:T(8,128)} %collective-permute-done.1), channel_id=1, source_target_pairs={{1,0},{2,3},{9,8},{10,11},{17,16},{18,19},{25,24},{26,27},{5,6},{6... | collective-permute-start | bytes 3932168 | tf_op jit(solution)/shard_map/ppermute | solution.py:169
  35.5 30.5 %collective-permute-start.10 = (f32[4,5,128,128]{3,2,1,0:T(8,128)}, f32[4,5,128,128]{3,2,1,0:T(8,128)S(1)}, u32[]{:S(2)}, u32[]{:S(2)}) collective-permute-start(f32[4,5,128,128]{3,2,1,0:T(8,128)} %collective-permute-done.1), channel_id=1, source_target_pairs={{5,13},{6,14},{13,21},{14,22},{21,29},{22,30},{29,5},{30,6}} | collective-permute-start | bytes 3932168 | tf_op jit(solution)/shard_map/ppermute | solution.py:169
  36.3 29.7 %collective-permute-start.9 = (f32[4,5,128,128]{3,2,1,0:T(8,128)}, f32[4,5,128,128]{3,2,1,0:T(8,128)S(1)}, u32[]{:S(2)}, u32[]{:S(2)}) collective-permute-start(f32[4,5,128,128]{3,2,1,0:T(8,128)} %collective-permute-done.2), channel_id=1, source_target_pairs={{1,5},{2,6},{9,13},{10,14},{17,21},{18,22},{25,29},{26,30}} | collective-permute-start | bytes 3932168 | tf_op jit(solution)/shard_map/ppermute | solution.py:169
  46.7 19.1 %collective-permute-start.8 = (s32[209]{0:T(256)S(1)}, s32[209]{0:T(256)S(1)}, u32[]{:S(2)}, u32[]{:S(2)}) collective-permute-start(s32[209]{0:T(256)S(1)} %pad_add_fusion.1), channel_id=1, source_target_pairs={{4,5},{7,6},{12,13},{15,14},{20,21},{23,22},{28,29},{31,30}} | collective-permute-start | bytes 2516 | tf_op jit(solution)/shard_map/ppermute | solution.py:169
  65.8 5.2 %collective-permute-start.7 = (f32[4,5,128,128]{3,2,1,0:T(8,128)}, f32[4,5,128,128]{3,2,1,0:T(8,128)}, u32[]{:S(2)}, u32[]{:S(2)}) collective-permute-start(f32[4,5,128,128]{3,2,1,0:T(8,128)} %collective-permute-done.4), channel_id=1, source_target_pairs={{0,4},{1,5},{2,6},{3,7},{8,12},{9,13},{10,14},{11,15},{16,20},{17,... | collective-permute-start | bytes 3932168 | tf_op jit(solution)/shard_map/ppermute | solution.py:169
  66.0 1.1 %copy-start.2 = (f32[4,5,128,128]{3,2,1,0:T(8,128)}, f32[4,5,128,128]{3,2,1,0:T(8,128)S(1)}, u32[]{:S(2)}) copy-start(f32[4,5,128,128]{3,2,1,0:T(8,128)S(1)} %collective-permute-done.3) | copy-start | bytes 3932164
  66.0 1.5 %copy-start.1 = (f32[4,5,128,128]{3,2,1,0:T(8,128)}, f32[4,5,128,128]{3,2,1,0:T(8,128)S(1)}, u32[]{:S(2)}) copy-start(f32[4,5,128,128]{3,2,1,0:T(8,128)S(1)} %collective-permute-done.5) | copy-start | bytes 3932164
  66.0 1.9 %copy-start.4 = (f32[4,5,128,128]{3,2,1,0:T(8,128)}, f32[4,5,128,128]{3,2,1,0:T(8,128)S(1)}, u32[]{:S(2)}) copy-start(f32[4,5,128,128]{3,2,1,0:T(8,128)S(1)} %collective-permute-done.9) | copy-start | bytes 3932164
  66.0 2.3 %copy-start.3 = (f32[4,5,128,128]{3,2,1,0:T(8,128)}, f32[4,5,128,128]{3,2,1,0:T(8,128)S(1)}, u32[]{:S(2)}) copy-start(f32[4,5,128,128]{3,2,1,0:T(8,128)S(1)} %collective-permute-done.10) | copy-start | bytes 3932164
  69.0 18.9 %collective-permute-start.11 = (f32[16,128,128]{2,1,0:T(8,128)S(1)}, f32[16,128,128]{2,1,0:T(8,128)S(1)}, u32[]{:S(2)}, u32[]{:S(2)}) collective-permute-start(f32[16,128,128]{2,1,0:T(8,128)S(1)} %shard_map.38), channel_id=1, source_target_pairs={{5,4},{6,7},{13,12},{14,15},{21,20},{22,23},{29,28},{30,31}} | collective-permute-start | bytes 3145736 | tf_op jit(solution)/shard_map/ppermute | solution.py:169

commit v6 on v5

--- a/solution.py
+++ b/solution.py
@@ -102,9 +102,6 @@
     placed = placed or [(b,) for b in range(len(lefts))]
     blocks = 1 + max(place for places in placed for place in places if place is not None)
     planned = jnp.append(planned, jnp.int32(kind))
-    lefts, rights = [
-        [pltpu.with_memory_space_constraint(x, pltpu.HBM) for x in xs] for xs in (lefts, rights)
-    ]
     operands = [planned, *lefts, *rights] + ([] if before is None else [before])
     size = (blocks * block + len(rights) * block + 3 * NC + 1) * tile * tile
     return pl.pallas_call(
@@ -205,7 +202,12 @@
     own, p1, p2, p3, q1, q2, h1, h2, two, alternate, swapped = [
         x.reshape(-1, tile, tile) for x in (own, p1, p2, p3, q1, q2, h1, h2, two, alternate, swapped)
     ]
-    part = contract(their_words + probe(alternate), [own, p3, q1], [p2, h1, h2, q2])
+    their_words = their_words + probe(alternate)
+    own, p1, p2, p3, two, q2, swapped, alternate = [
+        pltpu.with_memory_space_constraint(x, pltpu.HBM)
+        for x in (own, p1, p2, p3, two, q2, swapped, alternate)
+    ]
+    part = contract(their_words, [own, p3, q1], [p2, h1, h2, q2])
     part = send(part, (odd, outward, 0))
 
     lefts = [own, p1, p2, p3, q1, q2]

time: 89.1 us -> 88.3 us (level)
  local copies, waits for them, and re-layouts: 4.43 us -> 3.18 us
  waiting for transfers between devices: 34.5 us -> 35.6 us
    unnamed x10 -> x6, local copies, waits for them, and re-layouts: 2.26 us -> 1.03 us
    ppermute x12, waiting for transfers between devices: 34.5 us -> 35.6 us  [send(): return lax.ppermute(value, ('blk', 'rep'), pairs)]
  transfers between devices with their start and end apart: 12 -> 12, of which waited for: 4 -> 4; matrix products, arithmetic and copies ran while one was open for 9% -> 9% of each run, Pallas kernels for 6% -> 5%
where the time goes in v6:
time: 88.3 us; the launch traced here: 88.4 us
  starting transfers between devices  37.2 us (42%)
  waiting for transfers between devices  35.6 us (40%)
  other arithmetic  6.59 us (7%)
  Pallas kernels  4.85 us (5%)
  local copies, waits for them, and re-layouts  3.18 us (4%)
  between operations  0.9 us (1%)
    ppermute x12, starting transfers between devices, send(): return lax.ppermute(value, ('blk', 'rep'), pairs)  37.2 us
    ppermute x12, waiting for transfers between devices, send(): return lax.ppermute(value, ('blk', 'rep'), pairs)  35.6 us
    pallas_call x2, Pallas kernels, contract(): pl.pallas_call(functools.partial(contract_kernel, placed, len(lefts), len...  4.85 us
  transfers between devices with their start and end apart: 12, of which 4 were waited for; matrix products, arithmetic and copies ran while one was open for 9% of the time, Pallas kernels for 5%

profile of v6, /device:TPU:1, one launch (start us, length us, event | category | flops | bytes accessed | tf_op | source)
XLA Modules:
  0.0 88.4 jit_solution(15328250194661372208)
XLA Ops:
  0.0 0.7 collective-permute-start
  0.7 2.1 %collective-permute-start.4 = (f32[4,5,128,128]{3,2,1,0:T(8,128)}, f32[4,5,128,128]{3,2,1,0:T(8,128)}, u32[]{:S(2)}, u32[]{:S(2)}) collective-permute-start(f32[4,5,128,128]{3,2,1,0:T(8,128)} %bitcast.37), channel_id=1, source_target_pairs={{0,8},{1,9},{2,10},{3,11},{4,12},{5,13},{6,14},{7,15},{8,16},{9,17... | collective-permute-start | bytes 3932168 | tf_op jit(solution)/shard_map/ppermute | solution.py:166
  2.8 3.3 %collective-permute-start.1 = (f32[4,5,128,128]{3,2,1,0:T(8,128)}, f32[4,5,128,128]{3,2,1,0:T(8,128)S(1)}, u32[]{:S(2)}, u32[]{:S(2)}) collective-permute-start(f32[4,5,128,128]{3,2,1,0:T(8,128)} %bitcast.38), channel_id=1, source_target_pairs={{1,2},{2,1},{9,10},{10,9},{17,18},{18,17},{25,26},{26,25},{4,5},{7... | collective-permute-start | bytes 3932168 | tf_op jit(solution)/shard_map/ppermute | solution.py:166
  6.1 1.7 %collective-permute-start.2 = (f32[4,5,128,128]{3,2,1,0:T(8,128)}, f32[4,5,128,128]{3,2,1,0:T(8,128)}, u32[]{:S(2)}, u32[]{:S(2)}) collective-permute-start(f32[4,5,128,128]{3,2,1,0:T(8,128)} %bitcast.39), channel_id=1, source_target_pairs={{0,1},{3,2},{8,9},{11,10},{16,17},{19,18},{24,25},{27,26},{5,6},{6... | collective-permute-start | bytes 3932168 | tf_op jit(solution)/shard_map/ppermute | solution.py:166
  7.8 7.8 %collective-permute-start.6 = (f32[4,5,128,128]{3,2,1,0:T(8,128)}, f32[4,5,128,128]{3,2,1,0:T(8,128)}, u32[]{:S(2)}, u32[]{:S(2)}) collective-permute-start(f32[4,5,128,128]{3,2,1,0:T(8,128)} %bitcast.40), channel_id=1, source_target_pairs={{0,4},{1,5},{2,6},{3,7},{8,12},{9,13},{10,14},{11,15},{16,20},{17,... | collective-permute-start | bytes 3932168 | tf_op jit(solution)/shard_map/ppermute | solution.py:166
  15.9 0.7 fusion.2
  16.6 1.4 %slice_divide_fusion = (s32[4,1,48]{2,0,1:T(4,128)S(1)}, s32[4,1,48]{2,0,1:T(4,128)S(1)}, s32[4,1,48]{2,0,1:T(4,128)S(1)}, s32[4,1,48]{2,0,1:T(4,128)S(1)}, s32[...) fusion(s32[4,3,48]{2,0,1:T(4,128)} %bitcast.50, pred[4,1,48]{2,0,1:T(4,128)(4,1)S(1)} %get-tuple-element.13, ...), kind=kLoop, calls=%fused_computation.25 | loop fusion | flops 2878 | bytes 5771 | tf_op jit(solution)/shard_map/jit(floor_divide)/div | solution.py:172
  18.8 9.6 %collective-permute-done.4 = f32[4,5,128,128]{3,2,1,0:T(8,128)} collective-permute-done((f32[4,5,128,128]{3,2,1,0:T(8,128)}, f32[4,5,128,128]{3,2,1,0:T(8,128)}, u32[]{:S(2)}, u32[]{:S(2)}) %collective-permute-start.4) | collective-permute-done | bytes 1310752 | tf_op jit(solution)/shard_map/ppermute | solution.py:166
  28.3 1.5 %broadcast_select_fusion = f32[4,5,128,128]{3,2,1,0:T(8,128)S(1)} fusion(f32[4,5,128,128]{3,2,1,0:T(8,128)S(1)} %collective-permute-done, f32[4,5,128,128]{3,2,1,0:T(8,128)} %collective-permute-done.4, pred[]{:T(512)S(6)} %or.22), kind=kLoop, calls=%fused_computation.1 | loop fusion | flops 327680 | bytes 3932161 | tf_op jit(solution)/shard_map/jit(_where)/select_n | solution.py:197
  29.8 0.7 collective-permute-start.5
  30.6 4.2 %collective-permute-done.1 = f32[4,5,128,128]{3,2,1,0:T(8,128)S(1)} collective-permute-done((f32[4,5,128,128]{3,2,1,0:T(8,128)}, f32[4,5,128,128]{3,2,1,0:T(8,128)S(1)}, u32[]{:S(2)}, u32[]{:S(2)}) %collective-permute-start.1) | collective-permute-done | bytes 1310752 | tf_op jit(solution)/shard_map/ppermute | solution.py:166
  34.8 0.7 collective-permute-start.3
  35.5 0.7 collective-permute-start.10
  36.3 0.7 collective-permute-start.9
  37.6 0.7 pad_add_fusion.1
  38.3 8.4 %collective-permute-done.6 = f32[4,5,128,128]{3,2,1,0:T(8,128)} collective-permute-done((f32[4,5,128,128]{3,2,1,0:T(8,128)}, f32[4,5,128,128]{3,2,1,0:T(8,128)}, u32[]{:S(2)}, u32[]{:S(2)}) %collective-permute-start.6) | collective-permute-done | bytes 1310752 | tf_op jit(solution)/shard_map/ppermute | solution.py:166
  46.7 17.2 %collective-permute-start.8 = (s32[209]{0:T(256)S(1)}, s32[209]{0:T(256)S(1)}, u32[]{:S(2)}, u32[]{:S(2)}) collective-permute-start(s32[209]{0:T(256)S(1)} %pad_add_fusion.1), channel_id=1, source_target_pairs={{4,5},{7,6},{12,13},{15,14},{20,21},{23,22},{28,29},{31,30}} | collective-permute-start | bytes 2516 | tf_op jit(solution)/shard_map/ppermute | solution.py:166
  64.0 1.2 %slice.30 = f32[1,1,1]{2,1,0:T(1,128)} slice(f32[20,128,128]{2,1,0:T(8,128)} %bitcast.10.refs_7_), slice={[0:1], [0:1], [0:1]} | slice | bytes 8 | tf_op jit(solution)/shard_map/slice | solution.py:124
  66.0 1.0 %copy-done.2 = f32[4,5,128,128]{3,2,1,0:T(8,128)} copy-done((f32[4,5,128,128]{3,2,1,0:T(8,128)}, f32[4,5,128,128]{3,2,1,0:T(8,128)S(1)}, u32[]{:S(2)}) %copy-start.2) | copy-done | bytes 1310744
  67.0 0.7 shard_map.38
  67.7 1.3 %collective-permute-start.11 = (f32[16,128,128]{2,1,0:T(8,128)S(1)}, f32[16,128,128]{2,1,0:T(8,128)S(1)}, u32[]{:S(2)}, u32[]{:S(2)}) collective-permute-start(f32[16,128,128]{2,1,0:T(8,128)S(1)} %shard_map.38), channel_id=1, source_target_pairs={{5,4},{6,7},{13,12},{14,15},{21,20},{22,23},{29,28},{30,31}} | collective-permute-start | bytes 3145736 | tf_op jit(solution)/shard_map/ppermute | solution.py:166
  69.7 4.2 %shard_map.37 = f32[16,128,128]{2,1,0:T(8,128)S(1)} custom-call(s32[210]{0:T(256)S(1)} %pad_add_fusion.words_ref, f32[20,128,128]{2,1,0:T(8,128)} %bitcast.42, f32[20,128,128]{2,1,0:T(8,128)} %bitcast.44, f32[20,128,128]{2,1,0:T(8,128)} %bitcast.46, f32[20,128,128]{2,1,0:T(8,128)} %bitcast.7.refs_3_.refs_1_, f32[20,128,128]{2,1,0:T(8,128)S(1)} %bitcast.33, ...), custom_call_target="tpu_custom_call" | custom-call | flops 1000 | bytes 1000 | tf_op jit(solution)/shard_map/pallas_call | solution.py:107
  73.9 13.4 %collective-permute-done.11 = f32[16,128,128]{2,1,0:T(8,128)S(1)} collective-permute-done((f32[16,128,128]{2,1,0:T(8,128)S(1)}, f32[16,128,128]{2,1,0:T(8,128)S(1)}, u32[]{:S(2)}, u32[]{:S(2)}) %collective-permute-start.11) | collective-permute-done | bytes 1048608 | tf_op jit(solution)/shard_map/ppermute | solution.py:166
  87.3 1.1 %add_bitcast_fusion = f32[1,1,16,128,128]{4,3,2,1,0:T(8,128)} fusion(f32[16,128,128]{2,1,0:T(8,128)S(1)} %shard_map.37, f32[16,128,128]{2,1,0:T(8,128)S(1)} %collective-permute-done.11), kind=kLoop, calls=%fused_computation | loop fusion | flops 262144 | bytes 3145728 | tf_op jit(solution)/shard_map/broadcast_in_dim | solution.py:229
  (40 shorter events, 2.3 us)
Async XLA Ops:
  0.0 18.8 %collective-permute-start = (f32[4,5,128,128]{3,2,1,0:T(8,128)}, f32[4,5,128,128]{3,2,1,0:T(8,128)S(1)}, u32[]{:S(2)}, u32[]{:S(2)}) collective-permute-start(f32[4,5,128,128]{3,2,1,0:T(8,128)} %bitcast.36), channel_id=1, source_target_pairs={{0,2},{3,1},{1,0},{2,3},{8,10},{11,9},{9,8},{10,11},{16,18},{19,17... | collective-permute-start | bytes 3932168 | tf_op jit(solution)/shard_map/ppermute | solution.py:166
  0.7 27.6 %collective-permute-start.4 = (f32[4,5,128,128]{3,2,1,0:T(8,128)}, f32[4,5,128,128]{3,2,1,0:T(8,128)}, u32[]{:S(2)}, u32[]{:S(2)}) collective-permute-start(f32[4,5,128,128]{3,2,1,0:T(8,128)} %bitcast.37), channel_id=1, source_target_pairs={{0,8},{1,9},{2,10},{3,11},{4,12},{5,13},{6,14},{7,15},{8,16},{9,17... | collective-permute-start | bytes 3932168 | tf_op jit(solution)/shard_map/ppermute | solution.py:166
  2.8 31.9 %collective-permute-start.1 = (f32[4,5,128,128]{3,2,1,0:T(8,128)}, f32[4,5,128,128]{3,2,1,0:T(8,128)S(1)}, u32[]{:S(2)}, u32[]{:S(2)}) collective-permute-start(f32[4,5,128,128]{3,2,1,0:T(8,128)} %bitcast.38), channel_id=1, source_target_pairs={{1,2},{2,1},{9,10},{10,9},{17,18},{18,17},{25,26},{26,25},{4,5},{7... | collective-permute-start | bytes 3932168 | tf_op jit(solution)/shard_map/ppermute | solution.py:166
  6.1 30.2 %collective-permute-start.2 = (f32[4,5,128,128]{3,2,1,0:T(8,128)}, f32[4,5,128,128]{3,2,1,0:T(8,128)}, u32[]{:S(2)}, u32[]{:S(2)}) collective-permute-start(f32[4,5,128,128]{3,2,1,0:T(8,128)} %bitcast.39), channel_id=1, source_target_pairs={{0,1},{3,2},{8,9},{11,10},{16,17},{19,18},{24,25},{27,26},{5,6},{6... | collective-permute-start | bytes 3932168 | tf_op jit(solution)/shard_map/ppermute | solution.py:166
  7.8 38.9 %collective-permute-start.6 = (f32[4,5,128,128]{3,2,1,0:T(8,128)}, f32[4,5,128,128]{3,2,1,0:T(8,128)}, u32[]{:S(2)}, u32[]{:S(2)}) collective-permute-start(f32[4,5,128,128]{3,2,1,0:T(8,128)} %bitcast.40), channel_id=1, source_target_pairs={{0,4},{1,5},{2,6},{3,7},{8,12},{9,13},{10,14},{11,15},{16,20},{17,... | collective-permute-start | bytes 3932168 | tf_op jit(solution)/shard_map/ppermute | solution.py:166
  18.8 11.0 %copy-start = (f32[4,5,128,128]{3,2,1,0:T(8,128)}, f32[4,5,128,128]{3,2,1,0:T(8,128)S(1)}, u32[]{:S(2)}) copy-start(f32[4,5,128,128]{3,2,1,0:T(8,128)S(1)} %collective-permute-done) | copy-start | bytes 3932164
  29.8 36.2 %collective-permute-start.5 = (f32[4,5,128,128]{3,2,1,0:T(8,128)S(1)}, f32[4,5,128,128]{3,2,1,0:T(8,128)S(1)}, u32[]{:S(2)}, u32[]{:S(2)}) collective-permute-start(f32[4,5,128,128]{3,2,1,0:T(8,128)S(1)} %broadcast_select_fusion), channel_id=1, source_target_pairs={{1,0},{2,3},{9,8},{10,11},{17,16},{18,19},{25,24},{26,27},{0,5},{3... | collective-permute-start | bytes 3932168 | tf_op jit(solution)/shard_map/ppermute | solution.py:166
  34.8 31.2 %copy-start.1 = (f32[4,5,128,128]{3,2,1,0:T(8,128)}, f32[4,5,128,128]{3,2,1,0:T(8,128)S(1)}, u32[]{:S(2)}) copy-start(f32[4,5,128,128]{3,2,1,0:T(8,128)S(1)} %collective-permute-done.1) | copy-start | bytes 3932164
  34.8 31.2 %collective-permute-start.3 = (f32[4,5,128,128]{3,2,1,0:T(8,128)S(1)}, f32[4,5,128,128]{3,2,1,0:T(8,128)S(1)}, u32[]{:S(2)}, u32[]{:S(2)}) collective-permute-start(f32[4,5,128,128]{3,2,1,0:T(8,128)S(1)} %collective-permute-done.1), channel_id=1, source_target_pairs={{1,0},{2,3},{9,8},{10,11},{17,16},{18,19},{25,24},{26,27},{5,6},{6... | collective-permute-start | bytes 3932168 | tf_op jit(solution)/shard_map/ppermute | solution.py:166
  35.5 30.5 %collective-permute-start.10 = (f32[4,5,128,128]{3,2,1,0:T(8,128)S(1)}, f32[4,5,128,128]{3,2,1,0:T(8,128)S(1)}, u32[]{:S(2)}, u32[]{:S(2)}) collective-permute-start(f32[4,5,128,128]{3,2,1,0:T(8,128)S(1)} %collective-permute-done.1), channel_id=1, source_target_pairs={{5,13},{6,14},{13,21},{14,22},{21,29},{22,30},{29,5},{30,6}} | collective-permute-start | bytes 3932168 | tf_op jit(solution)/shard_map/ppermute | solution.py:166
  36.3 29.7 %collective-permute-start.9 = (f32[4,5,128,128]{3,2,1,0:T(8,128)}, f32[4,5,128,128]{3,2,1,0:T(8,128)S(1)}, u32[]{:S(2)}, u32[]{:S(2)}) collective-permute-start(f32[4,5,128,128]{3,2,1,0:T(8,128)} %collective-permute-done.2), channel_id=1, source_target_pairs={{1,5},{2,6},{9,13},{10,14},{17,21},{18,22},{25,29},{26,30}} | collective-permute-start | bytes 3932168 | tf_op jit(solution)/shard_map/ppermute | solution.py:166
  46.7 19.1 %collective-permute-start.8 = (s32[209]{0:T(256)S(1)}, s32[209]{0:T(256)S(1)}, u32[]{:S(2)}, u32[]{:S(2)}) collective-permute-start(s32[209]{0:T(256)S(1)} %pad_add_fusion.1), channel_id=1, source_target_pairs={{4,5},{7,6},{12,13},{15,14},{20,21},{23,22},{28,29},{31,30}} | collective-permute-start | bytes 2516 | tf_op jit(solution)/shard_map/ppermute | solution.py:166
  65.8 3.9 %collective-permute-start.7 = (f32[4,5,128,128]{3,2,1,0:T(8,128)}, f32[4,5,128,128]{3,2,1,0:T(8,128)}, u32[]{:S(2)}, u32[]{:S(2)}) collective-permute-start(f32[4,5,128,128]{3,2,1,0:T(8,128)} %collective-permute-done.4), channel_id=1, source_target_pairs={{0,4},{1,5},{2,6},{3,7},{8,12},{9,13},{10,14},{11,15},{16,20},{17,... | collective-permute-start | bytes 3932168 | tf_op jit(solution)/shard_map/ppermute | solution.py:166
  66.0 1.1 %copy-start.2 = (f32[4,5,128,128]{3,2,1,0:T(8,128)}, f32[4,5,128,128]{3,2,1,0:T(8,128)S(1)}, u32[]{:S(2)}) copy-start(f32[4,5,128,128]{3,2,1,0:T(8,128)S(1)} %collective-permute-done.5) | copy-start | bytes 3932164
  67.7 19.5 %collective-permute-start.11 = (f32[16,128,128]{2,1,0:T(8,128)S(1)}, f32[16,128,128]{2,1,0:T(8,128)S(1)}, u32[]{:S(2)}, u32[]{:S(2)}) collective-permute-start(f32[16,128,128]{2,1,0:T(8,128)S(1)} %shard_map.38), channel_id=1, source_target_pairs={{5,4},{6,7},{13,12},{14,15},{21,20},{22,23},{29,28},{30,31}} | collective-permute-start | bytes 3145736 | tf_op jit(solution)/shard_map/ppermute | solution.py:166

commit v7 on v6

--- a/solution.py
+++ b/solution.py
@@ -20,7 +20,7 @@
     return high, low
 
 
-def pack(words, keep):
+def pack(words, keep, kind=0):
     words, keep = words.reshape(-1), keep.reshape(-1)
     slots = words.shape[0]
     spare = NC << 16
@@ -29,14 +29,15 @@
     count = jnp.sum(keep.astype(jnp.int32), keepdims=True)
     chosen = keep[None, :] & (rank[None, :] == number[:, None])
     packed = jnp.sum(jnp.where(chosen, words[None, :] - spare, 0), axis=1) + spare
-    return jnp.concatenate([packed, count])
-
-
-def contract_kernel(placed, n_left, n_right, words_ref, *refs):
+    return jnp.concatenate([packed, count, jnp.full((1,), kind, jnp.int32)])
+
+
+def contract_kernel(placed, n_left, n_right, words_ref, after_ref, *refs):
     left_refs, right_refs = refs[:n_left], refs[n_left : n_left + n_right]
     *before_ref, out_ref, left_raw, right_raw, total, sems = refs[n_left + n_right :]
     block, tile = right_refs[0].shape[0], right_refs[0].shape[-1]
     count, kind = (words_ref[words_ref.shape[0] - i] for i in (2, 1))
+    del after_ref
 
     @pl.when(count > 0)
     def _():
@@ -97,17 +98,17 @@
         out_ref[...] = before_ref[0][...] if before_ref else jnp.zeros_like(out_ref)
 
 
-def contract(planned, lefts, rights, before=None, placed=None, kind=0):
+def contract(planned, lefts, rights, before=None, placed=None, after=None):
     block, tile = rights[0].shape[0], rights[0].shape[-1]
     placed = placed or [(b,) for b in range(len(lefts))]
     blocks = 1 + max(place for places in placed for place in places if place is not None)
-    planned = jnp.append(planned, jnp.int32(kind))
-    operands = [planned, *lefts, *rights] + ([] if before is None else [before])
+    after = jnp.zeros((1,), jnp.int32) if after is None else after
+    operands = [planned, after, *lefts, *rights] + ([] if before is None else [before])
     size = (blocks * block + len(rights) * block + 3 * NC + 1) * tile * tile
     return pl.pallas_call(
         functools.partial(contract_kernel, placed, len(lefts), len(rights)),
         out_shape=pltpu.VMEM((NC, tile, tile), jnp.float32),
-        in_specs=[SMEM] + [ANY] * (len(lefts) + len(rights)) + [VMEM] * (before is not None),
+        in_specs=[SMEM] * 2 + [ANY] * (len(lefts) + len(rights)) + [VMEM] * (before is not None),
         out_specs=VMEM,
         scratch_shapes=[
             pltpu.VMEM((blocks * block, tile, tile), jnp.float32),
@@ -184,7 +185,7 @@
         return word
 
     panel = jnp.where(is_odd, steps_of, jnp.array([0, 3, 2, 1])[:, None])
-    own_words = pack(words(panel, 0, block, 2 * block, 3 * block), live & (mine | full))
+    own_words = pack(words(panel, 0, block, 2 * block, 3 * block), live & (mine | full), kind)
     their_words = pack(words(steps_of, 0, 0, block, 2 * block), live & is_odd & ~is_middle & ~mine)
 
     p1 = send(own, (even, beyond + outward, 0))
@@ -202,12 +203,12 @@
     own, p1, p2, p3, q1, q2, h1, h2, two, alternate, swapped = [
         x.reshape(-1, tile, tile) for x in (own, p1, p2, p3, q1, q2, h1, h2, two, alternate, swapped)
     ]
-    their_words = their_words + probe(alternate)
+    late = probe(alternate)
     own, p1, p2, p3, two, q2, swapped, alternate = [
         pltpu.with_memory_space_constraint(x, pltpu.HBM)
         for x in (own, p1, p2, p3, two, q2, swapped, alternate)
     ]
-    part = contract(their_words, [own, p3, q1], [p2, h1, h2, q2])
+    part = contract(their_words, [own, p3, q1], [p2, h1, h2, q2], after=late)
     part = send(part, (odd, outward, 0))
 
     lefts = [own, p1, p2, p3, q1, q2]
@@ -219,7 +220,7 @@
         (None, 2, 3, None),
         (None, 3, None, None),
     ]
-    total = contract(own_words, lefts, [own, alternate, two, swapped], None, placed, kind)
+    total = contract(own_words, lefts, [own, alternate, two, swapped], None, placed)
     return total + part
 
 

time: 88.3 us -> 91 us (1.031)
  waiting for transfers between devices: 35.6 us -> 53 us
  starting transfers between devices: 37.2 us -> 22.5 us
    ppermute x12, waiting for transfers between devices: 35.6 us -> 53 us  [send(): return lax.ppermute(value, ('blk', 'rep'), pairs)]
    ppermute x12, starting transfers between devices: 37.2 us -> 22.5 us  [send(): return lax.ppermute(value, ('blk', 'rep'), pairs)]
  transfers between devices with their start and end apart: 12 -> 12, of which waited for: 4 -> 3; matrix products, arithmetic and copies ran while one was open for 9% -> 8% of each run, Pallas kernels for 5% -> 5%
where the time goes in v7:
time: 91 us
  waiting for transfers between devices  53 us (58%)
  starting transfers between devices  22.5 us (25%)
  other arithmetic  6.53 us (7%)
  Pallas kernels  4.86 us (5%)
  local copies, waits for them, and re-layouts  3.17 us (3%)
  between operations  0.92 us (1%)
    ppermute x12, waiting for transfers between devices, send(): return lax.ppermute(value, ('blk', 'rep'), pairs)  53 us
    ppermute x12, starting transfers between devices, send(): return lax.ppermute(value, ('blk', 'rep'), pairs)  22.5 us
    pallas_call x2, Pallas kernels, contract(): pl.pallas_call(functools.partial(contract_kernel, placed, len(lefts), len...  4.86 us
  transfers between devices with their start and end apart: 12, of which 3 were waited for; matrix products, arithmetic and copies ran while one was open for 8% of the time, Pallas kernels for 5%

profile of v7, /device:TPU:1, one launch (start us, length us, event | category | flops | bytes accessed | tf_op | source)
XLA Modules:
  0.0 91.0 jit_solution(4736607785984183704)
XLA Ops:
  0.0 0.7 collective-permute-start
  0.7 4.1 %collective-permute-start.1 = (f32[4,5,128,128]{3,2,1,0:T(8,128)}, f32[4,5,128,128]{3,2,1,0:T(8,128)S(1)}, u32[]{:S(2)}, u32[]{:S(2)}) collective-permute-start(f32[4,5,128,128]{3,2,1,0:T(8,128)} %bitcast.37), channel_id=1, source_target_pairs={{1,2},{2,1},{9,10},{10,9},{17,18},{18,17},{25,26},{26,25},{4,5},{7... | collective-permute-start | bytes 3932168 | tf_op jit(solution)/shard_map/ppermute | solution.py:167
  4.9 1.7 %collective-permute-start.2 = (f32[4,5,128,128]{3,2,1,0:T(8,128)}, f32[4,5,128,128]{3,2,1,0:T(8,128)}, u32[]{:S(2)}, u32[]{:S(2)}) collective-permute-start(f32[4,5,128,128]{3,2,1,0:T(8,128)} %bitcast.38), channel_id=1, source_target_pairs={{0,1},{3,2},{8,9},{11,10},{16,17},{19,18},{24,25},{27,26},{5,6},{6... | collective-permute-start | bytes 3932168 | tf_op jit(solution)/shard_map/ppermute | solution.py:167
  6.6 1.2 %collective-permute-start.4 = (f32[4,5,128,128]{3,2,1,0:T(8,128)}, f32[4,5,128,128]{3,2,1,0:T(8,128)}, u32[]{:S(2)}, u32[]{:S(2)}) collective-permute-start(f32[4,5,128,128]{3,2,1,0:T(8,128)} %bitcast.39), channel_id=1, source_target_pairs={{0,8},{1,9},{2,10},{3,11},{4,12},{5,13},{6,14},{7,15},{8,16},{9,17... | collective-permute-start | bytes 3932168 | tf_op jit(solution)/shard_map/ppermute | solution.py:167
  7.8 7.8 %collective-permute-start.6 = (f32[4,5,128,128]{3,2,1,0:T(8,128)}, f32[4,5,128,128]{3,2,1,0:T(8,128)}, u32[]{:S(2)}, u32[]{:S(2)}) collective-permute-start(f32[4,5,128,128]{3,2,1,0:T(8,128)} %bitcast.40), channel_id=1, source_target_pairs={{0,4},{1,5},{2,6},{3,7},{8,12},{9,13},{10,14},{11,15},{16,20},{17,... | collective-permute-start | bytes 3932168 | tf_op jit(solution)/shard_map/ppermute | solution.py:167
  15.7 0.7 fusion.2
  16.4 1.4 %slice_divide_fusion = (s32[4,1,48]{2,0,1:T(4,128)S(1)}, s32[4,1,48]{2,0,1:T(4,128)S(1)}, s32[4,1,48]{2,0,1:T(4,128)S(1)}, s32[4,1,48]{2,0,1:T(4,128)S(1)}, s32[...) fusion(s32[4,3,48]{2,0,1:T(4,128)} %bitcast.50, pred[4,1,48]{2,0,1:T(4,128)(4,1)S(1)} %get-tuple-element.13, ...), kind=kLoop, calls=%fused_computation.25 | loop fusion | flops 2878 | bytes 5771 | tf_op jit(solution)/shard_map/jit(floor_divide)/div | solution.py:173
  19.3 0.7 pad_add_fusion.1
  20.0 1.3 %collective-permute-start.8 = (s32[210]{0:T(256)S(1)}, s32[210]{0:T(256)S(1)}, u32[]{:S(2)}, u32[]{:S(2)}) collective-permute-start(s32[210]{0:T(256)S(1)} %pad_add_fusion.1), channel_id=1, source_target_pairs={{4,5},{7,6},{12,13},{15,14},{20,21},{23,22},{28,29},{31,30}} | collective-permute-start | bytes 2528 | tf_op jit(solution)/shard_map/ppermute | solution.py:167
  21.3 10.4 %collective-permute-done.4 = f32[4,5,128,128]{3,2,1,0:T(8,128)} collective-permute-done((f32[4,5,128,128]{3,2,1,0:T(8,128)}, f32[4,5,128,128]{3,2,1,0:T(8,128)}, u32[]{:S(2)}, u32[]{:S(2)}) %collective-permute-start.4) | collective-permute-done | bytes 1310752 | tf_op jit(solution)/shard_map/ppermute | solution.py:167
  31.7 1.5 %broadcast_select_fusion = f32[4,5,128,128]{3,2,1,0:T(8,128)S(1)} fusion(f32[4,5,128,128]{3,2,1,0:T(8,128)S(1)} %collective-permute-done, f32[4,5,128,128]{3,2,1,0:T(8,128)} %collective-permute-done.4, pred[]{:T(512)S(6)} %or.22), kind=kLoop, calls=%fused_computation.1 | loop fusion | flops 327680 | bytes 3932161 | tf_op jit(solution)/shard_map/jit(_where)/select_n | solution.py:198
  33.2 0.7 collective-permute-start.5
  33.9 0.7 collective-permute-start.3
  34.7 0.7 collective-permute-start.9
  35.5 0.7 collective-permute-start.10
  36.2 15.5 %collective-permute-done.6 = f32[4,5,128,128]{3,2,1,0:T(8,128)} collective-permute-done((f32[4,5,128,128]{3,2,1,0:T(8,128)}, f32[4,5,128,128]{3,2,1,0:T(8,128)}, u32[]{:S(2)}, u32[]{:S(2)}) %collective-permute-start.6) | collective-permute-done | bytes 1310752 | tf_op jit(solution)/shard_map/ppermute | solution.py:167
  51.7 1.4 %collective-permute-start.7 = (f32[4,5,128,128]{3,2,1,0:T(8,128)}, f32[4,5,128,128]{3,2,1,0:T(8,128)}, u32[]{:S(2)}, u32[]{:S(2)}) collective-permute-start(f32[4,5,128,128]{3,2,1,0:T(8,128)} %collective-permute-done.4), channel_id=1, source_target_pairs={{0,4},{1,5},{2,6},{3,7},{8,12},{9,13},{10,14},{11,15},{16,20},{17,... | collective-permute-start | bytes 3932168 | tf_op jit(solution)/shard_map/ppermute | solution.py:167
  53.0 1.2 %slice.30 = f32[1,1,1]{2,1,0:T(1,128)} slice(f32[20,128,128]{2,1,0:T(8,128)} %bitcast.10.refs_7_), slice={[0:1], [0:1], [0:1]} | slice | bytes 8 | tf_op jit(solution)/shard_map/slice | solution.py:125
  54.9 1.0 %copy-done.2 = f32[4,5,128,128]{3,2,1,0:T(8,128)} copy-done((f32[4,5,128,128]{3,2,1,0:T(8,128)}, f32[4,5,128,128]{3,2,1,0:T(8,128)S(1)}, u32[]{:S(2)}) %copy-start.2) | copy-done | bytes 1310744
  56.0 0.7 shard_map.38
  56.7 1.3 %collective-permute-start.11 = (f32[16,128,128]{2,1,0:T(8,128)S(1)}, f32[16,128,128]{2,1,0:T(8,128)S(1)}, u32[]{:S(2)}, u32[]{:S(2)}) collective-permute-start(f32[16,128,128]{2,1,0:T(8,128)S(1)} %shard_map.38), channel_id=1, source_target_pairs={{5,4},{6,7},{13,12},{14,15},{21,20},{22,23},{29,28},{30,31}} | collective-permute-start | bytes 3145736 | tf_op jit(solution)/shard_map/ppermute | solution.py:167
  58.6 4.2 %shard_map.37 = f32[16,128,128]{2,1,0:T(8,128)S(1)} custom-call(s32[210]{0:T(256)S(1)} %pad_add_fusion.words_ref, s32[1]{0:T(128)} %constant.69.clone.1.after_ref, f32[20,128,128]{2,1,0:T(8,128)} %bitcast.42, f32[20,128,128]{2,1,0:T(8,128)} %bitcast.44, f32[20,128,128]{2,1,0:T(8,128)} %bitcast.46, f32[20,128,128]{2,1,0:T(8,128)} %bitcast.7.refs_3_.refs_1_, ...), custom_call_target="tpu_custom_call" | custom-call | flops 1000 | bytes 1000 | tf_op jit(solution)/shard_map/pallas_call | solution.py:108
  62.8 27.1 %collective-permute-done.11 = f32[16,128,128]{2,1,0:T(8,128)S(1)} collective-permute-done((f32[16,128,128]{2,1,0:T(8,128)S(1)}, f32[16,128,128]{2,1,0:T(8,128)S(1)}, u32[]{:S(2)}, u32[]{:S(2)}) %collective-permute-start.11) | collective-permute-done | bytes 1048608 | tf_op jit(solution)/shard_map/ppermute | solution.py:167
  89.9 1.1 %add_bitcast_fusion = f32[1,1,16,128,128]{4,3,2,1,0:T(8,128)} fusion(f32[16,128,128]{2,1,0:T(8,128)S(1)} %shard_map.37, f32[16,128,128]{2,1,0:T(8,128)S(1)} %collective-permute-done.11), kind=kLoop, calls=%fused_computation | loop fusion | flops 262144 | bytes 3145728 | tf_op jit(solution)/shard_map/broadcast_in_dim | solution.py:230
  (38 shorter events, 2.2 us)
Async XLA Ops:
  0.0 20.0 %collective-permute-start = (f32[4,5,128,128]{3,2,1,0:T(8,128)}, f32[4,5,128,128]{3,2,1,0:T(8,128)S(1)}, u32[]{:S(2)}, u32[]{:S(2)}) collective-permute-start(f32[4,5,128,128]{3,2,1,0:T(8,128)} %bitcast.36), channel_id=1, source_target_pairs={{0,2},{3,1},{1,0},{2,3},{8,10},{11,9},{9,8},{10,11},{16,18},{19,17... | collective-permute-start | bytes 3932168 | tf_op jit(solution)/shard_map/ppermute | solution.py:167
  0.7 33.2 %collective-permute-start.1 = (f32[4,5,128,128]{3,2,1,0:T(8,128)}, f32[4,5,128,128]{3,2,1,0:T(8,128)S(1)}, u32[]{:S(2)}, u32[]{:S(2)}) collective-permute-start(f32[4,5,128,128]{3,2,1,0:T(8,128)} %bitcast.37), channel_id=1, source_target_pairs={{1,2},{2,1},{9,10},{10,9},{17,18},{18,17},{25,26},{26,25},{4,5},{7... | collective-permute-start | bytes 3932168 | tf_op jit(solution)/shard_map/ppermute | solution.py:167
  4.9 29.8 %collective-permute-start.2 = (f32[4,5,128,128]{3,2,1,0:T(8,128)}, f32[4,5,128,128]{3,2,1,0:T(8,128)}, u32[]{:S(2)}, u32[]{:S(2)}) collective-permute-start(f32[4,5,128,128]{3,2,1,0:T(8,128)} %bitcast.38), channel_id=1, source_target_pairs={{0,1},{3,2},{8,9},{11,10},{16,17},{19,18},{24,25},{27,26},{5,6},{6... | collective-permute-start | bytes 3932168 | tf_op jit(solution)/shard_map/ppermute | solution.py:167
  6.6 25.1 %collective-permute-start.4 = (f32[4,5,128,128]{3,2,1,0:T(8,128)}, f32[4,5,128,128]{3,2,1,0:T(8,128)}, u32[]{:S(2)}, u32[]{:S(2)}) collective-permute-start(f32[4,5,128,128]{3,2,1,0:T(8,128)} %bitcast.39), channel_id=1, source_target_pairs={{0,8},{1,9},{2,10},{3,11},{4,12},{5,13},{6,14},{7,15},{8,16},{9,17... | collective-permute-start | bytes 3932168 | tf_op jit(solution)/shard_map/ppermute | solution.py:167
  7.8 43.9 %collective-permute-start.6 = (f32[4,5,128,128]{3,2,1,0:T(8,128)}, f32[4,5,128,128]{3,2,1,0:T(8,128)}, u32[]{:S(2)}, u32[]{:S(2)}) collective-permute-start(f32[4,5,128,128]{3,2,1,0:T(8,128)} %bitcast.40), channel_id=1, source_target_pairs={{0,4},{1,5},{2,6},{3,7},{8,12},{9,13},{10,14},{11,15},{16,20},{17,... | collective-permute-start | bytes 3932168 | tf_op jit(solution)/shard_map/ppermute | solution.py:167
  20.0 13.1 %copy-start = (f32[4,5,128,128]{3,2,1,0:T(8,128)}, f32[4,5,128,128]{3,2,1,0:T(8,128)S(1)}, u32[]{:S(2)}) copy-start(f32[4,5,128,128]{3,2,1,0:T(8,128)S(1)} %collective-permute-done) | copy-start | bytes 3932164
  20.0 15.4 %collective-permute-start.8 = (s32[210]{0:T(256)S(1)}, s32[210]{0:T(256)S(1)}, u32[]{:S(2)}, u32[]{:S(2)}) collective-permute-start(s32[210]{0:T(256)S(1)} %pad_add_fusion.1), channel_id=1, source_target_pairs={{4,5},{7,6},{12,13},{15,14},{20,21},{23,22},{28,29},{31,30}} | collective-permute-start | bytes 2528 | tf_op jit(solution)/shard_map/ppermute | solution.py:167
  33.2 21.7 %collective-permute-start.5 = (f32[4,5,128,128]{3,2,1,0:T(8,128)S(1)}, f32[4,5,128,128]{3,2,1,0:T(8,128)S(1)}, u32[]{:S(2)}, u32[]{:S(2)}) collective-permute-start(f32[4,5,128,128]{3,2,1,0:T(8,128)S(1)} %broadcast_select_fusion), channel_id=1, source_target_pairs={{1,0},{2,3},{9,8},{10,11},{17,16},{18,19},{25,24},{26,27},{0,5},{3... | collective-permute-start | bytes 3932168 | tf_op jit(solution)/shard_map/ppermute | solution.py:167
  33.9 21.0 %copy-start.1 = (f32[4,5,128,128]{3,2,1,0:T(8,128)}, f32[4,5,128,128]{3,2,1,0:T(8,128)S(1)}, u32[]{:S(2)}) copy-start(f32[4,5,128,128]{3,2,1,0:T(8,128)S(1)} %collective-permute-done.1) | copy-start | bytes 3932164
  33.9 21.0 %collective-permute-start.3 = (f32[4,5,128,128]{3,2,1,0:T(8,128)S(1)}, f32[4,5,128,128]{3,2,1,0:T(8,128)S(1)}, u32[]{:S(2)}, u32[]{:S(2)}) collective-permute-start(f32[4,5,128,128]{3,2,1,0:T(8,128)S(1)} %collective-permute-done.1), channel_id=1, source_target_pairs={{1,0},{2,3},{9,8},{10,11},{17,16},{18,19},{25,24},{26,27},{5,6},{6... | collective-permute-start | bytes 3932168 | tf_op jit(solution)/shard_map/ppermute | solution.py:167
  34.7 20.2 %collective-permute-start.9 = (f32[4,5,128,128]{3,2,1,0:T(8,128)}, f32[4,5,128,128]{3,2,1,0:T(8,128)S(1)}, u32[]{:S(2)}, u32[]{:S(2)}) collective-permute-start(f32[4,5,128,128]{3,2,1,0:T(8,128)} %collective-permute-done.2), channel_id=1, source_target_pairs={{1,5},{2,6},{9,13},{10,14},{17,21},{18,22},{25,29},{26,30}} | collective-permute-start | bytes 3932168 | tf_op jit(solution)/shard_map/ppermute | solution.py:167
  35.5 19.5 %collective-permute-start.10 = (f32[4,5,128,128]{3,2,1,0:T(8,128)S(1)}, f32[4,5,128,128]{3,2,1,0:T(8,128)S(1)}, u32[]{:S(2)}, u32[]{:S(2)}) collective-permute-start(f32[4,5,128,128]{3,2,1,0:T(8,128)S(1)} %collective-permute-done.1), channel_id=1, source_target_pairs={{5,13},{6,14},{13,21},{14,22},{21,29},{22,30},{29,5},{30,6}} | collective-permute-start | bytes 3932168 | tf_op jit(solution)/shard_map/ppermute | solution.py:167
  51.7 6.9 %collective-permute-start.7 = (f32[4,5,128,128]{3,2,1,0:T(8,128)}, f32[4,5,128,128]{3,2,1,0:T(8,128)}, u32[]{:S(2)}, u32[]{:S(2)}) collective-permute-start(f32[4,5,128,128]{3,2,1,0:T(8,128)} %collective-permute-done.4), channel_id=1, source_target_pairs={{0,4},{1,5},{2,6},{3,7},{8,12},{9,13},{10,14},{11,15},{16,20},{17,... | collective-permute-start | bytes 3932168 | tf_op jit(solution)/shard_map/ppermute | solution.py:167
  54.9 1.1 %copy-start.2 = (f32[4,5,128,128]{3,2,1,0:T(8,128)}, f32[4,5,128,128]{3,2,1,0:T(8,128)S(1)}, u32[]{:S(2)}) copy-start(f32[4,5,128,128]{3,2,1,0:T(8,128)S(1)} %collective-permute-done.5) | copy-start | bytes 3932164
  56.7 33.2 %collective-permute-start.11 = (f32[16,128,128]{2,1,0:T(8,128)S(1)}, f32[16,128,128]{2,1,0:T(8,128)S(1)}, u32[]{:S(2)}, u32[]{:S(2)}) collective-permute-start(f32[16,128,128]{2,1,0:T(8,128)S(1)} %shard_map.38), channel_id=1, source_target_pairs={{5,4},{6,7},{13,12},{14,15},{21,20},{22,23},{29,28},{30,31}} | collective-permute-start | bytes 3145736 | tf_op jit(solution)/shard_map/ppermute | solution.py:167
